TPU v7x, 512 devices: a whole 4x8x8 slice. The times are simulated.
512 devices in a mesh: dp: 32 (over x, z), rep: 16 (over y, core).
Axes of the slice: x: 4, y: 8, z: 8, core: 2. Of those that a mesh axis runs over, the one named last changes fastest.
Arguments:
- layer_rows: bfloat16 [34816, 3584], P(('rep', 'dp')), parts along dimension 0, may hold values from -500 to 500
- norm_gain: float32 [3584], replicated, may hold values from 0.1 to 1.9
- w_gate: bfloat16 [3584, 9216], P(None, 'dp'), may hold values from -0.09375 to 0.09375
- req_len: int32 [1024], P('rep'), parts along dimension 0, may hold values from 1 to 67, as said below
- req_rank: int32 [1024], P('rep'), parts along dimension 0, may hold values from 0 to 31
Outputs:
- activated: bfloat16 [34816, 9216], P(('rep', 'dp')), parts along dimension 0
There are 16 independent parts, one for each index of `rep`. A program takes and returns all parts, laid end to end along the dimension named above; an argument that names none is the same for every part. Nothing has to cross between parts.
Inputs may be any that keep to these rules, and one draw needn't show every extreme that they name: `req_len`: each rank owns exactly 2 requests. The lengths add up to 2048. The requests of one rank hold at most 68 rows, and one rank holds exactly 68; one request has exactly 67 rows.
All inputs are finite; a program needn't handle non-finite values.
Results may differ from a plain program's by a relative error of at most 0.005.
Values may be sent and summed in bfloat16 or wider, within the bound.
No kernel may reach another device: no remote copies, remote signals or barrier semaphores. Data moves between devices by JAX's collectives and lax.ppermute only.
A program may use at most 128 MiB of HBM per device.

v0:
```python
import jax
import jax.numpy as jnp
from jax import lax
from jax.sharding import PartitionSpec as P


def tally(req_len, req_rank, rank_total):
    rank_ids = jnp.arange(rank_total, dtype=jnp.int32)
    member = (req_rank[:, None] == rank_ids[None, :]).astype(jnp.int32)
    return jnp.sum(member * req_len[:, None], axis=0)


def pick_small(table, chosen_rank):
    rank_ids = jnp.arange(table.shape[0], dtype=jnp.int32)
    chosen = rank_ids[None, :] == chosen_rank[:, None]
    return jnp.sum(jnp.where(chosen, table[None, :], 0), axis=1)


def live_slots(global_slot, counts, slot_count):
    owner_rank = global_slot // slot_count
    within = global_slot - owner_rank * slot_count
    return within < pick_small(counts, owner_rank)


def normalize(layer_rows, norm_gain, live_mask):
    wide_rows = layer_rows.astype(jnp.float32)
    mean_square = jnp.mean(wide_rows * wide_rows, axis=-1, keepdims=True)
    scaled = wide_rows * lax.rsqrt(mean_square + 1e-06) * norm_gain
    return jnp.where(live_mask[:, None], scaled, jnp.zeros((), jnp.float32)).astype(jnp.bfloat16)


def activate(rows_in, w_gate):
    return jax.nn.silu(jnp.dot(rows_in, w_gate, preferred_element_type=jnp.float32)).astype(
        jnp.bfloat16
    )


def shards(layer_rows, norm_gain, w_gate, req_len, req_rank):
    rank_total = lax.axis_size("dp")
    my_rank = lax.axis_index("dp")
    slot_count = layer_rows.shape[0]
    counts = tally(req_len, req_rank, rank_total)
    own_slots = my_rank * slot_count + jnp.arange(slot_count, dtype=jnp.int32)
    normed = normalize(layer_rows, norm_gain, live_slots(own_slots, counts, slot_count))
    hidden = activate(lax.all_gather(normed, "dp", axis=0, tiled=True), w_gate)
    return lax.all_to_all(hidden, "dp", split_axis=0, concat_axis=1, tiled=True)


def solution(mesh):
    in_specs = (P(("rep", "dp"), None), P(), P(None, "dp"), P("rep"), P("rep"))
    out_specs = P(("rep", "dp"), None)
    return jax.shard_map(shards, mesh=mesh, in_specs=in_specs, out_specs=out_specs, check_vma=False)
```

profile of v0, /device:TPU:1, one launch (start us, length us, event | category | flops | bytes accessed | tf_op | source)
XLA Modules:
  0.0 251.4 jit_solution(7095407742100872181)
XLA Ops:
  6.5 0.0 copy-start
  6.5 0.0 all-gather.3.cloned.1.call-start
  6.5 1.4 fusion
  8.0 0.8 select_reduce_fusion.1
  8.8 0.1 select_reduce_fusion
  8.9 2.0 fusion.4
  10.9 0.0 all-gather.3.cloned.1.call-update
  10.9 150.7 %all-gather.3.cloned.1.call-done = bf16[32,68,3584]{2,1,0:T(8,128)(2,1)} async-done(((bf16[1,68,3584]{2,1,0:T(8,128)(2,1)}), bf16[32,68,3584]{2,1,0:T(8,128)(2,1)}) %all-gather.3.cloned.1.call-update) | async-done | bytes 15597584 | tf_op jit(solution)/shard_map/all_gather | solution.py:45
  161.7 17.8 %reshape.35 = bf16[2176,3584]{1,0:T(8,128)(2,1)} reshape(bf16[32,68,3584]{2,1,0:T(8,128)(2,1)} %all-gather.3.cloned.1.call-done) | data formatting | bytes 31195136
  179.4 0.0 copy-done
  179.4 9.1 %multiply_convert_fusion = bf16[2176,288]{0,1:T(8,128)(2,1)S(1)} fusion(bf16[2176,3584]{1,0:T(8,128)(2,1)} %reshape.35, bf16[3584,288]{0,1:T(8,128)(2,1)S(1)} %copy-done), kind=kOutput, calls=%fused_computation | convolution fusion | flops 4495233024 | bytes 18915328 | tf_op jit(solution)/shard_map/dot_general | solution.py:33
  188.6 1.7 copy.12
  190.3 3.8 %all_to_all.14 = bf16[32,68,288]{2,1,0:T(8,128)(2,1)} reshape(bf16[2176,288]{1,0:T(8,128)(2,1)} %copy.12) | data formatting | bytes 2506752 | tf_op jit(solution)/shard_map/all_to_all | solution.py:46
  194.1 45.0 %all_to_all.19 = bf16[32,68,288]{2,1,0:T(8,128)(2,1)S(1)} all-to-all(bf16[32,68,288]{2,1,0:T(8,128)(2,1)} %all_to_all.14), channel_id=1, replica_groups=mesh['dp'=32,'rep'=16] {'dp'}, dimensions={0} | all-to-all | bytes 2506752 | tf_op jit(solution)/shard_map/all_to_all | solution.py:46
  239.1 1.4 copy.13
  240.5 4.0 %all_to_all.17 = bf16[68,9216]{1,0:T(8,128)(2,1)} reshape(bf16[68,32,288]{2,1,0:T(8,128)(2,1)} %copy.13) | data formatting | bytes 2506752 | tf_op jit(solution)/shard_map/all_to_all | solution.py:46
  (3 shorter events, 0.0 us)
Async XLA Ops:
  6.5 172.9 %copy-start = (bf16[3584,288]{0,1:T(8,128)(2,1)S(1)}, bf16[3584,288]{0,1:T(8,128)(2,1)}, u32[]{:S(2)}) copy-start(bf16[3584,288]{0,1:T(8,128)(2,1)} %param.7) | copy-start | bytes 6193156
  6.5 155.1 %all-gather.3.cloned.1.call-start = ((), (), s32[]{:S(2)}) async-start(), calls=%async_computation.1 | async-start | bytes 17031168 | tf_op jit(solution)/shard_map/all_gather | solution.py:45
Sparse Core Ops, SparseCore 0:
  11.1 150.5 all-gather.2
where the time goes:
time: 256 us; the launch traced here: 251 us
  waiting for transfers between devices  151 us (59%)
  blocking collectives  45 us (18%)
  local copies, waits for them, and re-layouts  28.8 us (11%)
  between operations  13.4 us (5%)
  matrix products  9.12 us (4%)
  other arithmetic  4.35 us (2%)
    all_gather x1, waiting for transfers between devices, shards(): hidden = activate(lax.all_gather(normed, 'dp', axis=0, tiled=True), w_gate)  151 us
    all_to_all x1, blocking collectives, shards(): return lax.all_to_all(hidden, 'dp', split_axis=0, concat_axis=1, tiled=True)  45 us
    unnamed x3, local copies, waits for them, and re-layouts  17.8 us
    all_to_all x3, local copies, waits for them, and re-layouts, shards(): return lax.all_to_all(hidden, 'dp', split_axis=0, concat_axis=1, tiled=True)  9.31 us
    dot_general x1, matrix products, activate(): jnp.dot(rows_in, w_gate, preferred_element_type=jnp.float32)  9.12 us
  transfers between devices with their start and end apart: 1, of which 1 were waited for; matrix products, arithmetic and copies ran while one was open for 0% of the time, Pallas kernels for 0%

commit v1 on v0

v1 whole, which is shorter than its diff:
```python
import jax
import jax.numpy as jnp
from jax import lax
from jax.experimental import pallas as pl
from jax.experimental.pallas import tpu as pltpu
from jax.sharding import Mesh
from jax.sharding import PartitionSpec as P

AXES = {"x": 4, "z": 8, "y": 8, "core": 2}
PAD = 80
MIB = 1024 * 1024


def hop(value, axes, move):
    sizes = [AXES[a] for a in axes]
    total = 1
    for s in sizes:
        total *= s
    pairs = []
    for source in range(total):
        rest, at = source, []
        for s in reversed(sizes):
            at.append(rest % s)
            rest //= s
        target = 0
        for s, c in zip(sizes, move(*reversed(at))):
            target = target * s + c % s
        pairs.append((source, target))
    return lax.ppermute(value, tuple(axes), pairs)


def along_z(value):
    return hop(value, ("z", "core"), lambda z, c: (z + 1 - 2 * c, c))


def along_y(value):
    return hop(value, ("y", "core"), lambda y, c: (y + 1 - 2 * c, c))


def along_x(value):
    return hop(value, ("x", "core"), lambda x, c: (x + 1 - 2 * c, c))


def other_core(value):
    return hop(value, ("core",), lambda c: (1 - c,))


def normalize(place, layer_rows, norm_gain, req_len, req_rank, after):
    rows, features = layer_rows.shape

    def body(place_ref, rows_ref, gain_ref, len_ref, rank_ref, after_ref, out):
        owned = jnp.where(rank_ref[...] == place_ref[4], len_ref[...], 0)
        live = lax.broadcasted_iota(jnp.int32, (rows, 1), 0) < jnp.sum(owned, axis=1, keepdims=True)
        wide = rows_ref[...].astype(jnp.float32)
        mean_square = jnp.mean(wide * wide, axis=-1, keepdims=True)
        scaled = wide * lax.rsqrt(mean_square + 1e-06) * gain_ref[...]
        out[...] = jnp.where(live, scaled, 0.0).astype(jnp.bfloat16)

    in_vmem = pl.BlockSpec(memory_space=pltpu.VMEM)
    return pl.pallas_call(
        body,
        out_shape=jax.ShapeDtypeStruct((rows, features), jnp.bfloat16),
        in_specs=[pl.BlockSpec(memory_space=pltpu.SMEM)] + [in_vmem] * 4 + [pl.BlockSpec(memory_space=pl.ANY)],
        out_specs=in_vmem,
        compiler_params=pltpu.CompilerParams(vmem_limit_bytes=8 * MIB),
        cost_estimate=pl.CostEstimate(flops=5 * rows * features, bytes_accessed=4 * rows * features, transcendentals=rows),
        name="normalize",
    )(place, layer_rows, norm_gain.reshape(1, -1), req_len.reshape(1, -1), req_rank.reshape(1, -1), after)


def line_up(place, pair, beside, far, swapped):
    rows, features = pair.shape[1:]

    def body(place_ref, pair_ref, beside_ref, far_ref, swapped_ref, out):
        x, c = place_ref[0], place_ref[1]
        back = 2 * c - 1

        def put(step, core, block):
            owner = lax.rem(x + step + 4, 4) * 2 + core
            out[pl.ds(pl.multiple_of(owner * PAD, 16), rows), :] = block

        put(0, c, pair_ref[0])
        put(0, 1 - c, pair_ref[1])
        put(back, c, beside_ref[0])
        put(back, 1 - c, beside_ref[1])
        put(2, c, far_ref[0])
        put(-back, 1 - c, swapped_ref[0])
        put(-back, c, swapped_ref[1])
        put(2, 1 - c, swapped_ref[2])

    return pl.pallas_call(
        body,
        out_shape=jax.ShapeDtypeStruct((8 * PAD, features), pair.dtype),
        in_specs=[pl.BlockSpec(memory_space=pltpu.SMEM)] + [pl.BlockSpec(memory_space=pltpu.VMEM)] * 4,
        out_specs=pl.BlockSpec(memory_space=pltpu.VMEM),
        compiler_params=pltpu.CompilerParams(vmem_limit_bytes=12 * MIB),
        cost_estimate=pl.CostEstimate(flops=0, bytes_accessed=32 * rows * features, transcendentals=0),
        name="line_up",
    )(place, pair, beside, far, swapped)


def project(place, rows_in, near, far, rows, after=()):
    total, features = rows_in.shape
    half = features // 2
    owners = total // PAD
    widths = [w.shape[0] for w in near]
    columns = sum(widths)
    given = list(near) + [w for w in far if w is not None]
    per = 2
    block = per * PAD

    def body(place_ref, a_ref, *refs):
        out = refs[-1]
        q = place_ref[2]
        first = pl.multiple_of(q * half, 128)
        second = pl.multiple_of((1 - q) * half, 128)
        a_first, a_second = a_ref[:, pl.ds(first, half)], a_ref[:, pl.ds(second, half)]
        w_first, w_second, rest = [], [], list(refs[len(near) : len(given)])
        for ref, other in zip(refs[: len(near)], far):
            if other is None:
                w_first.append(ref[:, pl.ds(first, half)])
                w_second.append(ref[:, pl.ds(second, half)])
            else:
                w_first.append(ref[...])
                w_second.append(rest.pop(0)[...])
        contract = (((1,), (1,)), ((), ()))
        gate = lax.dot_general(a_first, jnp.concatenate(w_first, 0), contract, preferred_element_type=jnp.float32)
        gate += lax.dot_general(a_second, jnp.concatenate(w_second, 0), contract, preferred_element_type=jnp.float32)
        act = (gate / (1.0 + jnp.exp(-gate))).astype(jnp.bfloat16)
        for i in range(per):
            out[i] = act[i * PAD : i * PAD + rows]

    return pl.pallas_call(
        body,
        grid=(owners // per,),
        out_shape=jax.ShapeDtypeStruct((owners, rows, columns), jnp.bfloat16),
        in_specs=[pl.BlockSpec(memory_space=pltpu.SMEM), pl.BlockSpec((block, features), lambda i: (i, 0))]
        + [pl.BlockSpec(w.shape, lambda i: (0, 0)) for w in given]
        + [pl.BlockSpec(memory_space=pl.ANY)] * len(after),
        out_specs=pl.BlockSpec((per, rows, columns), lambda i: (i, 0, 0)),
        compiler_params=pltpu.CompilerParams(vmem_limit_bytes=20 * MIB),
        cost_estimate=pl.CostEstimate(
            flops=2 * total * features * columns,
            bytes_accessed=2 * (total * features + features * columns + total * columns),
            transcendentals=total * columns,
        ),
        name="project",
    )(place, rows_in, *given, *after)


def settle(place, early, late, width):
    rows = early.shape[1]
    half = width // 2
    region = 8 * width

    def body(place_ref, early_ref, late_ref, out):
        z = place_ref[3]

        def take(ref, core, k, n=1):
            return ref[core, :, k * half : (k + n) * half]

        def flipped(ref, k):
            return [take(ref, 1, k + 1), take(ref, 1, k)]

        parts = [take(late_ref, 0, 0, 2), take(early_ref, 0, 3, 2), take(early_ref, 0, 1, 2)]
        parts += [take(early_ref, 0, 0), take(early_ref, 1, 0)]
        parts += flipped(early_ref, 1) + flipped(early_ref, 3) + flipped(late_ref, 0)
        parts += [take(late_ref, 0, 2), take(late_ref, 1, 2)]
        line = jnp.concatenate([p.astype(jnp.float32) for p in parts], axis=1)
        line = pltpu.roll(line, lax.rem(z + 5, 8) * width, 1)
        out[...] = line.astype(jnp.bfloat16)

    return pl.pallas_call(
        body,
        grid=(4,),
        out_shape=jax.ShapeDtypeStruct((rows, 4 * region), jnp.bfloat16),
        in_specs=[pl.BlockSpec(memory_space=pltpu.SMEM)]
        + [pl.BlockSpec((2, rows, g.shape[2]), lambda i: (i, 0, 0)) for g in (early, late)],
        out_specs=pl.BlockSpec((rows, region), lambda i: (0, i)),
        compiler_params=pltpu.CompilerParams(vmem_limit_bytes=20 * MIB),
        cost_estimate=pl.CostEstimate(flops=0, bytes_accessed=16 * rows * region, transcendentals=0),
        name="settle",
    )(place, early, late)


def shards(layer_rows, norm_gain, w_gate, req_len, req_rank):
    x, z, y, c = (lax.axis_index(a) for a in ("x", "z", "y", "core"))
    rows, features = layer_rows.shape
    width = w_gate.shape[1]
    half_width, half = width // 2, features // 2
    plane = lax.rem(y, 2)
    place = jnp.stack([x, c, plane, z, x * AXES["z"] + z]).astype(jnp.int32)

    weights = w_gate.T

    def own(core):
        return lax.dynamic_slice(weights, (core * half_width, plane * half), (half_width, half))

    together = lax.optimization_barrier
    a, b = [own(c)], [own(1 - c)]
    a.append(along_z(a[0]))
    b.append(along_z(b[0]))

    normed = normalize(place, layer_rows, norm_gain, req_len, req_rank, a[0])
    pair = jnp.stack([normed, other_core(normed)])
    pair, a[1] = together((pair, a[1]))
    beside = along_x(pair)
    a.append(along_z(a[1]))
    b.append(along_z(b[1]))
    near1 = [jnp.concatenate([a[1], b[1]], 0)]
    far1 = [along_y(near1[0])]
    onward, a[2], b[1] = together((beside[:1], a[2], b[1]))
    far = along_x(onward)
    a.append(along_z(a[2]))
    b.append(along_z(b[2]))
    near1.append(jnp.concatenate([a[2], b[2]], 0))
    far1.append(along_y(near1[1]))
    others, b[2], far1[0] = together((jnp.concatenate([beside, far], 0), b[2], far1[0]))
    swapped = other_core(others)
    a[3], far1[0] = together((a[3], far1[0]))
    a.append(along_z(a[3]))
    rows_in = line_up(place, pair, beside, far, swapped)

    own_half = lax.dynamic_slice(weights, (c * half_width, 0), (half_width, features))
    first = project(place, rows_in, [own_half] + near1, [None] + far1, rows)
    early = lax.all_to_all(first, ("x", "core"), 0, 0, tiled=True)
    a[4], first = together((a[4], first))
    near2 = [a[3], b[3], a[4]]
    far2 = [along_y(w) for w in near2]
    far2[0], early = together((far2[0], early))
    second = project(place, rows_in, near2, far2, rows, after=(first,))
    late = lax.all_to_all(second, ("x", "core"), 0, 0, tiled=True)
    return settle(place, early, late, width)


def solution(mesh):
    grid = Mesh(mesh.devices.reshape(tuple(AXES.values())), tuple(AXES))
    rows = P(("y", "core", "x", "z"), None)
    in_specs = (rows, P(), P(None, ("x", "z")), P(("y", "core")), P(("y", "core")))
    return jax.shard_map(shards, mesh=grid, in_specs=in_specs, out_specs=rows, check_vma=False)
```

time: 256 us -> 147 us (0.57); the launches traced: 251 us -> 146 us
  waiting for transfers between devices: 151 us -> 34.2 us
  starting transfers between devices: 0.01 us -> 68.4 us
  blocking collectives: 45 us -> 16.6 us
  local copies, waits for them, and re-layouts: 28.8 us -> 7.66 us
  Pallas kernels: 0 us -> 18.5 us
  between operations: 13.4 us -> 0.33 us
  matrix products: 9.12 us -> 0 us
  other arithmetic: 4.35 us -> 0.25 us
    all_gather x1 -> x0, waiting for transfers between devices: 151 us -> none  [shards(): hidden = activate(lax.all_gather(normed, 'dp', axis=0, tiled=True), w_gate)]
    ppermute x0 -> x16, starting transfers between devices: none -> 64.9 us  [hop(): return lax.ppermute(value, tuple(axes), pairs)]
    ppermute x0 -> x16, waiting for transfers between devices: none -> 34.2 us  [hop(): return lax.ppermute(value, tuple(axes), pairs)]
    all_to_all x1, blocking collectives: 45 us -> 16.6 us  [shards(): late = lax.all_to_all(second, ('x', 'core'), 0, 0, tiled=True)]
    pallas_call x0 -> x5, Pallas kernels: none -> 18.5 us  [the longest x2 13.7 us: project(): pl.pallas_call(body, grid=(owners // per,), out_shape=jax.ShapeDtypeStruc...]
    unnamed x3 -> x14, local copies, waits for them, and re-layouts: 17.8 us -> 4.48 us
    all_to_all x3 -> x0, local copies, waits for them, and re-layouts: 9.31 us -> none  [shards(): return lax.all_to_all(hidden, 'dp', split_axis=0, concat_axis=1, tiled=True)]
    dot_general x1 -> x0, matrix products: 9.12 us -> none  [activate(): jnp.dot(rows_in, w_gate, preferred_element_type=jnp.float32)]
  transfers between devices with their start and end apart: 1 -> 17, of which waited for: 1 -> 8; matrix products, arithmetic and copies ran while one was open for 0% -> 0% of each run, Pallas kernels for 0% -> 6%
where the time goes in v1:
time: 147 us; the launch traced here: 146 us
  starting transfers between devices  68.4 us (47%)
  waiting for transfers between devices  34.2 us (23%)
  Pallas kernels  18.5 us (13%)
  blocking collectives  16.6 us (11%)
  local copies, waits for them, and re-layouts  7.66 us (5%)
    ppermute x16, starting transfers between devices, hop(): return lax.ppermute(value, tuple(axes), pairs)  64.9 us
    ppermute x16, waiting for transfers between devices, hop(): return lax.ppermute(value, tuple(axes), pairs)  34.2 us
    all_to_all x1, blocking collectives, shards(): late = lax.all_to_all(second, ('x', 'core'), 0, 0, tiled=True)  16.6 us
    pallas_call x2, Pallas kernels, project(): pl.pallas_call(body, grid=(owners // per,), out_shape=jax.ShapeDtypeStruc...  13.7 us
    unnamed x14, local copies, waits for them, and re-layouts  4.48 us
    all_to_all x1, starting transfers between devices, shards(): early = lax.all_to_all(first, ('x', 'core'), 0, 0, tiled=True)  3.5 us
    pallas_call x1, Pallas kernels, settle(): pl.pallas_call(body, grid=(4,), out_shape=jax.ShapeDtypeStruct((rows, 4 *...  3.15 us
  transfers between devices with their start and end apart: 17, of which 8 were waited for; matrix products, arithmetic and copies ran while one was open for 0% of the time, Pallas kernels for 6%

profile of v1, /device:TPU:1, one launch (start us, length us, event | category | flops | bytes accessed | tf_op | source)
XLA Modules:
  0.0 146.0 jit_solution(14363113315405069261)
XLA Ops:
  0.0 0.8 reshape.9.gain_ref
  0.8 1.3 dynamic-slice_bitcast_fusion.1
  2.1 0.1 stack.32.place_ref
  2.2 0.8 normalize.1
  3.0 8.8 %collective-permute-start = (bf16[68,3584]{1,0:T(8,128)(2,1)S(1)}, bf16[68,3584]{1,0:T(8,128)(2,1)S(1)}, u32[]{:S(2)}, u32[]{:S(2)}) collective-permute-start(bf16[68,3584]{1,0:T(8,128)(2,1)S(1)} %normalize.1), channel_id=1, source_target_pairs={{0,1},{1,0},{2,3},{3,2},{4,5},{5,4},{6,7},{7,6},{8,9},{9,8},{10,11... | collective-permute-start | bytes 1462280 | tf_op jit(solution)/shard_map/ppermute | solution.py:29
  11.8 5.3 %collective-permute-start.1 = (bf16[144,1792]{1,0:T(8,128)(2,1)S(1)}, bf16[144,1792]{1,0:T(8,128)(2,1)S(1)}, u32[]{:S(2)}, u32[]{:S(2)}) collective-permute-start(bf16[144,1792]{1,0:T(8,128)(2,1)S(1)} %get-tuple-element.30.after_ref), channel_id=1, source_target_pairs={{0,16},{1,113},{16,32},{17,1},{32,48},{33,17},{48,64},{49,33},{64,... | collective-permute-start | bytes 1548296 | tf_op jit(solution)/shard_map/ppermute | solution.py:29
  17.1 0.0 collective-permute-done
  17.1 0.1 pad_maximum_fusion.1.pair_ref
  17.2 5.9 %collective-permute-done.1 = bf16[144,1792]{1,0:T(8,128)(2,1)S(1)} collective-permute-done((bf16[144,1792]{1,0:T(8,128)(2,1)S(1)}, bf16[144,1792]{1,0:T(8,128)(2,1)S(1)}, u32[]{:S(2)}, u32[]{:S(2)}) %collective-permute-start.1) | collective-permute-done | bytes 516128 | tf_op jit(solution)/shard_map/ppermute | solution.py:29
  23.1 0.8 copy.6
  23.9 4.4 %collective-permute-start.2 = (bf16[2,68,3584]{2,0,1:T(2,128)(2,1)S(1)}, bf16[2,68,3584]{2,0,1:T(2,128)(2,1)S(1)}, u32[]{:S(2)}, u32[]{:S(2)}) collective-permute-start(bf16[2,68,3584]{2,0,1:T(2,128)(2,1)S(1)} %copy.6), channel_id=1, source_target_pairs={{0,128},{1,385},{128,256},{129,1},{256,384},{257,129},{384,0},{385... | collective-permute-start | bytes 2924552 | tf_op jit(solution)/shard_map/ppermute | solution.py:29
  28.3 5.0 %collective-permute-start.4 = (bf16[144,1792]{1,0:T(8,128)(2,1)S(1)}, bf16[144,1792]{1,0:T(8,128)(2,1)S(1)}, u32[]{:S(2)}, u32[]{:S(2)}) collective-permute-start(bf16[144,1792]{1,0:T(8,128)(2,1)S(1)} %get-tuple-element.29), channel_id=1, source_target_pairs={{0,16},{1,113},{16,32},{17,1},{32,48},{33,17},{48,64},{49,33},{64,... | collective-permute-start | bytes 1548296 | tf_op jit(solution)/shard_map/ppermute | solution.py:29
  33.3 1.9 %collective-permute-start.3 = (bf16[144,1792]{1,0:T(8,128)(2,1)S(1)}, bf16[144,1792]{1,0:T(8,128)(2,1)S(1)}, u32[]{:S(2)}, u32[]{:S(2)}) collective-permute-start(bf16[144,1792]{1,0:T(8,128)(2,1)S(1)} %collective-permute-done.1), channel_id=1, source_target_pairs={{0,16},{1,113},{16,32},{17,1},{32,48},{33,17},{48,64},{49,33},{64,... | collective-permute-start | bytes 1548296 | tf_op jit(solution)/shard_map/ppermute | solution.py:29
  35.3 4.0 %collective-permute-done.4 = bf16[144,1792]{1,0:T(8,128)(2,1)S(1)} collective-permute-done((bf16[144,1792]{1,0:T(8,128)(2,1)S(1)}, bf16[144,1792]{1,0:T(8,128)(2,1)S(1)}, u32[]{:S(2)}, u32[]{:S(2)}) %collective-permute-start.4) | collective-permute-done | bytes 516128 | tf_op jit(solution)/shard_map/ppermute | solution.py:29
  39.4 5.1 %collective-permute-start.8 = (bf16[288,1792]{1,0:T(8,128)(2,1)S(1)}, bf16[288,1792]{1,0:T(8,128)(2,1)S(1)}, u32[]{:S(2)}, u32[]{:S(2)}) collective-permute-start(bf16[288,1792]{1,0:T(8,128)(2,1)S(1)} %constant_dynamic-update-slice_fusion.refs_1_), channel_id=1, source_target_pairs={{0,2},{1,15},{2,4},{3,1},{4,6},{5,3},{6,8},{7,5},{8,10},{9,7},{10,... | collective-permute-start | bytes 3096584 | tf_op jit(solution)/shard_map/ppermute | solution.py:29
  44.5 0.0 collective-permute-done.2
  44.5 0.1 copy.7.beside_ref
  44.7 0.2 collective-permute-done.3
  44.9 2.4 %collective-permute-start.6 = (bf16[1,68,3584]{2,1,0:T(8,128)(2,1)S(1)}, bf16[1,68,3584]{2,1,0:T(8,128)(2,1)S(1)}, u32[]{:S(2)}, u32[]{:S(2)}) collective-permute-start(bf16[1,68,3584]{2,1,0:T(8,128)(2,1)S(1)} %slice.4), channel_id=1, source_target_pairs={{0,128},{1,385},{128,256},{129,1},{256,384},{257,129},{384,0},{385... | collective-permute-start | bytes 1462280 | tf_op jit(solution)/shard_map/ppermute | solution.py:29
  47.3 5.0 %collective-permute-start.7 = (bf16[144,1792]{1,0:T(8,128)(2,1)S(1)}, bf16[144,1792]{1,0:T(8,128)(2,1)S(1)}, u32[]{:S(2)}, u32[]{:S(2)}) collective-permute-start(bf16[144,1792]{1,0:T(8,128)(2,1)S(1)} %collective-permute-done.4), channel_id=1, source_target_pairs={{0,16},{1,113},{16,32},{17,1},{32,48},{33,17},{48,64},{49,33},{64,... | collective-permute-start | bytes 1548296 | tf_op jit(solution)/shard_map/ppermute | solution.py:29
  52.4 2.6 %collective-permute-done.6.far_ref = bf16[1,68,3584]{2,1,0:T(8,128)(2,1)S(1)} collective-permute-done((bf16[1,68,3584]{2,1,0:T(8,128)(2,1)S(1)}, bf16[1,68,3584]{2,1,0:T(8,128)(2,1)S(1)}, u32[]{:S(2)}, u32[]{:S(2)}) %collective-permute-start.6) | collective-permute-done | bytes 487456 | tf_op jit(solution)/shard_map/ppermute | solution.py:29
  55.0 0.1 pad_maximum_fusion
  55.2 3.2 %collective-permute-done.7 = bf16[144,1792]{1,0:T(8,128)(2,1)S(1)} collective-permute-done((bf16[144,1792]{1,0:T(8,128)(2,1)S(1)}, bf16[144,1792]{1,0:T(8,128)(2,1)S(1)}, u32[]{:S(2)}, u32[]{:S(2)}) %collective-permute-start.7) | collective-permute-done | bytes 516128 | tf_op jit(solution)/shard_map/ppermute | solution.py:29
  58.4 0.0 collective-permute-done.8.refs_3_
  58.4 5.5 %collective-permute-start.10 = (bf16[3,68,3584]{2,1,0:T(8,128)(2,1)S(1)}, bf16[3,68,3584]{2,1,0:T(8,128)(2,1)S(1)}, u32[]{:S(2)}, u32[]{:S(2)}) collective-permute-start(bf16[3,68,3584]{2,1,0:T(8,128)(2,1)S(1)} %pad_maximum_fusion), channel_id=1, source_target_pairs={{0,1},{1,0},{2,3},{3,2},{4,5},{5,4},{6,7},{7,6},{8,9},{9,8},{10,11... | collective-permute-start | bytes 4386824 | tf_op jit(solution)/shard_map/ppermute | solution.py:29
  64.0 5.1 %collective-permute-start.11 = (bf16[288,1792]{1,0:T(8,128)(2,1)S(1)}, bf16[288,1792]{1,0:T(8,128)(2,1)S(1)}, u32[]{:S(2)}, u32[]{:S(2)}) collective-permute-start(bf16[288,1792]{1,0:T(8,128)(2,1)S(1)} %constant_dynamic-update-slice_fusion.2.refs_2_), channel_id=1, source_target_pairs={{0,2},{1,15},{2,4},{3,1},{4,6},{5,3},{6,8},{7,5},{8,10},{9,7},{10,... | collective-permute-start | bytes 3096584 | tf_op jit(solution)/shard_map/ppermute | solution.py:29
  69.1 1.9 %collective-permute-start.5 = (bf16[144,1792]{1,0:T(8,128)(2,1)S(1)}, bf16[144,1792]{1,0:T(8,128)(2,1)S(1)}, u32[]{:S(2)}, u32[]{:S(2)}) collective-permute-start(bf16[144,1792]{1,0:T(8,128)(2,1)S(1)} %collective-permute-done.3), channel_id=1, source_target_pairs={{0,16},{1,113},{16,32},{17,1},{32,48},{33,17},{48,64},{49,33},{64,... | collective-permute-start | bytes 1548296 | tf_op jit(solution)/shard_map/ppermute | solution.py:29
  71.0 1.9 %collective-permute-start.12 = (bf16[144,1792]{1,0:T(8,128)(2,1)S(1)}, bf16[144,1792]{1,0:T(8,128)(2,1)S(1)}, u32[]{:S(2)}, u32[]{:S(2)}) collective-permute-start(bf16[144,1792]{1,0:T(8,128)(2,1)S(1)} %collective-permute-done.7), channel_id=1, source_target_pairs={{0,16},{1,113},{16,32},{17,1},{32,48},{33,17},{48,64},{49,33},{64,... | collective-permute-start | bytes 1548296 | tf_op jit(solution)/shard_map/ppermute | solution.py:29
  72.9 6.3 %collective-permute-done.5.refs_0_ = bf16[144,1792]{1,0:T(8,128)(2,1)S(1)} collective-permute-done((bf16[144,1792]{1,0:T(8,128)(2,1)S(1)}, bf16[144,1792]{1,0:T(8,128)(2,1)S(1)}, u32[]{:S(2)}, u32[]{:S(2)}) %collective-permute-start.5) | collective-permute-done | bytes 516128 | tf_op jit(solution)/shard_map/ppermute | solution.py:29
  79.2 3.1 %collective-permute-start.13 = (bf16[144,1792]{1,0:T(8,128)(2,1)S(1)}, bf16[144,1792]{1,0:T(8,128)(2,1)S(1)}, u32[]{:S(2)}, u32[]{:S(2)}) collective-permute-start(bf16[144,1792]{1,0:T(8,128)(2,1)S(1)} %collective-permute-done.5.refs_0_), channel_id=1, source_target_pairs={{0,16},{1,113},{16,32},{17,1},{32,48},{33,17},{48,64},{49,33},{64,... | collective-permute-start | bytes 1548296 | tf_op jit(solution)/shard_map/ppermute | solution.py:29
  82.3 0.1 dynamic-slice_bitcast_fusion.refs_0_
  82.4 0.0 collective-permute-done.10.swapped_ref
  82.4 0.8 line_up.1.a_ref
  83.3 0.0 collective-permute-done.11.refs_4_
  83.3 8.4 %project.2.refs_6_ = bf16[8,68,720]{2,1,0:T(8,128)(2,1)} custom-call(s32[5]{0:T(128)S(1)} %stack.32.place_ref, bf16[640,3584]{1,0:T(8,128)(2,1)S(1)} %line_up.1.a_ref, bf16[144,3584]{1,0:T(8,128)(2,1)S(1)} %dynamic-slice_bitcast_fusion.refs_0_, bf16[288,1792]{1,0:T(8,128)(2,1)S(1)} %constant_dynamic-update-slice_fusion.refs_1_, ...), custom_call_target="tpu_custom_call" | custom-call | flops 3303014400 | bytes 10670080 | tf_op jit(solution)/shard_map/project/pallas_call | solution.py:133
  91.6 2.1 %copy-done = bf16[640,3584]{1,0:T(8,128)(2,1)} copy-done((bf16[640,3584]{1,0:T(8,128)(2,1)}, bf16[640,3584]{1,0:T(8,128)(2,1)S(1)}, u32[]{:S(2)}) %copy-start) | copy-done | bytes 4587544
  93.7 3.5 %all-to-all-start = ((bf16[8,68,720]{2,1,0:T(8,128)(2,1)}), bf16[8,68,720]{2,1,0:T(8,128)(2,1)S(1)}, u32[]{:S(2)}, u32[]{:S(2)}) async-start(bf16[8,68,720]{2,1,0:T(8,128)(2,1)} %project.2.refs_6_), calls=%async_computation | async-start | bytes 1769472 | tf_op jit(solution)/shard_map/all_to_all | solution.py:226
  97.2 0.0 collective-permute-done.12.refs_1_
  97.3 2.7 %collective-permute-start.14 = (bf16[144,1792]{1,0:T(8,128)(2,1)S(1)}, bf16[144,1792]{1,0:T(8,128)(2,1)S(1)}, u32[]{:S(2)}, u32[]{:S(2)}) collective-permute-start(bf16[144,1792]{1,0:T(8,128)(2,1)S(1)} %collective-permute-done.12.refs_1_), channel_id=1, source_target_pairs={{0,2},{1,15},{2,4},{3,1},{4,6},{5,3},{6,8},{7,5},{8,10},{9,7},{10,... | collective-permute-start | bytes 1548296 | tf_op jit(solution)/shard_map/ppermute | solution.py:29
  100.0 3.7 %collective-permute-start.9 = (bf16[144,1792]{1,0:T(8,128)(2,1)S(1)}, bf16[144,1792]{1,0:T(8,128)(2,1)S(1)}, u32[]{:S(2)}, u32[]{:S(2)}) collective-permute-start(bf16[144,1792]{1,0:T(8,128)(2,1)S(1)} %collective-permute-done.5.refs_0_), channel_id=1, source_target_pairs={{0,2},{1,15},{2,4},{3,1},{4,6},{5,3},{6,8},{7,5},{8,10},{9,7},{10,... | collective-permute-start | bytes 1548296 | tf_op jit(solution)/shard_map/ppermute | solution.py:29
  103.6 0.0 collective-permute-done.13.refs_2_
  103.6 3.0 %collective-permute-start.15 = (bf16[144,1792]{1,0:T(8,128)(2,1)S(1)}, bf16[144,1792]{1,0:T(8,128)(2,1)}, u32[]{:S(2)}, u32[]{:S(2)}) collective-permute-start(bf16[144,1792]{1,0:T(8,128)(2,1)S(1)} %collective-permute-done.13.refs_2_), channel_id=1, source_target_pairs={{0,2},{1,15},{2,4},{3,1},{4,6},{5,3},{6,8},{7,5},{8,10},{9,7},{10,... | collective-permute-start | bytes 1548296 | tf_op jit(solution)/shard_map/ppermute | solution.py:29
  106.6 6.3 %collective-permute-done.9.refs_3_ = bf16[144,1792]{1,0:T(8,128)(2,1)S(1)} collective-permute-done((bf16[144,1792]{1,0:T(8,128)(2,1)S(1)}, bf16[144,1792]{1,0:T(8,128)(2,1)S(1)}, u32[]{:S(2)}, u32[]{:S(2)}) %collective-permute-start.9) | collective-permute-done | bytes 516128 | tf_op jit(solution)/shard_map/ppermute | solution.py:29
  112.9 5.6 %collective-permute-done.15.refs_5_ = bf16[144,1792]{1,0:T(8,128)(2,1)} collective-permute-done((bf16[144,1792]{1,0:T(8,128)(2,1)S(1)}, bf16[144,1792]{1,0:T(8,128)(2,1)}, u32[]{:S(2)}, u32[]{:S(2)}) %collective-permute-start.15) | collective-permute-done | bytes 516128 | tf_op jit(solution)/shard_map/ppermute | solution.py:29
  118.6 2.3 %copy-done.1 = bf16[640,3584]{1,0:T(8,128)(2,1)S(1)} copy-done((bf16[640,3584]{1,0:T(8,128)(2,1)S(1)}, bf16[640,3584]{1,0:T(8,128)(2,1)}, u32[]{:S(2)}) %copy-start.1) | copy-done | bytes 4587544
  120.9 5.3 %project.3 = bf16[8,68,432]{2,1,0:T(8,128)(2,1)S(1)} custom-call(s32[5]{0:T(128)S(1)} %stack.32.place_ref, bf16[640,3584]{1,0:T(8,128)(2,1)S(1)} %copy-done.1, bf16[144,1792]{1,0:T(8,128)(2,1)S(1)} %collective-permute-done.5.refs_0_, bf16[144,1792]{1,0:T(8,128)(2,1)S(1)} %collective-permute-done.12.refs_1_, ...), custom_call_target="tpu_custom_call" | custom-call | flops 1981808640 | bytes 8237056 | tf_op jit(solution)/shard_map/project/pallas_call | solution.py:133
  126.2 16.6 %all_to_all.10.late_ref = bf16[8,68,432]{2,1,0:T(8,128)(2,1)S(1)} all-to-all(bf16[8,68,432]{2,1,0:T(8,128)(2,1)S(1)} %project.3), channel_id=1, replica_groups=mesh['x'=4,'z'=8,'y'=8,'core'=2] {'x','core'}, dimensions={0} | all-to-all | bytes 940032 | tf_op jit(solution)/shard_map/all_to_all | solution.py:232
  142.8 3.1 %settle.1 = bf16[68,9216]{1,0:T(8,128)(2,1)} custom-call(s32[5]{0:T(128)S(1)} %stack.32.place_ref, bf16[8,68,720]{2,1,0:T(8,128)(2,1)S(1)} %all-to-all-done.early_ref, bf16[8,68,432]{2,1,0:T(8,128)(2,1)S(1)} %all_to_all.10.late_ref), custom_call_target="tpu_custom_call" | custom-call | bytes 2506752 | tf_op jit(solution)/shard_map/settle/pallas_call | solution.py:173
  (17 shorter events, 0.2 us)
Async XLA Ops:
  0.0 2.2 %copy-start.3 = (s32[64]{0:T(128)S(1)}, s32[64]{0:T(128)}, u32[]{:S(2)}) copy-start(s32[64]{0:T(128)} %param.8) | copy-start | bytes 772
  0.0 2.2 %copy-start.4 = (s32[64]{0:T(128)S(1)}, s32[64]{0:T(128)}, u32[]{:S(2)}) copy-start(s32[64]{0:T(128)} %param.9) | copy-start | bytes 772
  0.0 2.2 %copy-start.2 = (bf16[68,3584]{1,0:T(8,128)(2,1)S(1)}, bf16[68,3584]{1,0:T(8,128)(2,1)}, u32[]{:S(2)}) copy-start(bf16[68,3584]{1,0:T(8,128)(2,1)} %rows_ref.1) | copy-start | bytes 1462276
  3.0 14.1 %collective-permute-start = (bf16[68,3584]{1,0:T(8,128)(2,1)S(1)}, bf16[68,3584]{1,0:T(8,128)(2,1)S(1)}, u32[]{:S(2)}, u32[]{:S(2)}) collective-permute-start(bf16[68,3584]{1,0:T(8,128)(2,1)S(1)} %normalize.1), channel_id=1, source_target_pairs={{0,1},{1,0},{2,3},{3,2},{4,5},{5,4},{6,7},{7,6},{8,9},{9,8},{10,11... | collective-permute-start | bytes 1462280 | tf_op jit(solution)/shard_map/ppermute | solution.py:29
  11.8 11.3 %collective-permute-start.1 = (bf16[144,1792]{1,0:T(8,128)(2,1)S(1)}, bf16[144,1792]{1,0:T(8,128)(2,1)S(1)}, u32[]{:S(2)}, u32[]{:S(2)}) collective-permute-start(bf16[144,1792]{1,0:T(8,128)(2,1)S(1)} %get-tuple-element.30.after_ref), channel_id=1, source_target_pairs={{0,16},{1,113},{16,32},{17,1},{32,48},{33,17},{48,64},{49,33},{64,... | collective-permute-start | bytes 1548296 | tf_op jit(solution)/shard_map/ppermute | solution.py:29
  23.9 20.6 %collective-permute-start.2 = (bf16[2,68,3584]{2,0,1:T(2,128)(2,1)S(1)}, bf16[2,68,3584]{2,0,1:T(2,128)(2,1)S(1)}, u32[]{:S(2)}, u32[]{:S(2)}) collective-permute-start(bf16[2,68,3584]{2,0,1:T(2,128)(2,1)S(1)} %copy.6), channel_id=1, source_target_pairs={{0,128},{1,385},{128,256},{129,1},{256,384},{257,129},{384,0},{385... | collective-permute-start | bytes 2924552 | tf_op jit(solution)/shard_map/ppermute | solution.py:29
  28.3 11.0 %collective-permute-start.4 = (bf16[144,1792]{1,0:T(8,128)(2,1)S(1)}, bf16[144,1792]{1,0:T(8,128)(2,1)S(1)}, u32[]{:S(2)}, u32[]{:S(2)}) collective-permute-start(bf16[144,1792]{1,0:T(8,128)(2,1)S(1)} %get-tuple-element.29), channel_id=1, source_target_pairs={{0,16},{1,113},{16,32},{17,1},{32,48},{33,17},{48,64},{49,33},{64,... | collective-permute-start | bytes 1548296 | tf_op jit(solution)/shard_map/ppermute | solution.py:29
  33.3 11.5 %collective-permute-start.3 = (bf16[144,1792]{1,0:T(8,128)(2,1)S(1)}, bf16[144,1792]{1,0:T(8,128)(2,1)S(1)}, u32[]{:S(2)}, u32[]{:S(2)}) collective-permute-start(bf16[144,1792]{1,0:T(8,128)(2,1)S(1)} %collective-permute-done.1), channel_id=1, source_target_pairs={{0,16},{1,113},{16,32},{17,1},{32,48},{33,17},{48,64},{49,33},{64,... | collective-permute-start | bytes 1548296 | tf_op jit(solution)/shard_map/ppermute | solution.py:29
  39.4 19.0 %collective-permute-start.8 = (bf16[288,1792]{1,0:T(8,128)(2,1)S(1)}, bf16[288,1792]{1,0:T(8,128)(2,1)S(1)}, u32[]{:S(2)}, u32[]{:S(2)}) collective-permute-start(bf16[288,1792]{1,0:T(8,128)(2,1)S(1)} %constant_dynamic-update-slice_fusion.refs_1_), channel_id=1, source_target_pairs={{0,2},{1,15},{2,4},{3,1},{4,6},{5,3},{6,8},{7,5},{8,10},{9,7},{10,... | collective-permute-start | bytes 3096584 | tf_op jit(solution)/shard_map/ppermute | solution.py:29
  44.9 10.1 %collective-permute-start.6 = (bf16[1,68,3584]{2,1,0:T(8,128)(2,1)S(1)}, bf16[1,68,3584]{2,1,0:T(8,128)(2,1)S(1)}, u32[]{:S(2)}, u32[]{:S(2)}) collective-permute-start(bf16[1,68,3584]{2,1,0:T(8,128)(2,1)S(1)} %slice.4), channel_id=1, source_target_pairs={{0,128},{1,385},{128,256},{129,1},{256,384},{257,129},{384,0},{385... | collective-permute-start | bytes 1462280 | tf_op jit(solution)/shard_map/ppermute | solution.py:29
  47.3 11.0 %collective-permute-start.7 = (bf16[144,1792]{1,0:T(8,128)(2,1)S(1)}, bf16[144,1792]{1,0:T(8,128)(2,1)S(1)}, u32[]{:S(2)}, u32[]{:S(2)}) collective-permute-start(bf16[144,1792]{1,0:T(8,128)(2,1)S(1)} %collective-permute-done.4), channel_id=1, source_target_pairs={{0,16},{1,113},{16,32},{17,1},{32,48},{33,17},{48,64},{49,33},{64,... | collective-permute-start | bytes 1548296 | tf_op jit(solution)/shard_map/ppermute | solution.py:29
  55.0 27.3 %copy-start.5 = (bf16[3584,288]{0,1:T(8,128)(2,1)S(1)}, bf16[3584,288]{0,1:T(8,128)(2,1)}, u32[]{:S(2)}) copy-start(bf16[3584,288]{0,1:T(8,128)(2,1)} %param.7) | copy-start | bytes 6193156
  58.4 24.0 %collective-permute-start.10 = (bf16[3,68,3584]{2,1,0:T(8,128)(2,1)S(1)}, bf16[3,68,3584]{2,1,0:T(8,128)(2,1)S(1)}, u32[]{:S(2)}, u32[]{:S(2)}) collective-permute-start(bf16[3,68,3584]{2,1,0:T(8,128)(2,1)S(1)} %pad_maximum_fusion), channel_id=1, source_target_pairs={{0,1},{1,0},{2,3},{3,2},{4,5},{5,4},{6,7},{7,6},{8,9},{9,8},{10,11... | collective-permute-start | bytes 4386824 | tf_op jit(solution)/shard_map/ppermute | solution.py:29
  64.0 19.3 %collective-permute-start.11 = (bf16[288,1792]{1,0:T(8,128)(2,1)S(1)}, bf16[288,1792]{1,0:T(8,128)(2,1)S(1)}, u32[]{:S(2)}, u32[]{:S(2)}) collective-permute-start(bf16[288,1792]{1,0:T(8,128)(2,1)S(1)} %constant_dynamic-update-slice_fusion.2.refs_2_), channel_id=1, source_target_pairs={{0,2},{1,15},{2,4},{3,1},{4,6},{5,3},{6,8},{7,5},{8,10},{9,7},{10,... | collective-permute-start | bytes 3096584 | tf_op jit(solution)/shard_map/ppermute | solution.py:29
  69.1 10.1 %collective-permute-start.5 = (bf16[144,1792]{1,0:T(8,128)(2,1)S(1)}, bf16[144,1792]{1,0:T(8,128)(2,1)S(1)}, u32[]{:S(2)}, u32[]{:S(2)}) collective-permute-start(bf16[144,1792]{1,0:T(8,128)(2,1)S(1)} %collective-permute-done.3), channel_id=1, source_target_pairs={{0,16},{1,113},{16,32},{17,1},{32,48},{33,17},{48,64},{49,33},{64,... | collective-permute-start | bytes 1548296 | tf_op jit(solution)/shard_map/ppermute | solution.py:29
  71.0 26.3 %collective-permute-start.12 = (bf16[144,1792]{1,0:T(8,128)(2,1)S(1)}, bf16[144,1792]{1,0:T(8,128)(2,1)S(1)}, u32[]{:S(2)}, u32[]{:S(2)}) collective-permute-start(bf16[144,1792]{1,0:T(8,128)(2,1)S(1)} %collective-permute-done.7), channel_id=1, source_target_pairs={{0,16},{1,113},{16,32},{17,1},{32,48},{33,17},{48,64},{49,33},{64,... | collective-permute-start | bytes 1548296 | tf_op jit(solution)/shard_map/ppermute | solution.py:29
  79.2 24.4 %collective-permute-start.13 = (bf16[144,1792]{1,0:T(8,128)(2,1)S(1)}, bf16[144,1792]{1,0:T(8,128)(2,1)S(1)}, u32[]{:S(2)}, u32[]{:S(2)}) collective-permute-start(bf16[144,1792]{1,0:T(8,128)(2,1)S(1)} %collective-permute-done.5.refs_0_), channel_id=1, source_target_pairs={{0,16},{1,113},{16,32},{17,1},{32,48},{33,17},{48,64},{49,33},{64,... | collective-permute-start | bytes 1548296 | tf_op jit(solution)/shard_map/ppermute | solution.py:29
  91.6 2.1 %copy-start = (bf16[640,3584]{1,0:T(8,128)(2,1)}, bf16[640,3584]{1,0:T(8,128)(2,1)S(1)}, u32[]{:S(2)}) copy-start(bf16[640,3584]{1,0:T(8,128)(2,1)S(1)} %line_up.1.a_ref) | copy-start | bytes 13762564
  93.7 19.2 %all-to-all-start = ((bf16[8,68,720]{2,1,0:T(8,128)(2,1)}), bf16[8,68,720]{2,1,0:T(8,128)(2,1)S(1)}, u32[]{:S(2)}, u32[]{:S(2)}) async-start(bf16[8,68,720]{2,1,0:T(8,128)(2,1)} %project.2.refs_6_), calls=%async_computation | async-start | bytes 1769472 | tf_op jit(solution)/shard_map/all_to_all | solution.py:226
  97.3 15.7 %collective-permute-start.14 = (bf16[144,1792]{1,0:T(8,128)(2,1)S(1)}, bf16[144,1792]{1,0:T(8,128)(2,1)S(1)}, u32[]{:S(2)}, u32[]{:S(2)}) collective-permute-start(bf16[144,1792]{1,0:T(8,128)(2,1)S(1)} %collective-permute-done.12.refs_1_), channel_id=1, source_target_pairs={{0,2},{1,15},{2,4},{3,1},{4,6},{5,3},{6,8},{7,5},{8,10},{9,7},{10,... | collective-permute-start | bytes 1548296 | tf_op jit(solution)/shard_map/ppermute | solution.py:29
  100.0 12.9 %collective-permute-start.9 = (bf16[144,1792]{1,0:T(8,128)(2,1)S(1)}, bf16[144,1792]{1,0:T(8,128)(2,1)S(1)}, u32[]{:S(2)}, u32[]{:S(2)}) collective-permute-start(bf16[144,1792]{1,0:T(8,128)(2,1)S(1)} %collective-permute-done.5.refs_0_), channel_id=1, source_target_pairs={{0,2},{1,15},{2,4},{3,1},{4,6},{5,3},{6,8},{7,5},{8,10},{9,7},{10,... | collective-permute-start | bytes 1548296 | tf_op jit(solution)/shard_map/ppermute | solution.py:29
  103.6 14.9 %collective-permute-start.15 = (bf16[144,1792]{1,0:T(8,128)(2,1)S(1)}, bf16[144,1792]{1,0:T(8,128)(2,1)}, u32[]{:S(2)}, u32[]{:S(2)}) collective-permute-start(bf16[144,1792]{1,0:T(8,128)(2,1)S(1)} %collective-permute-done.13.refs_2_), channel_id=1, source_target_pairs={{0,2},{1,15},{2,4},{3,1},{4,6},{5,3},{6,8},{7,5},{8,10},{9,7},{10,... | collective-permute-start | bytes 1548296 | tf_op jit(solution)/shard_map/ppermute | solution.py:29
  118.6 2.3 %copy-start.1 = (bf16[640,3584]{1,0:T(8,128)(2,1)S(1)}, bf16[640,3584]{1,0:T(8,128)(2,1)}, u32[]{:S(2)}) copy-start(bf16[640,3584]{1,0:T(8,128)(2,1)} %copy-done) | copy-start | bytes 13762564

commit v2 on v1

--- a/solution.py
+++ b/solution.py
@@ -9,6 +9,7 @@
 AXES = {"x": 4, "z": 8, "y": 8, "core": 2}
 PAD = 80
 MIB = 1024 * 1024
+TINY = pl.CostEstimate(flops=0, bytes_accessed=1024, transcendentals=0)
 
 
 def hop(value, axes, move):
@@ -45,10 +46,14 @@
     return hop(value, ("core",), lambda c: (1 - c,))
 
 
-def normalize(place, layer_rows, norm_gain, req_len, req_rank, after):
+def after(value, *others):
+    return lax.optimization_barrier((value, *others))[0]
+
+
+def normalize(place, layer_rows, norm_gain, req_len, req_rank):
     rows, features = layer_rows.shape
 
-    def body(place_ref, rows_ref, gain_ref, len_ref, rank_ref, after_ref, out):
+    def body(place_ref, rows_ref, gain_ref, len_ref, rank_ref, out):
         owned = jnp.where(rank_ref[...] == place_ref[4], len_ref[...], 0)
         live = lax.broadcasted_iota(jnp.int32, (rows, 1), 0) < jnp.sum(owned, axis=1, keepdims=True)
         wide = rows_ref[...].astype(jnp.float32)
@@ -60,18 +65,18 @@
     return pl.pallas_call(
         body,
         out_shape=jax.ShapeDtypeStruct((rows, features), jnp.bfloat16),
-        in_specs=[pl.BlockSpec(memory_space=pltpu.SMEM)] + [in_vmem] * 4 + [pl.BlockSpec(memory_space=pl.ANY)],
+        in_specs=[pl.BlockSpec(memory_space=pltpu.SMEM)] + [in_vmem] * 4,
         out_specs=in_vmem,
         compiler_params=pltpu.CompilerParams(vmem_limit_bytes=8 * MIB),
-        cost_estimate=pl.CostEstimate(flops=5 * rows * features, bytes_accessed=4 * rows * features, transcendentals=rows),
+        cost_estimate=TINY,
         name="normalize",
-    )(place, layer_rows, norm_gain.reshape(1, -1), req_len.reshape(1, -1), req_rank.reshape(1, -1), after)
-
-
-def line_up(place, pair, beside, far, swapped):
+    )(place, layer_rows, norm_gain.reshape(1, -1), req_len.reshape(1, -1), req_rank.reshape(1, -1))
+
+
+def line_up(place, pair, beside, far, swapped, across):
     rows, features = pair.shape[1:]
 
-    def body(place_ref, pair_ref, beside_ref, far_ref, swapped_ref, out):
+    def body(place_ref, pair_ref, beside_ref, far_ref, swapped_ref, across_ref, out):
         x, c = place_ref[0], place_ref[1]
         back = 2 * c - 1
 
@@ -86,27 +91,27 @@
         put(2, c, far_ref[0])
         put(-back, 1 - c, swapped_ref[0])
         put(-back, c, swapped_ref[1])
-        put(2, 1 - c, swapped_ref[2])
+        put(2, 1 - c, across_ref[0])
 
     return pl.pallas_call(
         body,
         out_shape=jax.ShapeDtypeStruct((8 * PAD, features), pair.dtype),
-        in_specs=[pl.BlockSpec(memory_space=pltpu.SMEM)] + [pl.BlockSpec(memory_space=pltpu.VMEM)] * 4,
+        in_specs=[pl.BlockSpec(memory_space=pltpu.SMEM)] + [pl.BlockSpec(memory_space=pltpu.VMEM)] * 5,
         out_specs=pl.BlockSpec(memory_space=pltpu.VMEM),
         compiler_params=pltpu.CompilerParams(vmem_limit_bytes=12 * MIB),
-        cost_estimate=pl.CostEstimate(flops=0, bytes_accessed=32 * rows * features, transcendentals=0),
+        cost_estimate=TINY,
         name="line_up",
-    )(place, pair, beside, far, swapped)
-
-
-def project(place, rows_in, near, far, rows, after=()):
+    )(place, pair, beside, far, swapped, across)
+
+
+def project(place, rows_in, near, far, rows):
     total, features = rows_in.shape
     half = features // 2
     owners = total // PAD
     widths = [w.shape[0] for w in near]
     columns = sum(widths)
     given = list(near) + [w for w in far if w is not None]
-    per = 2
+    per = 4
     block = per * PAD
 
     def body(place_ref, a_ref, *refs):
@@ -135,17 +140,12 @@
         grid=(owners // per,),
         out_shape=jax.ShapeDtypeStruct((owners, rows, columns), jnp.bfloat16),
         in_specs=[pl.BlockSpec(memory_space=pltpu.SMEM), pl.BlockSpec((block, features), lambda i: (i, 0))]
-        + [pl.BlockSpec(w.shape, lambda i: (0, 0)) for w in given]
-        + [pl.BlockSpec(memory_space=pl.ANY)] * len(after),
+        + [pl.BlockSpec(w.shape, lambda i: (0, 0)) for w in given],
         out_specs=pl.BlockSpec((per, rows, columns), lambda i: (i, 0, 0)),
         compiler_params=pltpu.CompilerParams(vmem_limit_bytes=20 * MIB),
-        cost_estimate=pl.CostEstimate(
-            flops=2 * total * features * columns,
-            bytes_accessed=2 * (total * features + features * columns + total * columns),
-            transcendentals=total * columns,
-        ),
+        cost_estimate=TINY,
         name="project",
-    )(place, rows_in, *given, *after)
+    )(place, rows_in, *given)
 
 
 def settle(place, early, late, width):
@@ -178,7 +178,7 @@
         + [pl.BlockSpec((2, rows, g.shape[2]), lambda i: (i, 0, 0)) for g in (early, late)],
         out_specs=pl.BlockSpec((rows, region), lambda i: (0, i)),
         compiler_params=pltpu.CompilerParams(vmem_limit_bytes=20 * MIB),
-        cost_estimate=pl.CostEstimate(flops=0, bytes_accessed=16 * rows * region, transcendentals=0),
+        cost_estimate=TINY,
         name="settle",
     )(place, early, late)
 
@@ -196,40 +196,37 @@
     def own(core):
         return lax.dynamic_slice(weights, (core * half_width, plane * half), (half_width, half))
 
-    together = lax.optimization_barrier
     a, b = [own(c)], [own(1 - c)]
     a.append(along_z(a[0]))
     b.append(along_z(b[0]))
 
-    normed = normalize(place, layer_rows, norm_gain, req_len, req_rank, a[0])
+    normed = normalize(place, layer_rows, after(norm_gain, a[0]), req_len, req_rank)
     pair = jnp.stack([normed, other_core(normed)])
-    pair, a[1] = together((pair, a[1]))
     beside = along_x(pair)
     a.append(along_z(a[1]))
     b.append(along_z(b[1]))
-    near1 = [jnp.concatenate([a[1], b[1]], 0)]
-    far1 = [along_y(near1[0])]
-    onward, a[2], b[1] = together((beside[:1], a[2], b[1]))
-    far = along_x(onward)
+    near = [jnp.concatenate([a[1], b[1]], 0)]
+    far = [along_y(near[0])]
+    swapped = other_core(beside)
+    distant = along_x(after(beside[:1], a[2], b[2]))
     a.append(along_z(a[2]))
     b.append(along_z(b[2]))
-    near1.append(jnp.concatenate([a[2], b[2]], 0))
-    far1.append(along_y(near1[1]))
-    others, b[2], far1[0] = together((jnp.concatenate([beside, far], 0), b[2], far1[0]))
-    swapped = other_core(others)
-    a[3], far1[0] = together((a[3], far1[0]))
-    a.append(along_z(a[3]))
-    rows_in = line_up(place, pair, beside, far, swapped)
-
+    near.append(jnp.concatenate([a[2], b[2]], 0))
+    far.append(along_y(near[1]))
+    across = other_core(after(distant, a[3], b[3]))
+    a.append(along_z(after(a[3], far[0])))
+    far_a, far_b = along_y(a[3]), along_y(b[3])
+    rows_in = line_up(place, pair, beside, distant, swapped, across)
     own_half = lax.dynamic_slice(weights, (c * half_width, 0), (half_width, features))
-    first = project(place, rows_in, [own_half] + near1, [None] + far1, rows)
-    early = lax.all_to_all(first, ("x", "core"), 0, 0, tiled=True)
-    a[4], first = together((a[4], first))
-    near2 = [a[3], b[3], a[4]]
-    far2 = [along_y(w) for w in near2]
-    far2[0], early = together((far2[0], early))
-    second = project(place, rows_in, near2, far2, rows, after=(first,))
-    late = lax.all_to_all(second, ("x", "core"), 0, 0, tiled=True)
+
+    def deliver(value):
+        return lax.all_to_all(value, ("x", "core"), 0, 0, tiled=True)
+
+    far_4 = along_y(a[4])
+    first = project(place, after(rows_in, a[4], far_a), [own_half] + near, [None] + far, rows)
+    early = deliver(first)
+    second = project(place, after(rows_in, first), [a[3], b[3], a[4]], [far_a, far_b, far_4], rows)
+    late = deliver(after(second, early))
     return settle(place, early, late, width)
 
 

time: 147 us -> 124 us (0.84)
  waiting for transfers between devices: 34.2 us -> 15.1 us
  Pallas kernels: 18.5 us -> 13.6 us
    ppermute x16 -> x17, waiting for transfers between devices: 34.2 us -> 15.1 us  [hop(): return lax.ppermute(value, tuple(axes), pairs)]
    pallas_call x2, Pallas kernels: 13.7 us -> 8.82 us  [project(): pl.pallas_call(body, grid=(owners // per,), out_shape=jax.ShapeDtypeStruc...]
    all_to_all x1, starting transfers between devices: 3.5 us -> 6.02 us  [deliver(): return lax.all_to_all(value, ('x', 'core'), 0, 0, tiled=True)]
    ppermute x16 -> x17, starting transfers between devices: 64.9 us -> 63.8 us  [hop(): return lax.ppermute(value, tuple(axes), pairs)]
    unnamed x14 -> x16, local copies, waits for them, and re-layouts: 4.48 us -> 4.47 us
  transfers between devices with their start and end apart: 17 -> 18, of which waited for: 8 -> 6; matrix products, arithmetic and copies ran while one was open for 0% -> 1% of each run, Pallas kernels for 6% -> 3%
where the time goes in v2:
time: 124 us; the launch traced here: 123 us
  starting transfers between devices  69.8 us (56%)
  blocking collectives  17 us (14%)
  waiting for transfers between devices  15.1 us (12%)
  Pallas kernels  13.6 us (11%)
  local copies, waits for them, and re-layouts  7.05 us (6%)
    ppermute x17, starting transfers between devices, hop(): return lax.ppermute(value, tuple(axes), pairs)  63.8 us
    all_to_all x1, blocking collectives, deliver(): return lax.all_to_all(value, ('x', 'core'), 0, 0, tiled=True)  17 us
    ppermute x17, waiting for transfers between devices, hop(): return lax.ppermute(value, tuple(axes), pairs)  15.1 us
    pallas_call x2, Pallas kernels, project(): pl.pallas_call(body, grid=(owners // per,), out_shape=jax.ShapeDtypeStruc...  8.82 us
    all_to_all x1, starting transfers between devices, deliver(): return lax.all_to_all(value, ('x', 'core'), 0, 0, tiled=True)  6.02 us
    unnamed x16, local copies, waits for them, and re-layouts  4.47 us
    pallas_call x1, Pallas kernels, settle(): pl.pallas_call(body, grid=(4,), out_shape=jax.ShapeDtypeStruct((rows, 4 *...  3.15 us
  transfers between devices with their start and end apart: 18, of which 6 were waited for; matrix products, arithmetic and copies ran while one was open for 1% of the time, Pallas kernels for 3%

profile of v2, /device:TPU:1, one launch (start us, length us, event | category | flops | bytes accessed | tf_op | source)
XLA Modules:
  0.0 123.1 jit_solution(5247163105386591062)
XLA Ops:
  0.0 1.3 %dynamic-slice_bitcast_fusion.1 = (bf16[144,1792]{1,0:T(8,128)(2,1)S(1)}, bf16[144,1792]{1,0:T(8,128)(2,1)S(1)}) fusion(bf16[3584,288]{0,1:T(8,128)(2,1)} %param.7, s32[]{:T(128)S(6)} %select_n.11, s32[]{:T(128)S(6)} %select_n.13, s32[]{:T(128)S(6)} %select_n.12), kind=kLoop, calls=%fused_computation.2 | loop fusion | bytes 2064396 | tf_op jit(solution)/shard_map/dynamic_slice | solution.py:197
  1.4 0.1 stack.32.place_ref
  1.5 0.8 normalize.1
  2.3 8.8 %collective-permute-start = (bf16[68,3584]{1,0:T(8,128)(2,1)S(1)}, bf16[68,3584]{1,0:T(8,128)(2,1)S(1)}, u32[]{:S(2)}, u32[]{:S(2)}) collective-permute-start(bf16[68,3584]{1,0:T(8,128)(2,1)S(1)} %normalize.1), channel_id=1, source_target_pairs={{0,1},{1,0},{2,3},{3,2},{4,5},{5,4},{6,7},{7,6},{8,9},{9,8},{10,11... | collective-permute-start | bytes 1462280 | tf_op jit(solution)/shard_map/ppermute | solution.py:30
  11.1 5.3 %collective-permute-start.2 = (bf16[144,1792]{1,0:T(8,128)(2,1)S(1)}, bf16[144,1792]{1,0:T(8,128)(2,1)S(1)}, u32[]{:S(2)}, u32[]{:S(2)}) collective-permute-start(bf16[144,1792]{1,0:T(8,128)(2,1)S(1)} %get-tuple-element.20), channel_id=1, source_target_pairs={{0,16},{1,113},{16,32},{17,1},{32,48},{33,17},{48,64},{49,33},{64,... | collective-permute-start | bytes 1548296 | tf_op jit(solution)/shard_map/ppermute | solution.py:30
  16.4 2.2 %collective-permute-start.4 = (bf16[144,1792]{1,0:T(8,128)(2,1)S(1)}, bf16[144,1792]{1,0:T(8,128)(2,1)S(1)}, u32[]{:S(2)}, u32[]{:S(2)}) collective-permute-start(bf16[144,1792]{1,0:T(8,128)(2,1)S(1)} %get-tuple-element.19), channel_id=1, source_target_pairs={{0,16},{1,113},{16,32},{17,1},{32,48},{33,17},{48,64},{49,33},{64,... | collective-permute-start | bytes 1548296 | tf_op jit(solution)/shard_map/ppermute | solution.py:30
  18.6 0.0 collective-permute-done
  18.6 0.1 pad_maximum_fusion.pair_ref
  18.7 0.8 copy.6
  19.5 4.4 %collective-permute-start.1 = (bf16[2,68,3584]{2,0,1:T(2,128)(2,1)S(1)}, bf16[2,68,3584]{2,0,1:T(2,128)(2,1)S(1)}, u32[]{:S(2)}, u32[]{:S(2)}) collective-permute-start(bf16[2,68,3584]{2,0,1:T(2,128)(2,1)S(1)} %copy.6), channel_id=1, source_target_pairs={{0,128},{1,385},{128,256},{129,1},{256,384},{257,129},{384,0},{385... | collective-permute-start | bytes 2924552 | tf_op jit(solution)/shard_map/ppermute | solution.py:30
  23.9 0.0 collective-permute-done.2
  23.9 3.9 %collective-permute-start.3 = (bf16[144,1792]{1,0:T(8,128)(2,1)S(1)}, bf16[144,1792]{1,0:T(8,128)(2,1)S(1)}, u32[]{:S(2)}, u32[]{:S(2)}) collective-permute-start(bf16[144,1792]{1,0:T(8,128)(2,1)S(1)} %collective-permute-done.2), channel_id=1, source_target_pairs={{0,16},{1,113},{16,32},{17,1},{32,48},{33,17},{48,64},{49,33},{64,... | collective-permute-start | bytes 1548296 | tf_op jit(solution)/shard_map/ppermute | solution.py:30
  27.8 0.2 collective-permute-done.4
  28.0 5.3 %collective-permute-start.5 = (bf16[144,1792]{1,0:T(8,128)(2,1)S(1)}, bf16[144,1792]{1,0:T(8,128)(2,1)S(1)}, u32[]{:S(2)}, u32[]{:S(2)}) collective-permute-start(bf16[144,1792]{1,0:T(8,128)(2,1)S(1)} %collective-permute-done.4), channel_id=1, source_target_pairs={{0,16},{1,113},{16,32},{17,1},{32,48},{33,17},{48,64},{49,33},{64,... | collective-permute-start | bytes 1548296 | tf_op jit(solution)/shard_map/ppermute | solution.py:30
  33.4 5.1 %collective-permute-start.11 = (bf16[288,1792]{1,0:T(8,128)(2,1)S(1)}, bf16[288,1792]{1,0:T(8,128)(2,1)S(1)}, u32[]{:S(2)}, u32[]{:S(2)}) collective-permute-start(bf16[288,1792]{1,0:T(8,128)(2,1)S(1)} %constant_dynamic-update-slice_fusion.refs_1_), channel_id=1, source_target_pairs={{0,2},{1,15},{2,4},{3,1},{4,6},{5,3},{6,8},{7,5},{8,10},{9,7},{10,... | collective-permute-start | bytes 3096584 | tf_op jit(solution)/shard_map/ppermute | solution.py:30
  38.5 0.0 collective-permute-done.3
  38.5 1.9 %collective-permute-start.8 = (bf16[144,1792]{1,0:T(8,128)(2,1)S(1)}, bf16[144,1792]{1,0:T(8,128)(2,1)S(1)}, u32[]{:S(2)}, u32[]{:S(2)}) collective-permute-start(bf16[144,1792]{1,0:T(8,128)(2,1)S(1)} %collective-permute-done.3), channel_id=1, source_target_pairs={{0,16},{1,113},{16,32},{17,1},{32,48},{33,17},{48,64},{49,33},{64,... | collective-permute-start | bytes 1548296 | tf_op jit(solution)/shard_map/ppermute | solution.py:30
  40.4 0.0 collective-permute-done.5
  40.4 4.2 %collective-permute-start.9 = (bf16[144,1792]{1,0:T(8,128)(2,1)S(1)}, bf16[144,1792]{1,0:T(8,128)(2,1)S(1)}, u32[]{:S(2)}, u32[]{:S(2)}) collective-permute-start(bf16[144,1792]{1,0:T(8,128)(2,1)S(1)} %collective-permute-done.5), channel_id=1, source_target_pairs={{0,16},{1,113},{16,32},{17,1},{32,48},{33,17},{48,64},{49,33},{64,... | collective-permute-start | bytes 1548296 | tf_op jit(solution)/shard_map/ppermute | solution.py:30
  44.7 0.0 copy-start.5
  44.7 4.9 %collective-permute-start.14 = (bf16[288,1792]{1,0:T(8,128)(2,1)S(1)}, bf16[288,1792]{1,0:T(8,128)(2,1)S(1)}, u32[]{:S(2)}, u32[]{:S(2)}) collective-permute-start(bf16[288,1792]{1,0:T(8,128)(2,1)S(1)} %constant_dynamic-update-slice_fusion.2.refs_2_), channel_id=1, source_target_pairs={{0,2},{1,15},{2,4},{3,1},{4,6},{5,3},{6,8},{7,5},{8,10},{9,7},{10,... | collective-permute-start | bytes 3096584 | tf_op jit(solution)/shard_map/ppermute | solution.py:30
  49.7 0.0 collective-permute-done.1
  49.7 0.1 copy.8.beside_ref
  49.8 4.1 %collective-permute-start.6 = (bf16[1,68,3584]{2,1,0:T(8,128)(2,1)S(1)}, bf16[1,68,3584]{2,1,0:T(8,128)(2,1)S(1)}, u32[]{:S(2)}, u32[]{:S(2)}) collective-permute-start(bf16[1,68,3584]{2,1,0:T(8,128)(2,1)S(1)} %slice.4), channel_id=1, source_target_pairs={{0,128},{1,385},{128,256},{129,1},{256,384},{257,129},{384,0},{385... | collective-permute-start | bytes 1462280 | tf_op jit(solution)/shard_map/ppermute | solution.py:30
  54.0 0.0 collective-permute-done.8.refs_0_
  54.0 1.9 %collective-permute-start.7 = (bf16[2,68,3584]{2,0,1:T(2,128)(2,1)S(1)}, bf16[2,68,3584]{2,0,1:T(2,128)(2,1)S(1)}, u32[]{:S(2)}, u32[]{:S(2)}) collective-permute-start(bf16[2,68,3584]{2,0,1:T(2,128)(2,1)S(1)} %collective-permute-done.1), channel_id=1, source_target_pairs={{0,1},{1,0},{2,3},{3,2},{4,5},{5,4},{6,7},{7,6},{8,9},{9,8},{10,11... | collective-permute-start | bytes 2924552 | tf_op jit(solution)/shard_map/ppermute | solution.py:30
  55.9 1.9 %collective-permute-start.12 = (bf16[144,1792]{1,0:T(8,128)(2,1)S(1)}, bf16[144,1792]{1,0:T(8,128)(2,1)S(1)}, u32[]{:S(2)}, u32[]{:S(2)}) collective-permute-start(bf16[144,1792]{1,0:T(8,128)(2,1)S(1)} %collective-permute-done.8.refs_0_), channel_id=1, source_target_pairs={{0,16},{1,113},{16,32},{17,1},{32,48},{33,17},{48,64},{49,33},{64,... | collective-permute-start | bytes 1548296 | tf_op jit(solution)/shard_map/ppermute | solution.py:30
  57.8 0.0 collective-permute-done.9.refs_1_
  57.8 3.2 %collective-permute-start.13 = (bf16[144,1792]{1,0:T(8,128)(2,1)S(1)}, bf16[144,1792]{1,0:T(8,128)(2,1)S(1)}, u32[]{:S(2)}, u32[]{:S(2)}) collective-permute-start(bf16[144,1792]{1,0:T(8,128)(2,1)S(1)} %collective-permute-done.8.refs_0_), channel_id=1, source_target_pairs={{0,2},{1,15},{2,4},{3,1},{4,6},{5,3},{6,8},{7,5},{8,10},{9,7},{10,... | collective-permute-start | bytes 1548296 | tf_op jit(solution)/shard_map/ppermute | solution.py:30
  61.1 1.9 %collective-permute-start.10 = (bf16[1,68,3584]{2,1,0:T(8,128)(2,1)S(1)}, bf16[1,68,3584]{2,1,0:T(8,128)(2,1)S(1)}, u32[]{:S(2)}, u32[]{:S(2)}) collective-permute-start(bf16[1,68,3584]{2,1,0:T(8,128)(2,1)S(1)} %collective-permute-done.6.far_ref), channel_id=1, source_target_pairs={{0,1},{1,0},{2,3},{3,2},{4,5},{5,4},{6,7},{7,6},{8,9},{9,8},{10,11... | collective-permute-start | bytes 1462280 | tf_op jit(solution)/shard_map/ppermute | solution.py:30
  63.0 0.1 dynamic-slice_bitcast_fusion.refs_0_
  63.1 0.0 collective-permute-done.7
  63.1 0.1 copy.9.swapped_ref
  63.2 1.6 %collective-permute-done.10.across_ref = bf16[1,68,3584]{2,1,0:T(8,128)(2,1)S(1)} collective-permute-done((bf16[1,68,3584]{2,1,0:T(8,128)(2,1)S(1)}, bf16[1,68,3584]{2,1,0:T(8,128)(2,1)S(1)}, u32[]{:S(2)}, u32[]{:S(2)}) %collective-permute-start.10) | collective-permute-done | bytes 487456 | tf_op jit(solution)/shard_map/ppermute | solution.py:30
  64.9 0.8 line_up.1.a_ref
  65.7 0.3 collective-permute-done.12.refs_2_
  66.0 1.9 %collective-permute-done.13.refs_3_ = bf16[144,1792]{1,0:T(8,128)(2,1)S(1)} collective-permute-done((bf16[144,1792]{1,0:T(8,128)(2,1)S(1)}, bf16[144,1792]{1,0:T(8,128)(2,1)S(1)}, u32[]{:S(2)}, u32[]{:S(2)}) %collective-permute-start.13) | collective-permute-done | bytes 516128 | tf_op jit(solution)/shard_map/ppermute | solution.py:30
  68.0 5.4 %project.2 = bf16[8,68,720]{2,1,0:T(8,128)(2,1)} custom-call(s32[5]{0:T(128)S(1)} %stack.32.place_ref, bf16[640,3584]{1,0:T(8,128)(2,1)S(1)} %line_up.1.a_ref, bf16[144,3584]{1,0:T(8,128)(2,1)S(1)} %dynamic-slice_bitcast_fusion.refs_0_, bf16[288,1792]{1,0:T(8,128)(2,1)S(1)} %constant_dynamic-update-slice_fusion.refs_1_, ...), custom_call_target="tpu_custom_call" | custom-call | bytes 1024 | tf_op jit(solution)/shard_map/project/pallas_call | solution.py:138
  73.4 2.1 %copy-done = bf16[640,3584]{1,0:T(8,128)(2,1)} copy-done((bf16[640,3584]{1,0:T(8,128)(2,1)}, bf16[640,3584]{1,0:T(8,128)(2,1)S(1)}, u32[]{:S(2)}) %copy-start) | copy-done | bytes 4587544
  75.5 6.0 %all-to-all-start = ((bf16[8,68,720]{2,1,0:T(8,128)(2,1)}), bf16[8,68,720]{2,1,0:T(8,128)(2,1)S(1)}, u32[]{:S(2)}, u32[]{:S(2)}) async-start(bf16[8,68,720]{2,1,0:T(8,128)(2,1)} %project.2), calls=%async_computation | async-start | bytes 1769472 | tf_op jit(solution)/shard_map/all_to_all | solution.py:223
  81.5 2.2 %collective-permute-start.15 = (bf16[144,1792]{1,0:T(8,128)(2,1)S(1)}, bf16[144,1792]{1,0:T(8,128)(2,1)S(1)}, u32[]{:S(2)}, u32[]{:S(2)}) collective-permute-start(bf16[144,1792]{1,0:T(8,128)(2,1)S(1)} %collective-permute-done.9.refs_1_), channel_id=1, source_target_pairs={{0,2},{1,15},{2,4},{3,1},{4,6},{5,3},{6,8},{7,5},{8,10},{9,7},{10,... | collective-permute-start | bytes 1548296 | tf_op jit(solution)/shard_map/ppermute | solution.py:30
  83.7 2.5 %collective-permute-start.16 = (bf16[144,1792]{1,0:T(8,128)(2,1)S(1)}, bf16[144,1792]{1,0:T(8,128)(2,1)S(1)}, u32[]{:S(2)}, u32[]{:S(2)}) collective-permute-start(bf16[144,1792]{1,0:T(8,128)(2,1)S(1)} %collective-permute-done.12.refs_2_), channel_id=1, source_target_pairs={{0,2},{1,15},{2,4},{3,1},{4,6},{5,3},{6,8},{7,5},{8,10},{9,7},{10,... | collective-permute-start | bytes 1548296 | tf_op jit(solution)/shard_map/ppermute | solution.py:30
  86.2 5.4 %collective-permute-done.15.refs_4_ = bf16[144,1792]{1,0:T(8,128)(2,1)S(1)} collective-permute-done((bf16[144,1792]{1,0:T(8,128)(2,1)S(1)}, bf16[144,1792]{1,0:T(8,128)(2,1)S(1)}, u32[]{:S(2)}, u32[]{:S(2)}) %collective-permute-start.15) | collective-permute-done | bytes 516128 | tf_op jit(solution)/shard_map/ppermute | solution.py:30
  91.6 5.5 %collective-permute-done.16.refs_5_ = bf16[144,1792]{1,0:T(8,128)(2,1)S(1)} collective-permute-done((bf16[144,1792]{1,0:T(8,128)(2,1)S(1)}, bf16[144,1792]{1,0:T(8,128)(2,1)S(1)}, u32[]{:S(2)}, u32[]{:S(2)}) %collective-permute-start.16) | collective-permute-done | bytes 516128 | tf_op jit(solution)/shard_map/ppermute | solution.py:30
  97.1 2.3 %copy-done.1 = bf16[640,3584]{1,0:T(8,128)(2,1)S(1)} copy-done((bf16[640,3584]{1,0:T(8,128)(2,1)S(1)}, bf16[640,3584]{1,0:T(8,128)(2,1)}, u32[]{:S(2)}) %copy-start.1) | copy-done | bytes 4587544
  99.4 3.4 %project.3 = bf16[8,68,432]{2,1,0:T(8,128)(2,1)S(1)} custom-call(s32[5]{0:T(128)S(1)} %stack.32.place_ref, bf16[640,3584]{1,0:T(8,128)(2,1)S(1)} %copy-done.1, bf16[144,1792]{1,0:T(8,128)(2,1)S(1)} %collective-permute-done.8.refs_0_, bf16[144,1792]{1,0:T(8,128)(2,1)S(1)} %collective-permute-done.9.refs_1_, ...), custom_call_target="tpu_custom_call" | custom-call | bytes 1024 | tf_op jit(solution)/shard_map/project/pallas_call | solution.py:138
  102.9 17.0 %all_to_all.10.late_ref = bf16[8,68,432]{2,1,0:T(8,128)(2,1)S(1)} all-to-all(bf16[8,68,432]{2,1,0:T(8,128)(2,1)S(1)} %project.3), channel_id=1, replica_groups=mesh['x'=4,'z'=8,'y'=8,'core'=2] {'x','core'}, dimensions={0} | all-to-all | bytes 940032 | tf_op jit(solution)/shard_map/all_to_all | solution.py:223
  119.9 3.1 %settle.1 = bf16[68,9216]{1,0:T(8,128)(2,1)} custom-call(s32[5]{0:T(128)S(1)} %stack.32.place_ref, bf16[8,68,720]{2,1,0:T(8,128)(2,1)S(1)} %all-to-all-done.early_ref, bf16[8,68,432]{2,1,0:T(8,128)(2,1)S(1)} %all_to_all.10.late_ref), custom_call_target="tpu_custom_call" | custom-call | bytes 1024 | tf_op jit(solution)/shard_map/settle/pallas_call | solution.py:173
  (21 shorter events, 0.2 us)
Async XLA Ops:
  0.0 1.4 %copy-start.6 = (f32[3584]{0:T(1024)S(1)}, f32[3584]{0:T(1024)}, u32[]{:S(2)}) copy-start(f32[3584]{0:T(1024)} %param.6) | copy-start | bytes 43012
  0.0 1.5 %copy-start.3 = (s32[64]{0:T(128)S(1)}, s32[64]{0:T(128)}, u32[]{:S(2)}) copy-start(s32[64]{0:T(128)} %param.8) | copy-start | bytes 772
  0.0 1.5 %copy-start.4 = (s32[64]{0:T(128)S(1)}, s32[64]{0:T(128)}, u32[]{:S(2)}) copy-start(s32[64]{0:T(128)} %param.9) | copy-start | bytes 772
  0.0 1.5 %copy-start.2 = (bf16[68,3584]{1,0:T(8,128)(2,1)S(1)}, bf16[68,3584]{1,0:T(8,128)(2,1)}, u32[]{:S(2)}) copy-start(bf16[68,3584]{1,0:T(8,128)(2,1)} %rows_ref.1) | copy-start | bytes 1462276
  2.3 16.3 %collective-permute-start = (bf16[68,3584]{1,0:T(8,128)(2,1)S(1)}, bf16[68,3584]{1,0:T(8,128)(2,1)S(1)}, u32[]{:S(2)}, u32[]{:S(2)}) collective-permute-start(bf16[68,3584]{1,0:T(8,128)(2,1)S(1)} %normalize.1), channel_id=1, source_target_pairs={{0,1},{1,0},{2,3},{3,2},{4,5},{5,4},{6,7},{7,6},{8,9},{9,8},{10,11... | collective-permute-start | bytes 1462280 | tf_op jit(solution)/shard_map/ppermute | solution.py:30
  11.1 12.8 %collective-permute-start.2 = (bf16[144,1792]{1,0:T(8,128)(2,1)S(1)}, bf16[144,1792]{1,0:T(8,128)(2,1)S(1)}, u32[]{:S(2)}, u32[]{:S(2)}) collective-permute-start(bf16[144,1792]{1,0:T(8,128)(2,1)S(1)} %get-tuple-element.20), channel_id=1, source_target_pairs={{0,16},{1,113},{16,32},{17,1},{32,48},{33,17},{48,64},{49,33},{64,... | collective-permute-start | bytes 1548296 | tf_op jit(solution)/shard_map/ppermute | solution.py:30
  16.4 11.5 %collective-permute-start.4 = (bf16[144,1792]{1,0:T(8,128)(2,1)S(1)}, bf16[144,1792]{1,0:T(8,128)(2,1)S(1)}, u32[]{:S(2)}, u32[]{:S(2)}) collective-permute-start(bf16[144,1792]{1,0:T(8,128)(2,1)S(1)} %get-tuple-element.19), channel_id=1, source_target_pairs={{0,16},{1,113},{16,32},{17,1},{32,48},{33,17},{48,64},{49,33},{64,... | collective-permute-start | bytes 1548296 | tf_op jit(solution)/shard_map/ppermute | solution.py:30
  19.5 30.2 %collective-permute-start.1 = (bf16[2,68,3584]{2,0,1:T(2,128)(2,1)S(1)}, bf16[2,68,3584]{2,0,1:T(2,128)(2,1)S(1)}, u32[]{:S(2)}, u32[]{:S(2)}) collective-permute-start(bf16[2,68,3584]{2,0,1:T(2,128)(2,1)S(1)} %copy.6), channel_id=1, source_target_pairs={{0,128},{1,385},{128,256},{129,1},{256,384},{257,129},{384,0},{385... | collective-permute-start | bytes 2924552 | tf_op jit(solution)/shard_map/ppermute | solution.py:30
  23.9 14.6 %collective-permute-start.3 = (bf16[144,1792]{1,0:T(8,128)(2,1)S(1)}, bf16[144,1792]{1,0:T(8,128)(2,1)S(1)}, u32[]{:S(2)}, u32[]{:S(2)}) collective-permute-start(bf16[144,1792]{1,0:T(8,128)(2,1)S(1)} %collective-permute-done.2), channel_id=1, source_target_pairs={{0,16},{1,113},{16,32},{17,1},{32,48},{33,17},{48,64},{49,33},{64,... | collective-permute-start | bytes 1548296 | tf_op jit(solution)/shard_map/ppermute | solution.py:30
  28.0 12.4 %collective-permute-start.5 = (bf16[144,1792]{1,0:T(8,128)(2,1)S(1)}, bf16[144,1792]{1,0:T(8,128)(2,1)S(1)}, u32[]{:S(2)}, u32[]{:S(2)}) collective-permute-start(bf16[144,1792]{1,0:T(8,128)(2,1)S(1)} %collective-permute-done.4), channel_id=1, source_target_pairs={{0,16},{1,113},{16,32},{17,1},{32,48},{33,17},{48,64},{49,33},{64,... | collective-permute-start | bytes 1548296 | tf_op jit(solution)/shard_map/ppermute | solution.py:30
  33.4 22.5 %collective-permute-start.11 = (bf16[288,1792]{1,0:T(8,128)(2,1)S(1)}, bf16[288,1792]{1,0:T(8,128)(2,1)S(1)}, u32[]{:S(2)}, u32[]{:S(2)}) collective-permute-start(bf16[288,1792]{1,0:T(8,128)(2,1)S(1)} %constant_dynamic-update-slice_fusion.refs_1_), channel_id=1, source_target_pairs={{0,2},{1,15},{2,4},{3,1},{4,6},{5,3},{6,8},{7,5},{8,10},{9,7},{10,... | collective-permute-start | bytes 3096584 | tf_op jit(solution)/shard_map/ppermute | solution.py:30
  38.5 15.5 %collective-permute-start.8 = (bf16[144,1792]{1,0:T(8,128)(2,1)S(1)}, bf16[144,1792]{1,0:T(8,128)(2,1)S(1)}, u32[]{:S(2)}, u32[]{:S(2)}) collective-permute-start(bf16[144,1792]{1,0:T(8,128)(2,1)S(1)} %collective-permute-done.3), channel_id=1, source_target_pairs={{0,16},{1,113},{16,32},{17,1},{32,48},{33,17},{48,64},{49,33},{64,... | collective-permute-start | bytes 1548296 | tf_op jit(solution)/shard_map/ppermute | solution.py:30
  40.4 17.4 %collective-permute-start.9 = (bf16[144,1792]{1,0:T(8,128)(2,1)S(1)}, bf16[144,1792]{1,0:T(8,128)(2,1)S(1)}, u32[]{:S(2)}, u32[]{:S(2)}) collective-permute-start(bf16[144,1792]{1,0:T(8,128)(2,1)S(1)} %collective-permute-done.5), channel_id=1, source_target_pairs={{0,16},{1,113},{16,32},{17,1},{32,48},{33,17},{48,64},{49,33},{64,... | collective-permute-start | bytes 1548296 | tf_op jit(solution)/shard_map/ppermute | solution.py:30
  44.7 18.3 %copy-start.5 = (bf16[3584,288]{0,1:T(8,128)(2,1)S(1)}, bf16[3584,288]{0,1:T(8,128)(2,1)}, u32[]{:S(2)}) copy-start(bf16[3584,288]{0,1:T(8,128)(2,1)} %param.7) | copy-start | bytes 6193156
  44.7 23.3 %collective-permute-start.14 = (bf16[288,1792]{1,0:T(8,128)(2,1)S(1)}, bf16[288,1792]{1,0:T(8,128)(2,1)S(1)}, u32[]{:S(2)}, u32[]{:S(2)}) collective-permute-start(bf16[288,1792]{1,0:T(8,128)(2,1)S(1)} %constant_dynamic-update-slice_fusion.2.refs_2_), channel_id=1, source_target_pairs={{0,2},{1,15},{2,4},{3,1},{4,6},{5,3},{6,8},{7,5},{8,10},{9,7},{10,... | collective-permute-start | bytes 3096584 | tf_op jit(solution)/shard_map/ppermute | solution.py:30
  49.8 11.2 %collective-permute-start.6 = (bf16[1,68,3584]{2,1,0:T(8,128)(2,1)S(1)}, bf16[1,68,3584]{2,1,0:T(8,128)(2,1)S(1)}, u32[]{:S(2)}, u32[]{:S(2)}) collective-permute-start(bf16[1,68,3584]{2,1,0:T(8,128)(2,1)S(1)} %slice.4), channel_id=1, source_target_pairs={{0,128},{1,385},{128,256},{129,1},{256,384},{257,129},{384,0},{385... | collective-permute-start | bytes 1462280 | tf_op jit(solution)/shard_map/ppermute | solution.py:30
  54.0 9.1 %collective-permute-start.7 = (bf16[2,68,3584]{2,0,1:T(2,128)(2,1)S(1)}, bf16[2,68,3584]{2,0,1:T(2,128)(2,1)S(1)}, u32[]{:S(2)}, u32[]{:S(2)}) collective-permute-start(bf16[2,68,3584]{2,0,1:T(2,128)(2,1)S(1)} %collective-permute-done.1), channel_id=1, source_target_pairs={{0,1},{1,0},{2,3},{3,2},{4,5},{5,4},{6,7},{7,6},{8,9},{9,8},{10,11... | collective-permute-start | bytes 2924552 | tf_op jit(solution)/shard_map/ppermute | solution.py:30
  55.9 10.1 %collective-permute-start.12 = (bf16[144,1792]{1,0:T(8,128)(2,1)S(1)}, bf16[144,1792]{1,0:T(8,128)(2,1)S(1)}, u32[]{:S(2)}, u32[]{:S(2)}) collective-permute-start(bf16[144,1792]{1,0:T(8,128)(2,1)S(1)} %collective-permute-done.8.refs_0_), channel_id=1, source_target_pairs={{0,16},{1,113},{16,32},{17,1},{32,48},{33,17},{48,64},{49,33},{64,... | collective-permute-start | bytes 1548296 | tf_op jit(solution)/shard_map/ppermute | solution.py:30
  57.8 10.1 %collective-permute-start.13 = (bf16[144,1792]{1,0:T(8,128)(2,1)S(1)}, bf16[144,1792]{1,0:T(8,128)(2,1)S(1)}, u32[]{:S(2)}, u32[]{:S(2)}) collective-permute-start(bf16[144,1792]{1,0:T(8,128)(2,1)S(1)} %collective-permute-done.8.refs_0_), channel_id=1, source_target_pairs={{0,2},{1,15},{2,4},{3,1},{4,6},{5,3},{6,8},{7,5},{8,10},{9,7},{10,... | collective-permute-start | bytes 1548296 | tf_op jit(solution)/shard_map/ppermute | solution.py:30
  61.1 3.8 %collective-permute-start.10 = (bf16[1,68,3584]{2,1,0:T(8,128)(2,1)S(1)}, bf16[1,68,3584]{2,1,0:T(8,128)(2,1)S(1)}, u32[]{:S(2)}, u32[]{:S(2)}) collective-permute-start(bf16[1,68,3584]{2,1,0:T(8,128)(2,1)S(1)} %collective-permute-done.6.far_ref), channel_id=1, source_target_pairs={{0,1},{1,0},{2,3},{3,2},{4,5},{5,4},{6,7},{7,6},{8,9},{9,8},{10,11... | collective-permute-start | bytes 1462280 | tf_op jit(solution)/shard_map/ppermute | solution.py:30
  73.4 2.1 %copy-start = (bf16[640,3584]{1,0:T(8,128)(2,1)}, bf16[640,3584]{1,0:T(8,128)(2,1)S(1)}, u32[]{:S(2)}) copy-start(bf16[640,3584]{1,0:T(8,128)(2,1)S(1)} %line_up.1.a_ref) | copy-start | bytes 13762564
  75.5 27.4 %all-to-all-start = ((bf16[8,68,720]{2,1,0:T(8,128)(2,1)}), bf16[8,68,720]{2,1,0:T(8,128)(2,1)S(1)}, u32[]{:S(2)}, u32[]{:S(2)}) async-start(bf16[8,68,720]{2,1,0:T(8,128)(2,1)} %project.2), calls=%async_computation | async-start | bytes 1769472 | tf_op jit(solution)/shard_map/all_to_all | solution.py:223
  81.5 10.1 %collective-permute-start.15 = (bf16[144,1792]{1,0:T(8,128)(2,1)S(1)}, bf16[144,1792]{1,0:T(8,128)(2,1)S(1)}, u32[]{:S(2)}, u32[]{:S(2)}) collective-permute-start(bf16[144,1792]{1,0:T(8,128)(2,1)S(1)} %collective-permute-done.9.refs_1_), channel_id=1, source_target_pairs={{0,2},{1,15},{2,4},{3,1},{4,6},{5,3},{6,8},{7,5},{8,10},{9,7},{10,... | collective-permute-start | bytes 1548296 | tf_op jit(solution)/shard_map/ppermute | solution.py:30
  83.7 13.4 %collective-permute-start.16 = (bf16[144,1792]{1,0:T(8,128)(2,1)S(1)}, bf16[144,1792]{1,0:T(8,128)(2,1)S(1)}, u32[]{:S(2)}, u32[]{:S(2)}) collective-permute-start(bf16[144,1792]{1,0:T(8,128)(2,1)S(1)} %collective-permute-done.12.refs_2_), channel_id=1, source_target_pairs={{0,2},{1,15},{2,4},{3,1},{4,6},{5,3},{6,8},{7,5},{8,10},{9,7},{10,... | collective-permute-start | bytes 1548296 | tf_op jit(solution)/shard_map/ppermute | solution.py:30
  97.1 2.3 %copy-start.1 = (bf16[640,3584]{1,0:T(8,128)(2,1)S(1)}, bf16[640,3584]{1,0:T(8,128)(2,1)}, u32[]{:S(2)}) copy-start(bf16[640,3584]{1,0:T(8,128)(2,1)} %copy-done) | copy-start | bytes 13762564

commit v3 on v2

--- a/solution.py
+++ b/solution.py
@@ -73,10 +73,10 @@
     )(place, layer_rows, norm_gain.reshape(1, -1), req_len.reshape(1, -1), req_rank.reshape(1, -1))
 
 
-def line_up(place, pair, beside, far, swapped, across):
+def line_up(place, pair, beside, distant, swapped, across):
     rows, features = pair.shape[1:]
 
-    def body(place_ref, pair_ref, beside_ref, far_ref, swapped_ref, across_ref, out):
+    def body(place_ref, pair_ref, beside_ref, distant_ref, swapped_ref, across_ref, out):
         x, c = place_ref[0], place_ref[1]
         back = 2 * c - 1
 
@@ -88,7 +88,7 @@
         put(0, 1 - c, pair_ref[1])
         put(back, c, beside_ref[0])
         put(back, 1 - c, beside_ref[1])
-        put(2, c, far_ref[0])
+        put(2, c, distant_ref[0])
         put(-back, 1 - c, swapped_ref[0])
         put(-back, c, swapped_ref[1])
         put(2, 1 - c, across_ref[0])
@@ -101,26 +101,27 @@
         compiler_params=pltpu.CompilerParams(vmem_limit_bytes=12 * MIB),
         cost_estimate=TINY,
         name="line_up",
-    )(place, pair, beside, far, swapped, across)
-
-
-def project(place, rows_in, near, far, rows):
+    )(place, pair, beside, distant, swapped, across)
+
+
+def project(place, rows_in, near, far, rows, columns, into=None):
     total, features = rows_in.shape
     half = features // 2
     owners = total // PAD
-    widths = [w.shape[0] for w in near]
-    columns = sum(widths)
     given = list(near) + [w for w in far if w is not None]
+    made = sum(w.shape[0] for w in near)
+    span = columns if into is None else -(-made // 128) * 128
     per = 4
     block = per * PAD
 
     def body(place_ref, a_ref, *refs):
-        out = refs[-1]
+        out, rest = refs[-1], list(refs[len(near) : len(given)])
         q = place_ref[2]
         first = pl.multiple_of(q * half, 128)
         second = pl.multiple_of((1 - q) * half, 128)
-        a_first, a_second = a_ref[:, pl.ds(first, half)], a_ref[:, pl.ds(second, half)]
-        w_first, w_second, rest = [], [], list(refs[len(near) : len(given)])
+        here = pl.ds(pl.multiple_of(pl.program_id(0) * block, 16), block)
+        a_first, a_second = a_ref[here, pl.ds(first, half)], a_ref[here, pl.ds(second, half)]
+        w_first, w_second = [], []
         for ref, other in zip(refs[: len(near)], far):
             if other is None:
                 w_first.append(ref[:, pl.ds(first, half)])
@@ -132,40 +133,42 @@
         gate = lax.dot_general(a_first, jnp.concatenate(w_first, 0), contract, preferred_element_type=jnp.float32)
         gate += lax.dot_general(a_second, jnp.concatenate(w_second, 0), contract, preferred_element_type=jnp.float32)
         act = (gate / (1.0 + jnp.exp(-gate))).astype(jnp.bfloat16)
+        if into is not None:
+            out[...] = refs[len(given)][...]
         for i in range(per):
-            out[i] = act[i * PAD : i * PAD + rows]
-
+            out[i, :, :made] = act[i * PAD : i * PAD + rows]
+
+    whole = pl.BlockSpec(memory_space=pltpu.VMEM)
+    part = pl.BlockSpec((per, rows, span), lambda i: (i, 0, 0))
+    kept = [] if into is None else [into]
     return pl.pallas_call(
         body,
         grid=(owners // per,),
         out_shape=jax.ShapeDtypeStruct((owners, rows, columns), jnp.bfloat16),
-        in_specs=[pl.BlockSpec(memory_space=pltpu.SMEM), pl.BlockSpec((block, features), lambda i: (i, 0))]
-        + [pl.BlockSpec(w.shape, lambda i: (0, 0)) for w in given],
-        out_specs=pl.BlockSpec((per, rows, columns), lambda i: (i, 0, 0)),
+        in_specs=[pl.BlockSpec(memory_space=pltpu.SMEM)] + [whole] * (1 + len(given)) + [part] * len(kept),
+        out_specs=part,
+        input_output_aliases={2 + len(given): 0} if kept else {},
         compiler_params=pltpu.CompilerParams(vmem_limit_bytes=20 * MIB),
         cost_estimate=TINY,
         name="project",
-    )(place, rows_in, *given)
-
-
-def settle(place, early, late, width):
-    rows = early.shape[1]
+    )(place, rows_in, *given, *kept)
+
+
+def settle(place, received, width):
+    rows = received.shape[1]
     half = width // 2
     region = 8 * width
 
-    def body(place_ref, early_ref, late_ref, out):
+    def body(place_ref, ref, out):
         z = place_ref[3]
 
-        def take(ref, core, k, n=1):
+        def take(core, k, n=1):
             return ref[core, :, k * half : (k + n) * half]
 
-        def flipped(ref, k):
-            return [take(ref, 1, k + 1), take(ref, 1, k)]
-
-        parts = [take(late_ref, 0, 0, 2), take(early_ref, 0, 3, 2), take(early_ref, 0, 1, 2)]
-        parts += [take(early_ref, 0, 0), take(early_ref, 1, 0)]
-        parts += flipped(early_ref, 1) + flipped(early_ref, 3) + flipped(late_ref, 0)
-        parts += [take(late_ref, 0, 2), take(late_ref, 1, 2)]
+        parts = [take(0, 6, 2), take(0, 4, 2), take(0, 2, 2), take(0, 1), take(1, 1)]
+        for k in (2, 4, 6):
+            parts += [take(1, k + 1), take(1, k)]
+        parts += [take(0, 0), take(1, 0)]
         line = jnp.concatenate([p.astype(jnp.float32) for p in parts], axis=1)
         line = pltpu.roll(line, lax.rem(z + 5, 8) * width, 1)
         out[...] = line.astype(jnp.bfloat16)
@@ -174,13 +177,15 @@
         body,
         grid=(4,),
         out_shape=jax.ShapeDtypeStruct((rows, 4 * region), jnp.bfloat16),
-        in_specs=[pl.BlockSpec(memory_space=pltpu.SMEM)]
-        + [pl.BlockSpec((2, rows, g.shape[2]), lambda i: (i, 0, 0)) for g in (early, late)],
+        in_specs=[
+            pl.BlockSpec(memory_space=pltpu.SMEM),
+            pl.BlockSpec((2, rows, received.shape[2]), lambda i: (i, 0, 0)),
+        ],
         out_specs=pl.BlockSpec((rows, region), lambda i: (0, i)),
         compiler_params=pltpu.CompilerParams(vmem_limit_bytes=20 * MIB),
         cost_estimate=TINY,
         name="settle",
-    )(place, early, late)
+    )(place, received)
 
 
 def shards(layer_rows, norm_gain, w_gate, req_len, req_rank):
@@ -203,31 +208,28 @@
     normed = normalize(place, layer_rows, after(norm_gain, a[0]), req_len, req_rank)
     pair = jnp.stack([normed, other_core(normed)])
     beside = along_x(pair)
-    a.append(along_z(a[1]))
+    a.append(along_z(after(a[1], pair)))
     b.append(along_z(b[1]))
     near = [jnp.concatenate([a[1], b[1]], 0)]
     far = [along_y(near[0])]
-    swapped = other_core(beside)
-    distant = along_x(after(beside[:1], a[2], b[2]))
+    distant = along_x(after(beside[:1], a[2]))
     a.append(along_z(a[2]))
-    b.append(along_z(b[2]))
+    b.append(along_z(after(b[2], beside)))
     near.append(jnp.concatenate([a[2], b[2]], 0))
     far.append(along_y(near[1]))
-    across = other_core(after(distant, a[3], b[3]))
     a.append(along_z(after(a[3], far[0])))
-    far_a, far_b = along_y(a[3]), along_y(b[3])
+    near += [a[3], b[3]]
+    far += [along_y(a[3]), along_y(after(b[3], distant))]
+    far_4 = along_y(after(a[4], far[1], far[2]))
+    swapped, across = other_core(after(beside, a[3])), other_core(distant)
     rows_in = line_up(place, pair, beside, distant, swapped, across)
+
+    columns = 4 * width
     own_half = lax.dynamic_slice(weights, (c * half_width, 0), (half_width, features))
-
-    def deliver(value):
-        return lax.all_to_all(value, ("x", "core"), 0, 0, tiled=True)
-
-    far_4 = along_y(a[4])
-    first = project(place, after(rows_in, a[4], far_a), [own_half] + near, [None] + far, rows)
-    early = deliver(first)
-    second = project(place, after(rows_in, first), [a[3], b[3], a[4]], [far_a, far_b, far_4], rows)
-    late = deliver(after(second, early))
-    return settle(place, early, late, width)
+    gate = project(place, after(rows_in, a[4]), [own_half, own_half] + near, [None, None] + far, rows, columns)
+    gate = project(place, rows_in, a[4:], [far_4], rows, columns, gate)
+    received = lax.all_to_all(gate, ("x", "core"), 0, 0, tiled=True)
+    return settle(place, received, width)
 
 
 def solution(mesh):

time: 124 us -> 112 us (0.903)
  waiting for transfers between devices: 15.1 us -> 4.87 us
  blocking collectives: 17 us -> 22.6 us
  local copies, waits for them, and re-layouts: 7.05 us -> 2.67 us
  starting transfers between devices: 69.8 us -> 66.6 us
    ppermute x17, waiting for transfers between devices: 15.1 us -> 4.87 us  [hop(): return lax.ppermute(value, tuple(axes), pairs)]
    all_to_all x1 -> x0, starting transfers between devices: 6.02 us -> none  [deliver(): return lax.all_to_all(value, ('x', 'core'), 0, 0, tiled=True)]
    all_to_all x1, blocking collectives: 17 us -> 22.6 us  [shards(): received = lax.all_to_all(gate, ('x', 'core'), 0, 0, tiled=True)]
    unnamed x16 -> x12, local copies, waits for them, and re-layouts: 4.47 us -> 0.09 us
    ppermute x17, starting transfers between devices: 63.8 us -> 66.6 us  [hop(): return lax.ppermute(value, tuple(axes), pairs)]
  transfers between devices with their start and end apart: 18 -> 17, of which waited for: 6 -> 4; matrix products, arithmetic and copies ran while one was open for 1% -> 1% of each run, Pallas kernels for 3% -> 7%
where the time goes in v3:
time: 112 us; the launch traced here: 111 us
  starting transfers between devices  66.6 us (59%)
  blocking collectives  22.6 us (20%)
  Pallas kernels  14.1 us (13%)
  waiting for transfers between devices  4.87 us (4%)
  local copies, waits for them, and re-layouts  2.67 us (2%)
    ppermute x17, starting transfers between devices, hop(): return lax.ppermute(value, tuple(axes), pairs)  66.6 us
    all_to_all x1, blocking collectives, shards(): received = lax.all_to_all(gate, ('x', 'core'), 0, 0, tiled=True)  22.6 us
    pallas_call x2, Pallas kernels, project(): pl.pallas_call(body, grid=(owners // per,), out_shape=jax.ShapeDtypeStruc...  9.2 us
    ppermute x17, waiting for transfers between devices, hop(): return lax.ppermute(value, tuple(axes), pairs)  4.87 us
    pallas_call x1, Pallas kernels, settle(): pl.pallas_call(body, grid=(4,), out_shape=jax.ShapeDtypeStruct((rows, 4 *...  3.27 us
  transfers between devices with their start and end apart: 17, of which 4 were waited for; matrix products, arithmetic and copies ran while one was open for 1% of the time, Pallas kernels for 7%

profile of v3, /device:TPU:1, one launch (start us, length us, event | category | flops | bytes accessed | tf_op | source)
XLA Modules:
  0.0 111.4 jit_solution(13505937589145307028)
XLA Ops:
  0.0 1.3 %dynamic-slice_bitcast_fusion.1 = (bf16[144,1792]{1,0:T(8,128)(2,1)S(1)}, bf16[144,1792]{1,0:T(8,128)(2,1)S(1)}) fusion(bf16[3584,288]{0,1:T(8,128)(2,1)} %param.7, s32[]{:T(128)S(6)} %select_n.11, s32[]{:T(128)S(6)} %select_n.13, s32[]{:T(128)S(6)} %select_n.12), kind=kLoop, calls=%fused_computation.2 | loop fusion | bytes 2064396 | tf_op jit(solution)/shard_map/dynamic_slice | solution.py:202
  1.4 0.1 stack.32.place_ref
  1.5 0.8 normalize.1
  2.3 8.8 %collective-permute-start = (bf16[68,3584]{1,0:T(8,128)(2,1)S(1)}, bf16[68,3584]{1,0:T(8,128)(2,1)S(1)}, u32[]{:S(2)}, u32[]{:S(2)}) collective-permute-start(bf16[68,3584]{1,0:T(8,128)(2,1)S(1)} %normalize.1), channel_id=1, source_target_pairs={{0,1},{1,0},{2,3},{3,2},{4,5},{5,4},{6,7},{7,6},{8,9},{9,8},{10,11... | collective-permute-start | bytes 1462280 | tf_op jit(solution)/shard_map/ppermute | solution.py:30
  11.1 5.3 %collective-permute-start.2 = (bf16[144,1792]{1,0:T(8,128)(2,1)S(1)}, bf16[144,1792]{1,0:T(8,128)(2,1)S(1)}, u32[]{:S(2)}, u32[]{:S(2)}) collective-permute-start(bf16[144,1792]{1,0:T(8,128)(2,1)S(1)} %get-tuple-element.24), channel_id=1, source_target_pairs={{0,16},{1,113},{16,32},{17,1},{32,48},{33,17},{48,64},{49,33},{64,... | collective-permute-start | bytes 1548296 | tf_op jit(solution)/shard_map/ppermute | solution.py:30
  16.4 2.2 %collective-permute-start.8 = (bf16[144,1792]{1,0:T(8,128)(2,1)S(1)}, bf16[144,1792]{1,0:T(8,128)(2,1)S(1)}, u32[]{:S(2)}, u32[]{:S(2)}) collective-permute-start(bf16[144,1792]{1,0:T(8,128)(2,1)S(1)} %get-tuple-element.23), channel_id=1, source_target_pairs={{0,16},{1,113},{16,32},{17,1},{32,48},{33,17},{48,64},{49,33},{64,... | collective-permute-start | bytes 1548296 | tf_op jit(solution)/shard_map/ppermute | solution.py:30
  18.6 0.0 collective-permute-done
  18.6 0.1 pad_maximum_fusion.pair_ref
  18.7 0.8 copy.7
  19.5 4.4 %collective-permute-start.1 = (bf16[2,68,3584]{2,0,1:T(2,128)(2,1)S(1)}, bf16[2,68,3584]{2,0,1:T(2,128)(2,1)S(1)}, u32[]{:S(2)}, u32[]{:S(2)}) collective-permute-start(bf16[2,68,3584]{2,0,1:T(2,128)(2,1)S(1)} %copy.7), channel_id=1, source_target_pairs={{0,128},{1,385},{128,256},{129,1},{256,384},{257,129},{384,0},{385... | collective-permute-start | bytes 2924552 | tf_op jit(solution)/shard_map/ppermute | solution.py:30
  23.9 0.0 collective-permute-done.2
  23.9 3.9 %collective-permute-start.3 = (bf16[144,1792]{1,0:T(8,128)(2,1)S(1)}, bf16[144,1792]{1,0:T(8,128)(2,1)S(1)}, u32[]{:S(2)}, u32[]{:S(2)}) collective-permute-start(bf16[144,1792]{1,0:T(8,128)(2,1)S(1)} %collective-permute-done.2), channel_id=1, source_target_pairs={{0,16},{1,113},{16,32},{17,1},{32,48},{33,17},{48,64},{49,33},{64,... | collective-permute-start | bytes 1548296 | tf_op jit(solution)/shard_map/ppermute | solution.py:30
  27.8 0.2 collective-permute-done.8
  28.0 5.3 %collective-permute-start.11 = (bf16[144,1792]{1,0:T(8,128)(2,1)S(1)}, bf16[144,1792]{1,0:T(8,128)(2,1)S(1)}, u32[]{:S(2)}, u32[]{:S(2)}) collective-permute-start(bf16[144,1792]{1,0:T(8,128)(2,1)S(1)} %collective-permute-done.8), channel_id=1, source_target_pairs={{0,16},{1,113},{16,32},{17,1},{32,48},{33,17},{48,64},{49,33},{64,... | collective-permute-start | bytes 1548296 | tf_op jit(solution)/shard_map/ppermute | solution.py:30
  33.4 5.1 %collective-permute-start.9 = (bf16[288,1792]{1,0:T(8,128)(2,1)S(1)}, bf16[288,1792]{1,0:T(8,128)(2,1)S(1)}, u32[]{:S(2)}, u32[]{:S(2)}) collective-permute-start(bf16[288,1792]{1,0:T(8,128)(2,1)S(1)} %constant_dynamic-update-slice_fusion.refs_2_), channel_id=1, source_target_pairs={{0,2},{1,15},{2,4},{3,1},{4,6},{5,3},{6,8},{7,5},{8,10},{9,7},{10,... | collective-permute-start | bytes 3096584 | tf_op jit(solution)/shard_map/ppermute | solution.py:30
  38.5 0.0 collective-permute-done.3
  38.5 1.9 %collective-permute-start.5 = (bf16[144,1792]{1,0:T(8,128)(2,1)S(1)}, bf16[144,1792]{1,0:T(8,128)(2,1)S(1)}, u32[]{:S(2)}, u32[]{:S(2)}) collective-permute-start(bf16[144,1792]{1,0:T(8,128)(2,1)S(1)} %collective-permute-done.3), channel_id=1, source_target_pairs={{0,16},{1,113},{16,32},{17,1},{32,48},{33,17},{48,64},{49,33},{64,... | collective-permute-start | bytes 1548296 | tf_op jit(solution)/shard_map/ppermute | solution.py:30
  40.5 0.0 copy-start.3
  40.5 0.0 collective-permute-done.11
  40.5 4.2 %collective-permute-start.12 = (bf16[288,1792]{1,0:T(8,128)(2,1)S(1)}, bf16[288,1792]{1,0:T(8,128)(2,1)S(1)}, u32[]{:S(2)}, u32[]{:S(2)}) collective-permute-start(bf16[288,1792]{1,0:T(8,128)(2,1)S(1)} %constant_dynamic-update-slice_fusion.2.refs_3_), channel_id=1, source_target_pairs={{0,2},{1,15},{2,4},{3,1},{4,6},{5,3},{6,8},{7,5},{8,10},{9,7},{10,... | collective-permute-start | bytes 3096584 | tf_op jit(solution)/shard_map/ppermute | solution.py:30
  44.7 0.0 collective-permute-done.1
  44.7 0.1 copy.9.beside_ref
  44.9 4.0 %collective-permute-start.4 = (bf16[1,68,3584]{2,1,0:T(8,128)(2,1)S(1)}, bf16[1,68,3584]{2,1,0:T(8,128)(2,1)S(1)}, u32[]{:S(2)}, u32[]{:S(2)}) collective-permute-start(bf16[1,68,3584]{2,1,0:T(8,128)(2,1)S(1)} %slice.4), channel_id=1, source_target_pairs={{0,128},{1,385},{128,256},{129,1},{256,384},{257,129},{384,0},{385... | collective-permute-start | bytes 1462280 | tf_op jit(solution)/shard_map/ppermute | solution.py:30
  48.9 4.9 %collective-permute-start.15 = (bf16[144,1792]{1,0:T(8,128)(2,1)S(1)}, bf16[144,1792]{1,0:T(8,128)(2,1)S(1)}, u32[]{:S(2)}, u32[]{:S(2)}) collective-permute-start(bf16[144,1792]{1,0:T(8,128)(2,1)S(1)} %collective-permute-done.11), channel_id=1, source_target_pairs={{0,16},{1,113},{16,32},{17,1},{32,48},{33,17},{48,64},{49,33},{64,... | collective-permute-start | bytes 1548296 | tf_op jit(solution)/shard_map/ppermute | solution.py:30
  53.8 0.0 collective-permute-done.5.refs_4_
  53.8 0.0 collective-permute-done.9.refs_6_
  53.8 1.9 %collective-permute-start.10 = (bf16[144,1792]{1,0:T(8,128)(2,1)S(1)}, bf16[144,1792]{1,0:T(8,128)(2,1)S(1)}, u32[]{:S(2)}, u32[]{:S(2)}) collective-permute-start(bf16[144,1792]{1,0:T(8,128)(2,1)S(1)} %collective-permute-done.5.refs_4_), channel_id=1, source_target_pairs={{0,16},{1,113},{16,32},{17,1},{32,48},{33,17},{48,64},{49,33},{64,... | collective-permute-start | bytes 1548296 | tf_op jit(solution)/shard_map/ppermute | solution.py:30
  55.7 3.0 %collective-permute-start.13 = (bf16[144,1792]{1,0:T(8,128)(2,1)S(1)}, bf16[144,1792]{1,0:T(8,128)(2,1)S(1)}, u32[]{:S(2)}, u32[]{:S(2)}) collective-permute-start(bf16[144,1792]{1,0:T(8,128)(2,1)S(1)} %collective-permute-done.5.refs_4_), channel_id=1, source_target_pairs={{0,2},{1,15},{2,4},{3,1},{4,6},{5,3},{6,8},{7,5},{8,10},{9,7},{10,... | collective-permute-start | bytes 1548296 | tf_op jit(solution)/shard_map/ppermute | solution.py:30
  58.7 0.0 collective-permute-done.4.distant_ref
  58.7 1.9 %collective-permute-start.6 = (bf16[2,68,3584]{2,0,1:T(2,128)(2,1)S(1)}, bf16[2,68,3584]{2,0,1:T(2,128)(2,1)S(1)}, u32[]{:S(2)}, u32[]{:S(2)}) collective-permute-start(bf16[2,68,3584]{2,0,1:T(2,128)(2,1)S(1)} %collective-permute-done.1), channel_id=1, source_target_pairs={{0,1},{1,0},{2,3},{3,2},{4,5},{5,4},{6,7},{7,6},{8,9},{9,8},{10,11... | collective-permute-start | bytes 2924552 | tf_op jit(solution)/shard_map/ppermute | solution.py:30
  60.6 0.0 collective-permute-done.15.refs_5_
  60.7 3.0 %collective-permute-start.16 = (bf16[144,1792]{1,0:T(8,128)(2,1)S(1)}, bf16[144,1792]{1,0:T(8,128)(2,1)S(1)}, u32[]{:S(2)}, u32[]{:S(2)}) collective-permute-start(bf16[144,1792]{1,0:T(8,128)(2,1)S(1)} %collective-permute-done.15.refs_5_), channel_id=1, source_target_pairs={{0,2},{1,15},{2,4},{3,1},{4,6},{5,3},{6,8},{7,5},{8,10},{9,7},{10,... | collective-permute-start | bytes 1548296 | tf_op jit(solution)/shard_map/ppermute | solution.py:30
  63.6 1.7 %collective-permute-done.10.refs_0_ = bf16[144,1792]{1,0:T(8,128)(2,1)S(1)} collective-permute-done((bf16[144,1792]{1,0:T(8,128)(2,1)S(1)}, bf16[144,1792]{1,0:T(8,128)(2,1)S(1)}, u32[]{:S(2)}, u32[]{:S(2)}) %collective-permute-start.10) | collective-permute-done | bytes 516128 | tf_op jit(solution)/shard_map/ppermute | solution.py:30
  65.3 0.0 collective-permute-done.12.refs_7_
  65.3 1.3 %collective-permute-done.13.refs_8_ = bf16[144,1792]{1,0:T(8,128)(2,1)S(1)} collective-permute-done((bf16[144,1792]{1,0:T(8,128)(2,1)S(1)}, bf16[144,1792]{1,0:T(8,128)(2,1)S(1)}, u32[]{:S(2)}, u32[]{:S(2)}) %collective-permute-start.13) | collective-permute-done | bytes 516128 | tf_op jit(solution)/shard_map/ppermute | solution.py:30
  66.6 5.0 %collective-permute-start.14 = (bf16[144,1792]{1,0:T(8,128)(2,1)S(1)}, bf16[144,1792]{1,0:T(8,128)(2,1)S(1)}, u32[]{:S(2)}, u32[]{:S(2)}) collective-permute-start(bf16[144,1792]{1,0:T(8,128)(2,1)S(1)} %collective-permute-done.10.refs_0_), channel_id=1, source_target_pairs={{0,2},{1,15},{2,4},{3,1},{4,6},{5,3},{6,8},{7,5},{8,10},{9,7},{10,... | collective-permute-start | bytes 1548296 | tf_op jit(solution)/shard_map/ppermute | solution.py:30
  71.6 1.9 %collective-permute-start.7 = (bf16[1,68,3584]{2,1,0:T(8,128)(2,1)S(1)}, bf16[1,68,3584]{2,1,0:T(8,128)(2,1)S(1)}, u32[]{:S(2)}, u32[]{:S(2)}) collective-permute-start(bf16[1,68,3584]{2,1,0:T(8,128)(2,1)S(1)} %collective-permute-done.4.distant_ref), channel_id=1, source_target_pairs={{0,1},{1,0},{2,3},{3,2},{4,5},{5,4},{6,7},{7,6},{8,9},{9,8},{10,11... | collective-permute-start | bytes 1462280 | tf_op jit(solution)/shard_map/ppermute | solution.py:30
  73.6 0.1 dynamic-slice_bitcast_fusion.refs_0_.refs_1_
  73.7 0.0 collective-permute-done.6
  73.7 0.1 copy.10.swapped_ref
  73.8 1.6 %collective-permute-done.7.across_ref = bf16[1,68,3584]{2,1,0:T(8,128)(2,1)S(1)} collective-permute-done((bf16[1,68,3584]{2,1,0:T(8,128)(2,1)S(1)}, bf16[1,68,3584]{2,1,0:T(8,128)(2,1)S(1)}, u32[]{:S(2)}, u32[]{:S(2)}) %collective-permute-start.7) | collective-permute-done | bytes 487456 | tf_op jit(solution)/shard_map/ppermute | solution.py:30
  75.4 0.8 line_up.1.a_ref
  76.3 0.0 collective-permute-done.16.refs_9_
  76.3 7.0 %project.2.refs_2_ = bf16[8,68,1152]{2,1,0:T(8,128)(2,1)S(1)} custom-call(s32[5]{0:T(128)S(1)} %stack.32.place_ref, bf16[640,3584]{1,0:T(8,128)(2,1)S(1)} %line_up.1.a_ref, bf16[144,3584]{1,0:T(8,128)(2,1)S(1)} %dynamic-slice_bitcast_fusion.refs_0_.refs_1_, bf16[144,3584]{1,0:T(8,128)(2,1)S(1)} %dynamic-slice_bitcast_fusion.refs_0_.refs_1_, ...), custom_call_target="tpu_custom_call" | custom-call | bytes 1024 | tf_op jit(solution)/shard_map/project/pallas_call | solution.py:144
  83.3 0.0 collective-permute-done.14.refs_1_
  83.3 2.2 %project.3 = bf16[8,68,1152]{2,1,0:T(8,128)(2,1)S(1)} custom-call(s32[5]{0:T(128)S(1)} %stack.32.place_ref, bf16[640,3584]{1,0:T(8,128)(2,1)S(1)} %line_up.1.a_ref, bf16[144,1792]{1,0:T(8,128)(2,1)S(1)} %collective-permute-done.10.refs_0_, bf16[144,1792]{1,0:T(8,128)(2,1)S(1)} %collective-permute-done.14.refs_1_, ...), custom_call_target="tpu_custom_call", output_to_operand_aliasing={{}: (4, {})} | custom-call | bytes 1024 | tf_op jit(solution)/shard_map/project/pallas_call | solution.py:144
  85.5 22.6 %all_to_all.5.ref = bf16[8,68,1152]{2,1,0:T(8,128)(2,1)S(1)} all-to-all(bf16[8,68,1152]{2,1,0:T(8,128)(2,1)S(1)} %project.3), channel_id=1, replica_groups=mesh['x'=4,'z'=8,'y'=8,'core'=2] {'x','core'}, dimensions={0} | all-to-all | bytes 2506752 | tf_op jit(solution)/shard_map/all_to_all | solution.py:231
  108.1 3.3 %settle.1 = bf16[68,9216]{1,0:T(8,128)(2,1)} custom-call(s32[5]{0:T(128)S(1)} %stack.32.place_ref, bf16[8,68,1152]{2,1,0:T(8,128)(2,1)S(1)} %all_to_all.5.ref), custom_call_target="tpu_custom_call" | custom-call | bytes 1024 | tf_op jit(solution)/shard_map/settle/pallas_call | solution.py:176
  (15 shorter events, 0.2 us)
Async XLA Ops:
  0.0 1.4 %copy-start.4 = (f32[3584]{0:T(1024)S(1)}, f32[3584]{0:T(1024)}, u32[]{:S(2)}) copy-start(f32[3584]{0:T(1024)} %param.6) | copy-start | bytes 43012
  0.0 1.5 %copy-start.1 = (s32[64]{0:T(128)S(1)}, s32[64]{0:T(128)}, u32[]{:S(2)}) copy-start(s32[64]{0:T(128)} %param.8) | copy-start | bytes 772
  0.0 1.5 %copy-start.2 = (s32[64]{0:T(128)S(1)}, s32[64]{0:T(128)}, u32[]{:S(2)}) copy-start(s32[64]{0:T(128)} %param.9) | copy-start | bytes 772
  0.0 1.5 %copy-start = (bf16[68,3584]{1,0:T(8,128)(2,1)S(1)}, bf16[68,3584]{1,0:T(8,128)(2,1)}, u32[]{:S(2)}) copy-start(bf16[68,3584]{1,0:T(8,128)(2,1)} %rows_ref.1) | copy-start | bytes 1462276
  2.3 16.3 %collective-permute-start = (bf16[68,3584]{1,0:T(8,128)(2,1)S(1)}, bf16[68,3584]{1,0:T(8,128)(2,1)S(1)}, u32[]{:S(2)}, u32[]{:S(2)}) collective-permute-start(bf16[68,3584]{1,0:T(8,128)(2,1)S(1)} %normalize.1), channel_id=1, source_target_pairs={{0,1},{1,0},{2,3},{3,2},{4,5},{5,4},{6,7},{7,6},{8,9},{9,8},{10,11... | collective-permute-start | bytes 1462280 | tf_op jit(solution)/shard_map/ppermute | solution.py:30
  11.1 12.8 %collective-permute-start.2 = (bf16[144,1792]{1,0:T(8,128)(2,1)S(1)}, bf16[144,1792]{1,0:T(8,128)(2,1)S(1)}, u32[]{:S(2)}, u32[]{:S(2)}) collective-permute-start(bf16[144,1792]{1,0:T(8,128)(2,1)S(1)} %get-tuple-element.24), channel_id=1, source_target_pairs={{0,16},{1,113},{16,32},{17,1},{32,48},{33,17},{48,64},{49,33},{64,... | collective-permute-start | bytes 1548296 | tf_op jit(solution)/shard_map/ppermute | solution.py:30
  16.4 11.5 %collective-permute-start.8 = (bf16[144,1792]{1,0:T(8,128)(2,1)S(1)}, bf16[144,1792]{1,0:T(8,128)(2,1)S(1)}, u32[]{:S(2)}, u32[]{:S(2)}) collective-permute-start(bf16[144,1792]{1,0:T(8,128)(2,1)S(1)} %get-tuple-element.23), channel_id=1, source_target_pairs={{0,16},{1,113},{16,32},{17,1},{32,48},{33,17},{48,64},{49,33},{64,... | collective-permute-start | bytes 1548296 | tf_op jit(solution)/shard_map/ppermute | solution.py:30
  19.5 25.2 %collective-permute-start.1 = (bf16[2,68,3584]{2,0,1:T(2,128)(2,1)S(1)}, bf16[2,68,3584]{2,0,1:T(2,128)(2,1)S(1)}, u32[]{:S(2)}, u32[]{:S(2)}) collective-permute-start(bf16[2,68,3584]{2,0,1:T(2,128)(2,1)S(1)} %copy.7), channel_id=1, source_target_pairs={{0,128},{1,385},{128,256},{129,1},{256,384},{257,129},{384,0},{385... | collective-permute-start | bytes 2924552 | tf_op jit(solution)/shard_map/ppermute | solution.py:30
  23.9 14.6 %collective-permute-start.3 = (bf16[144,1792]{1,0:T(8,128)(2,1)S(1)}, bf16[144,1792]{1,0:T(8,128)(2,1)S(1)}, u32[]{:S(2)}, u32[]{:S(2)}) collective-permute-start(bf16[144,1792]{1,0:T(8,128)(2,1)S(1)} %collective-permute-done.2), channel_id=1, source_target_pairs={{0,16},{1,113},{16,32},{17,1},{32,48},{33,17},{48,64},{49,33},{64,... | collective-permute-start | bytes 1548296 | tf_op jit(solution)/shard_map/ppermute | solution.py:30
  28.0 12.5 %collective-permute-start.11 = (bf16[144,1792]{1,0:T(8,128)(2,1)S(1)}, bf16[144,1792]{1,0:T(8,128)(2,1)S(1)}, u32[]{:S(2)}, u32[]{:S(2)}) collective-permute-start(bf16[144,1792]{1,0:T(8,128)(2,1)S(1)} %collective-permute-done.8), channel_id=1, source_target_pairs={{0,16},{1,113},{16,32},{17,1},{32,48},{33,17},{48,64},{49,33},{64,... | collective-permute-start | bytes 1548296 | tf_op jit(solution)/shard_map/ppermute | solution.py:30
  33.4 20.4 %collective-permute-start.9 = (bf16[288,1792]{1,0:T(8,128)(2,1)S(1)}, bf16[288,1792]{1,0:T(8,128)(2,1)S(1)}, u32[]{:S(2)}, u32[]{:S(2)}) collective-permute-start(bf16[288,1792]{1,0:T(8,128)(2,1)S(1)} %constant_dynamic-update-slice_fusion.refs_2_), channel_id=1, source_target_pairs={{0,2},{1,15},{2,4},{3,1},{4,6},{5,3},{6,8},{7,5},{8,10},{9,7},{10,... | collective-permute-start | bytes 3096584 | tf_op jit(solution)/shard_map/ppermute | solution.py:30
  38.5 15.3 %collective-permute-start.5 = (bf16[144,1792]{1,0:T(8,128)(2,1)S(1)}, bf16[144,1792]{1,0:T(8,128)(2,1)S(1)}, u32[]{:S(2)}, u32[]{:S(2)}) collective-permute-start(bf16[144,1792]{1,0:T(8,128)(2,1)S(1)} %collective-permute-done.3), channel_id=1, source_target_pairs={{0,16},{1,113},{16,32},{17,1},{32,48},{33,17},{48,64},{49,33},{64,... | collective-permute-start | bytes 1548296 | tf_op jit(solution)/shard_map/ppermute | solution.py:30
  40.5 33.1 %copy-start.3 = (bf16[3584,288]{0,1:T(8,128)(2,1)S(1)}, bf16[3584,288]{0,1:T(8,128)(2,1)}, u32[]{:S(2)}) copy-start(bf16[3584,288]{0,1:T(8,128)(2,1)} %param.7) | copy-start | bytes 6193156
  40.5 24.8 %collective-permute-start.12 = (bf16[288,1792]{1,0:T(8,128)(2,1)S(1)}, bf16[288,1792]{1,0:T(8,128)(2,1)S(1)}, u32[]{:S(2)}, u32[]{:S(2)}) collective-permute-start(bf16[288,1792]{1,0:T(8,128)(2,1)S(1)} %constant_dynamic-update-slice_fusion.2.refs_3_), channel_id=1, source_target_pairs={{0,2},{1,15},{2,4},{3,1},{4,6},{5,3},{6,8},{7,5},{8,10},{9,7},{10,... | collective-permute-start | bytes 3096584 | tf_op jit(solution)/shard_map/ppermute | solution.py:30
  44.9 13.8 %collective-permute-start.4 = (bf16[1,68,3584]{2,1,0:T(8,128)(2,1)S(1)}, bf16[1,68,3584]{2,1,0:T(8,128)(2,1)S(1)}, u32[]{:S(2)}, u32[]{:S(2)}) collective-permute-start(bf16[1,68,3584]{2,1,0:T(8,128)(2,1)S(1)} %slice.4), channel_id=1, source_target_pairs={{0,128},{1,385},{128,256},{129,1},{256,384},{257,129},{384,0},{385... | collective-permute-start | bytes 1462280 | tf_op jit(solution)/shard_map/ppermute | solution.py:30
  48.9 11.8 %collective-permute-start.15 = (bf16[144,1792]{1,0:T(8,128)(2,1)S(1)}, bf16[144,1792]{1,0:T(8,128)(2,1)S(1)}, u32[]{:S(2)}, u32[]{:S(2)}) collective-permute-start(bf16[144,1792]{1,0:T(8,128)(2,1)S(1)} %collective-permute-done.11), channel_id=1, source_target_pairs={{0,16},{1,113},{16,32},{17,1},{32,48},{33,17},{48,64},{49,33},{64,... | collective-permute-start | bytes 1548296 | tf_op jit(solution)/shard_map/ppermute | solution.py:30
  53.8 11.5 %collective-permute-start.10 = (bf16[144,1792]{1,0:T(8,128)(2,1)S(1)}, bf16[144,1792]{1,0:T(8,128)(2,1)S(1)}, u32[]{:S(2)}, u32[]{:S(2)}) collective-permute-start(bf16[144,1792]{1,0:T(8,128)(2,1)S(1)} %collective-permute-done.5.refs_4_), channel_id=1, source_target_pairs={{0,16},{1,113},{16,32},{17,1},{32,48},{33,17},{48,64},{49,33},{64,... | collective-permute-start | bytes 1548296 | tf_op jit(solution)/shard_map/ppermute | solution.py:30
  55.7 10.9 %collective-permute-start.13 = (bf16[144,1792]{1,0:T(8,128)(2,1)S(1)}, bf16[144,1792]{1,0:T(8,128)(2,1)S(1)}, u32[]{:S(2)}, u32[]{:S(2)}) collective-permute-start(bf16[144,1792]{1,0:T(8,128)(2,1)S(1)} %collective-permute-done.5.refs_4_), channel_id=1, source_target_pairs={{0,2},{1,15},{2,4},{3,1},{4,6},{5,3},{6,8},{7,5},{8,10},{9,7},{10,... | collective-permute-start | bytes 1548296 | tf_op jit(solution)/shard_map/ppermute | solution.py:30
  58.7 15.0 %collective-permute-start.6 = (bf16[2,68,3584]{2,0,1:T(2,128)(2,1)S(1)}, bf16[2,68,3584]{2,0,1:T(2,128)(2,1)S(1)}, u32[]{:S(2)}, u32[]{:S(2)}) collective-permute-start(bf16[2,68,3584]{2,0,1:T(2,128)(2,1)S(1)} %collective-permute-done.1), channel_id=1, source_target_pairs={{0,1},{1,0},{2,3},{3,2},{4,5},{5,4},{6,7},{7,6},{8,9},{9,8},{10,11... | collective-permute-start | bytes 2924552 | tf_op jit(solution)/shard_map/ppermute | solution.py:30
  60.7 15.6 %collective-permute-start.16 = (bf16[144,1792]{1,0:T(8,128)(2,1)S(1)}, bf16[144,1792]{1,0:T(8,128)(2,1)S(1)}, u32[]{:S(2)}, u32[]{:S(2)}) collective-permute-start(bf16[144,1792]{1,0:T(8,128)(2,1)S(1)} %collective-permute-done.15.refs_5_), channel_id=1, source_target_pairs={{0,2},{1,15},{2,4},{3,1},{4,6},{5,3},{6,8},{7,5},{8,10},{9,7},{10,... | collective-permute-start | bytes 1548296 | tf_op jit(solution)/shard_map/ppermute | solution.py:30
  66.6 16.7 %collective-permute-start.14 = (bf16[144,1792]{1,0:T(8,128)(2,1)S(1)}, bf16[144,1792]{1,0:T(8,128)(2,1)S(1)}, u32[]{:S(2)}, u32[]{:S(2)}) collective-permute-start(bf16[144,1792]{1,0:T(8,128)(2,1)S(1)} %collective-permute-done.10.refs_0_), channel_id=1, source_target_pairs={{0,2},{1,15},{2,4},{3,1},{4,6},{5,3},{6,8},{7,5},{8,10},{9,7},{10,... | collective-permute-start | bytes 1548296 | tf_op jit(solution)/shard_map/ppermute | solution.py:30
  71.6 3.8 %collective-permute-start.7 = (bf16[1,68,3584]{2,1,0:T(8,128)(2,1)S(1)}, bf16[1,68,3584]{2,1,0:T(8,128)(2,1)S(1)}, u32[]{:S(2)}, u32[]{:S(2)}) collective-permute-start(bf16[1,68,3584]{2,1,0:T(8,128)(2,1)S(1)} %collective-permute-done.4.distant_ref), channel_id=1, source_target_pairs={{0,1},{1,0},{2,3},{3,2},{4,5},{5,4},{6,7},{7,6},{8,9},{9,8},{10,11... | collective-permute-start | bytes 1462280 | tf_op jit(solution)/shard_map/ppermute | solution.py:30

commit v4 on v3

--- a/solution.py
+++ b/solution.py
@@ -50,6 +50,21 @@
     return lax.optimization_barrier((value, *others))[0]
 
 
+def mark(*seen):
+    def body(*refs):
+        refs[-1][...] = jnp.zeros_like(refs[-1])
+
+    return pl.pallas_call(
+        body,
+        out_shape=jax.ShapeDtypeStruct((8, 128), jnp.float32),
+        in_specs=[pl.BlockSpec(memory_space=pl.ANY)] * len(seen),
+        out_specs=pl.BlockSpec(memory_space=pltpu.VMEM),
+        compiler_params=pltpu.CompilerParams(has_side_effects=True),
+        cost_estimate=pl.CostEstimate(flops=10**11, bytes_accessed=1024, transcendentals=0),
+        name="mark",
+    )(*seen)
+
+
 def normalize(place, layer_rows, norm_gain, req_len, req_rank):
     rows, features = layer_rows.shape
 
@@ -88,10 +103,10 @@
         put(0, 1 - c, pair_ref[1])
         put(back, c, beside_ref[0])
         put(back, 1 - c, beside_ref[1])
-        put(2, c, distant_ref[0])
+        put(2, c, distant_ref[...])
         put(-back, 1 - c, swapped_ref[0])
         put(-back, c, swapped_ref[1])
-        put(2, 1 - c, across_ref[0])
+        put(2, 1 - c, across_ref[...])
 
     return pl.pallas_call(
         body,
@@ -204,29 +219,42 @@
     a, b = [own(c)], [own(1 - c)]
     a.append(along_z(a[0]))
     b.append(along_z(b[0]))
-
     normed = normalize(place, layer_rows, after(norm_gain, a[0]), req_len, req_rank)
     pair = jnp.stack([normed, other_core(normed)])
-    beside = along_x(pair)
-    a.append(along_z(after(a[1], pair)))
-    b.append(along_z(b[1]))
-    near = [jnp.concatenate([a[1], b[1]], 0)]
+    point = mark(pair)
+    beside = along_x(after(pair, point))
+    point = mark(point, a[1])
+    a.append(along_z(after(a[1], point)))
+    point = mark(point, b[1])
+    b.append(along_z(after(b[1], point)))
+    near = [jnp.concatenate([a[1], after(b[1], point)], 0)]
     far = [along_y(near[0])]
-    distant = along_x(after(beside[:1], a[2]))
-    a.append(along_z(a[2]))
-    b.append(along_z(after(b[2], beside)))
-    near.append(jnp.concatenate([a[2], b[2]], 0))
+    point = mark(point, a[2])
+    a.append(along_z(after(a[2], point)))
+    point = mark(point, beside)
+    distant = along_x(after(beside[0], point))
+    point = mark(point, b[2])
+    b.append(along_z(after(b[2], point)))
+    near.append(jnp.concatenate([a[2], after(b[2], point)], 0))
     far.append(along_y(near[1]))
-    a.append(along_z(after(a[3], far[0])))
+    point = mark(point, a[3], far[0])
+    a.append(along_z(after(a[3], point)))
+    far.append(along_y(after(a[3], point)))
+    point = mark(point, distant)
+    swapped = other_core(after(beside, point))
+    point = mark(point, b[3])
+    far.append(along_y(after(b[3], point)))
+    point = mark(point, swapped)
+    across = other_core(after(distant, point))
+    point = mark(point, a[4], far[1])
+    far_4 = along_y(after(a[4], point))
+    point = mark(point, across, far[2])
     near += [a[3], b[3]]
-    far += [along_y(a[3]), along_y(after(b[3], distant))]
-    far_4 = along_y(after(a[4], far[1], far[2]))
-    swapped, across = other_core(after(beside, a[3])), other_core(distant)
-    rows_in = line_up(place, pair, beside, distant, swapped, across)
+    rows_in = line_up(place, pair, beside, after(distant, point), swapped, across)
 
     columns = 4 * width
     own_half = lax.dynamic_slice(weights, (c * half_width, 0), (half_width, features))
-    gate = project(place, after(rows_in, a[4]), [own_half, own_half] + near, [None, None] + far, rows, columns)
+    gate = project(place, rows_in, [own_half, own_half] + near, [None, None] + far, rows, columns)
     gate = project(place, rows_in, a[4:], [far_4], rows, columns, gate)
     received = lax.all_to_all(gate, ("x", "core"), 0, 0, tiled=True)
     return settle(place, received, width)

time: 112 us -> 130 us (1.16)
  local copies, waits for them, and re-layouts: 2.67 us -> 20.5 us
  Pallas kernels: 14.1 us -> 24.5 us
  starting transfers between devices: 66.6 us -> 59.7 us
  waiting for transfers between devices: 4.87 us -> 0.04 us
    pallas_call x0 -> x12, Pallas kernels: none -> 7.09 us  [mark(): pl.pallas_call(body, out_shape=jax.ShapeDtypeStruct((8, 128), jnp.float32...]
    unnamed x12 -> x26, local copies, waits for them, and re-layouts: 0.09 us -> 7.11 us
    ppermute x17, starting transfers between devices: 66.6 us -> 59.7 us  [hop(): return lax.ppermute(value, tuple(axes), pairs)]
    ppermute x17, waiting for transfers between devices: 4.87 us -> 0.04 us  [hop(): return lax.ppermute(value, tuple(axes), pairs)]
    ppermute x2, local copies, waits for them, and re-layouts: 0.21 us -> 4.52 us  [hop(): return lax.ppermute(value, tuple(axes), pairs)]
    concatenate x2, local copies, waits for them, and re-layouts: 0.07 us -> 3.73 us  [the longest x1 1.88 us: shards(): near.append(jnp.concatenate([a[2], after(b[2], point)], 0))]
    pallas_call x2, Pallas kernels: 9.2 us -> 11.8 us  [project(): pl.pallas_call(body, grid=(owners // per,), out_shape=jax.ShapeDtypeStruc...]
    optimization_barrier x0 -> x1, local copies, waits for them, and re-layouts: none -> 1.69 us  [after(): return lax.optimization_barrier((value, *others))[0]]
  transfers between devices with their start and end apart: 17 -> 17, of which waited for: 4 -> 0; matrix products, arithmetic and copies ran while one was open for 1% -> 12% of each run, Pallas kernels for 7% -> 14%
where the time goes in v4:
time: 130 us; the launch traced here: 129 us
  starting transfers between devices  59.7 us (46%)
  Pallas kernels  24.5 us (19%)
  blocking collectives  22.7 us (17%)
  local copies, waits for them, and re-layouts  20.5 us (16%)
    ppermute x17, starting transfers between devices, hop(): return lax.ppermute(value, tuple(axes), pairs)  59.7 us
    all_to_all x1, blocking collectives, shards(): received = lax.all_to_all(gate, ('x', 'core'), 0, 0, tiled=True)  22.7 us
    pallas_call x2, Pallas kernels, project(): pl.pallas_call(body, grid=(owners // per,), out_shape=jax.ShapeDtypeStruc...  11.8 us
    unnamed x26, local copies, waits for them, and re-layouts  7.11 us
    pallas_call x12, Pallas kernels, mark(): pl.pallas_call(body, out_shape=jax.ShapeDtypeStruct((8, 128), jnp.float32...  7.09 us
    ppermute x2, local copies, waits for them, and re-layouts, hop(): return lax.ppermute(value, tuple(axes), pairs)  4.52 us
    pallas_call x1, Pallas kernels, settle(): pl.pallas_call(body, grid=(4,), out_shape=jax.ShapeDtypeStruct((rows, 4 *...  3.27 us
  transfers between devices with their start and end apart: 17, of which 0 were waited for; matrix products, arithmetic and copies ran while one was open for 12% of the time, Pallas kernels for 14%

profile of v4, /device:TPU:1, one launch (start us, length us, event | category | flops | bytes accessed | tf_op | source)
XLA Modules:
  0.0 129.0 jit_solution(1013231081232217775)
XLA Ops:
  0.0 2.4 %dynamic-slice_bitcast_fusion.1 = (bf16[144,1792]{1,0:T(8,128)(2,1)}, bf16[144,1792]{1,0:T(8,128)(2,1)}) fusion(bf16[3584,288]{0,1:T(8,128)(2,1)} %param.7, s32[]{:T(128)S(6)} %select_n.11, s32[]{:T(128)S(6)} %select_n.13, s32[]{:T(128)S(6)} %select_n.12), kind=kLoop, calls=%fused_computation.3 | loop fusion | bytes 2064396 | tf_op jit(solution)/shard_map/dynamic_slice | solution.py:217
  2.6 0.8 normalize.1
  3.4 8.8 %collective-permute-start = (bf16[68,3584]{1,0:T(8,128)(2,1)S(1)}, bf16[68,3584]{1,0:T(8,128)(2,1)S(1)}, u32[]{:S(2)}, u32[]{:S(2)}) collective-permute-start(bf16[68,3584]{1,0:T(8,128)(2,1)S(1)} %normalize.1), channel_id=1, source_target_pairs={{0,1},{1,0},{2,3},{3,2},{4,5},{5,4},{6,7},{7,6},{8,9},{9,8},{10,11... | collective-permute-start | bytes 1462280 | tf_op jit(solution)/shard_map/ppermute | solution.py:30
  12.2 5.3 %collective-permute-start.2 = (bf16[144,1792]{1,0:T(8,128)(2,1)}, bf16[144,1792]{1,0:T(8,128)(2,1)}, u32[]{:S(2)}, u32[]{:S(2)}) collective-permute-start(bf16[144,1792]{1,0:T(8,128)(2,1)} %get-tuple-element.32), channel_id=1, source_target_pairs={{0,16},{1,113},{16,32},{17,1},{32,48},{33,17},{48,64},{49,33},{64,... | collective-permute-start | bytes 1548296 | tf_op jit(solution)/shard_map/ppermute | solution.py:30
  17.5 2.2 %collective-permute-start.3 = (bf16[144,1792]{1,0:T(8,128)(2,1)}, bf16[144,1792]{1,0:T(8,128)(2,1)}, u32[]{:S(2)}, u32[]{:S(2)}) collective-permute-start(bf16[144,1792]{1,0:T(8,128)(2,1)} %get-tuple-element.31), channel_id=1, source_target_pairs={{0,16},{1,113},{16,32},{17,1},{32,48},{33,17},{48,64},{49,33},{64,... | collective-permute-start | bytes 1548296 | tf_op jit(solution)/shard_map/ppermute | solution.py:30
  19.8 1.1 pad_maximum_fusion.refs_0_.pair_ref
  20.9 0.6 mark.12.refs_0_
  21.5 0.6 copy-done
  22.1 1.7 %copy.7 = bf16[2,68,3584]{2,0,1:T(2,128)(2,1)} copy(bf16[2,68,3584]{2,1,0:T(8,128)(2,1)S(1)} %copy-done) | data formatting | bytes 1949696 | tf_op jit(solution)/shard_map/optimization_barrier | solution.py:50
  23.8 4.4 %collective-permute-start.1 = (bf16[2,68,3584]{2,0,1:T(2,128)(2,1)}, bf16[2,68,3584]{2,0,1:T(2,128)(2,1)}, u32[]{:S(2)}, u32[]{:S(2)}) collective-permute-start(bf16[2,68,3584]{2,0,1:T(2,128)(2,1)} %copy.7), channel_id=1, source_target_pairs={{0,128},{1,385},{128,256},{129,1},{256,384},{257,129},{384,0},{385... | collective-permute-start | bytes 2924552 | tf_op jit(solution)/shard_map/ppermute | solution.py:30
  28.2 0.6 mark.13.refs_0_
  28.8 2.2 %collective-permute-start.4 = (bf16[144,1792]{1,0:T(8,128)(2,1)}, bf16[144,1792]{1,0:T(8,128)(2,1)S(1)}, u32[]{:S(2)}, u32[]{:S(2)}) collective-permute-start(bf16[144,1792]{1,0:T(8,128)(2,1)} %collective-permute-done.2.refs_1_), channel_id=1, source_target_pairs={{0,16},{1,113},{16,32},{17,1},{32,48},{33,17},{48,64},{49,33},{64,... | collective-permute-start | bytes 1548296 | tf_op jit(solution)/shard_map/ppermute | solution.py:30
  31.0 0.6 mark.14.refs_0_
  31.6 3.7 %collective-permute-start.6 = (bf16[144,1792]{1,0:T(8,128)(2,1)}, bf16[144,1792]{1,0:T(8,128)(2,1)}, u32[]{:S(2)}, u32[]{:S(2)}) collective-permute-start(bf16[144,1792]{1,0:T(8,128)(2,1)} %collective-permute-done.3.refs_1_), channel_id=1, source_target_pairs={{0,16},{1,113},{16,32},{17,1},{32,48},{33,17},{48,64},{49,33},{64,... | collective-permute-start | bytes 1548296 | tf_op jit(solution)/shard_map/ppermute | solution.py:30
  35.3 1.9 %constant_dynamic-update-slice_fusion.1 = bf16[288,1792]{1,0:T(8,128)(2,1)} fusion(bf16[144,1792]{1,0:T(8,128)(2,1)} %collective-permute-done.2.refs_1_), kind=kLoop, calls=%fused_computation.6 | loop fusion | bytes 1032192
  37.2 1.9 %constant_dynamic-update-slice_fusion.refs_2_ = bf16[288,1792]{1,0:T(8,128)(2,1)} fusion(bf16[288,1792]{1,0:T(8,128)(2,1)} %constant_dynamic-update-slice_fusion.1, bf16[144,1792]{1,0:T(8,128)(2,1)} %collective-permute-done.3.refs_1_), kind=kLoop, calls=%fused_computation.5 | loop fusion | bytes 1032192 | tf_op jit(solution)/shard_map/concatenate | solution.py:230
  39.0 5.1 %collective-permute-start.8 = (bf16[288,1792]{1,0:T(8,128)(2,1)}, bf16[288,1792]{1,0:T(8,128)(2,1)}, u32[]{:S(2)}, u32[]{:S(2)}) collective-permute-start(bf16[288,1792]{1,0:T(8,128)(2,1)} %constant_dynamic-update-slice_fusion.refs_2_), channel_id=1, source_target_pairs={{0,2},{1,15},{2,4},{3,1},{4,6},{5,3},{6,8},{7,5},{8,10},{9,7},{10,... | collective-permute-start | bytes 3096584 | tf_op jit(solution)/shard_map/ppermute | solution.py:30
  44.1 0.8 copy-done.10
  45.0 0.6 mark.15.refs_0_
  45.6 1.9 %collective-permute-start.7 = (bf16[144,1792]{1,0:T(8,128)(2,1)}, bf16[144,1792]{1,0:T(8,128)(2,1)}, u32[]{:S(2)}, u32[]{:S(2)}) collective-permute-start(bf16[144,1792]{1,0:T(8,128)(2,1)} %copy-done.10), channel_id=1, source_target_pairs={{0,16},{1,113},{16,32},{17,1},{32,48},{33,17},{48,64},{49,33},{64,... | collective-permute-start | bytes 1548296 | tf_op jit(solution)/shard_map/ppermute | solution.py:30
  47.5 1.9 %constant_dynamic-update-slice_fusion.3 = bf16[288,1792]{1,0:T(8,128)(2,1)} fusion(bf16[144,1792]{1,0:T(8,128)(2,1)} %copy-done.10), kind=kLoop, calls=%fused_computation.8 | loop fusion | bytes 1032192
  49.4 2.3 %copy.11.refs_1_.beside_ref = bf16[2,68,3584]{2,1,0:T(8,128)(2,1)} copy(bf16[2,68,3584]{2,0,1:T(2,128)(2,1)} %collective-permute-done.1) | data formatting | bytes 1949696 | tf_op jit(solution)/shard_map/ppermute | solution.py:30
  52.2 0.6 copy-done.1
  52.8 0.8 slice_bitcast_fusion
  53.7 4.1 %collective-permute-start.5 = (bf16[68,3584]{1,0:T(8,128)(2,1)}, bf16[68,3584]{1,0:T(8,128)(2,1)}, u32[]{:S(2)}, u32[]{:S(2)}) collective-permute-start(bf16[68,3584]{1,0:T(8,128)(2,1)} %slice_bitcast_fusion), channel_id=1, source_target_pairs={{0,128},{1,385},{128,256},{129,1},{256,384},{257,129},{384,0},{385... | collective-permute-start | bytes 1462280 | tf_op jit(solution)/shard_map/ppermute | solution.py:30
  57.8 0.6 mark.17.refs_0_
  58.4 1.9 %collective-permute-start.9 = (bf16[144,1792]{1,0:T(8,128)(2,1)}, bf16[144,1792]{1,0:T(8,128)(2,1)}, u32[]{:S(2)}, u32[]{:S(2)}) collective-permute-start(bf16[144,1792]{1,0:T(8,128)(2,1)} %collective-permute-done.6.refs_1_), channel_id=1, source_target_pairs={{0,16},{1,113},{16,32},{17,1},{32,48},{33,17},{48,64},{49,33},{64,... | collective-permute-start | bytes 1548296 | tf_op jit(solution)/shard_map/ppermute | solution.py:30
  60.3 1.9 %constant_dynamic-update-slice_fusion.2.refs_3_ = bf16[288,1792]{1,0:T(8,128)(2,1)} fusion(bf16[288,1792]{1,0:T(8,128)(2,1)} %constant_dynamic-update-slice_fusion.3, bf16[144,1792]{1,0:T(8,128)(2,1)} %collective-permute-done.6.refs_1_), kind=kLoop, calls=%fused_computation.7 | loop fusion | bytes 1032192 | tf_op jit(solution)/shard_map/concatenate | solution.py:238
  62.2 3.0 %collective-permute-start.12 = (bf16[288,1792]{1,0:T(8,128)(2,1)}, bf16[288,1792]{1,0:T(8,128)(2,1)}, u32[]{:S(2)}, u32[]{:S(2)}) collective-permute-start(bf16[288,1792]{1,0:T(8,128)(2,1)} %constant_dynamic-update-slice_fusion.2.refs_3_), channel_id=1, source_target_pairs={{0,2},{1,15},{2,4},{3,1},{4,6},{5,3},{6,8},{7,5},{8,10},{9,7},{10,... | collective-permute-start | bytes 3096584 | tf_op jit(solution)/shard_map/ppermute | solution.py:30
  65.2 0.6 mark.18.refs_0_
  65.7 1.9 %collective-permute-start.11 = (bf16[144,1792]{1,0:T(8,128)(2,1)}, bf16[144,1792]{1,0:T(8,128)(2,1)}, u32[]{:S(2)}, u32[]{:S(2)}) collective-permute-start(bf16[144,1792]{1,0:T(8,128)(2,1)} %collective-permute-done.7.refs_1_.refs_4_), channel_id=1, source_target_pairs={{0,16},{1,113},{16,32},{17,1},{32,48},{33,17},{48,64},{49,33},{64,... | collective-permute-start | bytes 1548296 | tf_op jit(solution)/shard_map/ppermute | solution.py:30
  67.7 3.0 %collective-permute-start.14 = (bf16[144,1792]{1,0:T(8,128)(2,1)}, bf16[144,1792]{1,0:T(8,128)(2,1)}, u32[]{:S(2)}, u32[]{:S(2)}) collective-permute-start(bf16[144,1792]{1,0:T(8,128)(2,1)} %collective-permute-done.7.refs_1_.refs_4_), channel_id=1, source_target_pairs={{0,2},{1,15},{2,4},{3,1},{4,6},{5,3},{6,8},{7,5},{8,10},{9,7},{10,... | collective-permute-start | bytes 1548296 | tf_op jit(solution)/shard_map/ppermute | solution.py:30
  70.7 0.6 mark.19.refs_0_
  71.2 3.6 %collective-permute-start.10 = (bf16[2,68,3584]{2,0,1:T(2,128)(2,1)}, bf16[2,68,3584]{2,0,1:T(2,128)(2,1)}, u32[]{:S(2)}, u32[]{:S(2)}) collective-permute-start(bf16[2,68,3584]{2,0,1:T(2,128)(2,1)} %collective-permute-done.1), channel_id=1, source_target_pairs={{0,1},{1,0},{2,3},{3,2},{4,5},{5,4},{6,7},{7,6},{8,9},{9,8},{10,11... | collective-permute-start | bytes 2924552 | tf_op jit(solution)/shard_map/ppermute | solution.py:30
  74.9 0.6 mark.20.refs_0_
  75.4 3.3 %collective-permute-start.16 = (bf16[144,1792]{1,0:T(8,128)(2,1)}, bf16[144,1792]{1,0:T(8,128)(2,1)}, u32[]{:S(2)}, u32[]{:S(2)}) collective-permute-start(bf16[144,1792]{1,0:T(8,128)(2,1)} %collective-permute-done.9.refs_1_.refs_5_), channel_id=1, source_target_pairs={{0,2},{1,15},{2,4},{3,1},{4,6},{5,3},{6,8},{7,5},{8,10},{9,7},{10,... | collective-permute-start | bytes 1548296 | tf_op jit(solution)/shard_map/ppermute | solution.py:30
  78.7 2.3 %copy.10.refs_1_.swapped_ref = bf16[2,68,3584]{2,1,0:T(8,128)(2,1)} copy(bf16[2,68,3584]{2,0,1:T(2,128)(2,1)} %collective-permute-done.10) | data formatting | bytes 1949696 | tf_op jit(solution)/shard_map/ppermute | solution.py:30
  81.0 0.6 mark.21.refs_0_
  81.6 3.3 %collective-permute-start.13 = (bf16[68,3584]{1,0:T(8,128)(2,1)}, bf16[68,3584]{1,0:T(8,128)(2,1)}, u32[]{:S(2)}, u32[]{:S(2)}) collective-permute-start(bf16[68,3584]{1,0:T(8,128)(2,1)} %collective-permute-done.5.refs_1_.distant_ref), channel_id=1, source_target_pairs={{0,1},{1,0},{2,3},{3,2},{4,5},{5,4},{6,7},{7,6},{8,9},{9,8},{10,11... | collective-permute-start | bytes 1462280 | tf_op jit(solution)/shard_map/ppermute | solution.py:30
  84.9 0.6 mark.22.refs_0_
  85.5 2.2 %collective-permute-start.15 = (bf16[144,1792]{1,0:T(8,128)(2,1)}, bf16[144,1792]{1,0:T(8,128)(2,1)}, u32[]{:S(2)}, u32[]{:S(2)}) collective-permute-start(bf16[144,1792]{1,0:T(8,128)(2,1)} %collective-permute-done.11.refs_1_.refs_0_), channel_id=1, source_target_pairs={{0,2},{1,15},{2,4},{3,1},{4,6},{5,3},{6,8},{7,5},{8,10},{9,7},{10,... | collective-permute-start | bytes 1548296 | tf_op jit(solution)/shard_map/ppermute | solution.py:30
  87.8 0.6 mark.23
  88.4 1.2 copy-done.2
  89.6 1.6 %line_up.1.a_ref = bf16[640,3584]{1,0:T(8,128)(2,1)S(1)} custom-call(s32[5]{0:T(128)S(1)} %copy-done.6, bf16[2,68,3584]{2,1,0:T(8,128)(2,1)S(1)} %copy-done, bf16[2,68,3584]{2,1,0:T(8,128)(2,1)S(1)} %copy-done.1, bf16[68,3584]{1,0:T(8,128)(2,1)} %collective-permute-done.5.refs_1_.distant_ref, bf16[2,68,3584]{2,1,0:T(8,128)(2,1)S(1)} %copy-done.2, ...), custom_call_target="tpu_custom_call" | custom-call | bytes 1024 | tf_op jit(solution)/shard_map/line_up/pallas_call | solution.py:111
  91.2 8.9 %project.2.refs_2_ = bf16[8,68,1152]{2,1,0:T(8,128)(2,1)S(1)} custom-call(s32[5]{0:T(128)S(1)} %copy-done.6, bf16[640,3584]{1,0:T(8,128)(2,1)S(1)} %line_up.1.a_ref, bf16[144,3584]{1,0:T(8,128)(2,1)S(1)} %dynamic-slice_bitcast_fusion.refs_0_.refs_1_, bf16[144,3584]{1,0:T(8,128)(2,1)S(1)} %dynamic-slice_bitcast_fusion.refs_0_.refs_1_, ...), custom_call_target="tpu_custom_call" | custom-call | bytes 1024 | tf_op jit(solution)/shard_map/project/pallas_call | solution.py:159
  100.1 2.9 %project.3 = bf16[8,68,1152]{2,1,0:T(8,128)(2,1)S(1)} custom-call(s32[5]{0:T(128)S(1)} %copy-done.6, bf16[640,3584]{1,0:T(8,128)(2,1)S(1)} %line_up.1.a_ref, bf16[144,1792]{1,0:T(8,128)(2,1)} %collective-permute-done.11.refs_1_.refs_0_, bf16[144,1792]{1,0:T(8,128)(2,1)} %collective-permute-done.15.refs_1_, ...), custom_call_target="tpu_custom_call", output_to_operand_aliasing={{}: (4, {})} | custom-call | bytes 1024 | tf_op jit(solution)/shard_map/project/pallas_call | solution.py:159
  103.0 22.7 %all_to_all.5.ref = bf16[8,68,1152]{2,1,0:T(8,128)(2,1)S(1)} all-to-all(bf16[8,68,1152]{2,1,0:T(8,128)(2,1)S(1)} %project.3), channel_id=1, replica_groups=mesh['x'=4,'z'=8,'y'=8,'core'=2] {'x','core'}, dimensions={0} | all-to-all | bytes 2506752 | tf_op jit(solution)/shard_map/all_to_all | solution.py:259
  125.7 3.3 %settle.1 = bf16[68,9216]{1,0:T(8,128)(2,1)} custom-call(s32[5]{0:T(128)S(1)} %copy-done.6, bf16[8,68,1152]{2,1,0:T(8,128)(2,1)S(1)} %all_to_all.5.ref), custom_call_target="tpu_custom_call" | custom-call | bytes 1024 | tf_op jit(solution)/shard_map/settle/pallas_call | solution.py:191
  (41 shorter events, 0.8 us)
Async XLA Ops:
  0.0 2.5 %copy-start.11 = (f32[3584]{0:T(1024)S(1)}, f32[3584]{0:T(1024)}, u32[]{:S(2)}) copy-start(f32[3584]{0:T(1024)} %param.6) | copy-start | bytes 43012
  0.0 2.6 %copy-start.4 = (bf16[68,3584]{1,0:T(8,128)(2,1)S(1)}, bf16[68,3584]{1,0:T(8,128)(2,1)}, u32[]{:S(2)}) copy-start(bf16[68,3584]{1,0:T(8,128)(2,1)} %rows_ref.1) | copy-start | bytes 1462276
  0.0 2.6 %copy-start.7 = (s32[64]{0:T(128)S(1)}, s32[64]{0:T(128)}, u32[]{:S(2)}) copy-start(s32[64]{0:T(128)} %param.8) | copy-start | bytes 772
  0.0 2.6 %copy-start.8 = (s32[64]{0:T(128)S(1)}, s32[64]{0:T(128)}, u32[]{:S(2)}) copy-start(s32[64]{0:T(128)} %param.9) | copy-start | bytes 772
  0.0 19.7 %copy-start.9 = (bf16[3584,288]{0,1:T(8,128)(2,1)S(1)}, bf16[3584,288]{0,1:T(8,128)(2,1)}, u32[]{:S(2)}) copy-start(bf16[3584,288]{0,1:T(8,128)(2,1)} %param.7) | copy-start | bytes 6193156
  2.6 14.9 %copy-start.5 = (s32[5]{0:T(128)}, s32[5]{0:T(128)S(1)}, u32[]{:S(2)}) copy-start(s32[5]{0:T(128)S(1)} %stack.32.place_ref) | copy-start | bytes 64
  3.4 16.4 %collective-permute-start = (bf16[68,3584]{1,0:T(8,128)(2,1)S(1)}, bf16[68,3584]{1,0:T(8,128)(2,1)S(1)}, u32[]{:S(2)}, u32[]{:S(2)}) collective-permute-start(bf16[68,3584]{1,0:T(8,128)(2,1)S(1)} %normalize.1), channel_id=1, source_target_pairs={{0,1},{1,0},{2,3},{3,2},{4,5},{5,4},{6,7},{7,6},{8,9},{9,8},{10,11... | collective-permute-start | bytes 1462280 | tf_op jit(solution)/shard_map/ppermute | solution.py:30
  12.2 16.0 %collective-permute-start.2 = (bf16[144,1792]{1,0:T(8,128)(2,1)}, bf16[144,1792]{1,0:T(8,128)(2,1)}, u32[]{:S(2)}, u32[]{:S(2)}) collective-permute-start(bf16[144,1792]{1,0:T(8,128)(2,1)} %get-tuple-element.32), channel_id=1, source_target_pairs={{0,16},{1,113},{16,32},{17,1},{32,48},{33,17},{48,64},{49,33},{64,... | collective-permute-start | bytes 1548296 | tf_op jit(solution)/shard_map/ppermute | solution.py:30
  17.5 13.4 %collective-permute-start.3 = (bf16[144,1792]{1,0:T(8,128)(2,1)}, bf16[144,1792]{1,0:T(8,128)(2,1)}, u32[]{:S(2)}, u32[]{:S(2)}) collective-permute-start(bf16[144,1792]{1,0:T(8,128)(2,1)} %get-tuple-element.31), channel_id=1, source_target_pairs={{0,16},{1,113},{16,32},{17,1},{32,48},{33,17},{48,64},{49,33},{64,... | collective-permute-start | bytes 1548296 | tf_op jit(solution)/shard_map/ppermute | solution.py:30
  20.9 1.2 copy-start
  23.8 25.6 %collective-permute-start.1 = (bf16[2,68,3584]{2,0,1:T(2,128)(2,1)}, bf16[2,68,3584]{2,0,1:T(2,128)(2,1)}, u32[]{:S(2)}, u32[]{:S(2)}) collective-permute-start(bf16[2,68,3584]{2,0,1:T(2,128)(2,1)} %copy.7), channel_id=1, source_target_pairs={{0,128},{1,385},{128,256},{129,1},{256,384},{257,129},{384,0},{385... | collective-permute-start | bytes 2924552 | tf_op jit(solution)/shard_map/ppermute | solution.py:30
  28.8 15.3 %collective-permute-start.4 = (bf16[144,1792]{1,0:T(8,128)(2,1)}, bf16[144,1792]{1,0:T(8,128)(2,1)S(1)}, u32[]{:S(2)}, u32[]{:S(2)}) collective-permute-start(bf16[144,1792]{1,0:T(8,128)(2,1)} %collective-permute-done.2.refs_1_), channel_id=1, source_target_pairs={{0,16},{1,113},{16,32},{17,1},{32,48},{33,17},{48,64},{49,33},{64,... | collective-permute-start | bytes 1548296 | tf_op jit(solution)/shard_map/ppermute | solution.py:30
  31.6 26.2 %collective-permute-start.6 = (bf16[144,1792]{1,0:T(8,128)(2,1)}, bf16[144,1792]{1,0:T(8,128)(2,1)}, u32[]{:S(2)}, u32[]{:S(2)}) collective-permute-start(bf16[144,1792]{1,0:T(8,128)(2,1)} %collective-permute-done.3.refs_1_), channel_id=1, source_target_pairs={{0,16},{1,113},{16,32},{17,1},{32,48},{33,17},{48,64},{49,33},{64,... | collective-permute-start | bytes 1548296 | tf_op jit(solution)/shard_map/ppermute | solution.py:30
  39.0 26.1 %collective-permute-start.8 = (bf16[288,1792]{1,0:T(8,128)(2,1)}, bf16[288,1792]{1,0:T(8,128)(2,1)}, u32[]{:S(2)}, u32[]{:S(2)}) collective-permute-start(bf16[288,1792]{1,0:T(8,128)(2,1)} %constant_dynamic-update-slice_fusion.refs_2_), channel_id=1, source_target_pairs={{0,2},{1,15},{2,4},{3,1},{4,6},{5,3},{6,8},{7,5},{8,10},{9,7},{10,... | collective-permute-start | bytes 3096584 | tf_op jit(solution)/shard_map/ppermute | solution.py:30
  44.1 0.8 copy-start.10
  45.6 19.6 %collective-permute-start.7 = (bf16[144,1792]{1,0:T(8,128)(2,1)}, bf16[144,1792]{1,0:T(8,128)(2,1)}, u32[]{:S(2)}, u32[]{:S(2)}) collective-permute-start(bf16[144,1792]{1,0:T(8,128)(2,1)} %copy-done.10), channel_id=1, source_target_pairs={{0,16},{1,113},{16,32},{17,1},{32,48},{33,17},{48,64},{49,33},{64,... | collective-permute-start | bytes 1548296 | tf_op jit(solution)/shard_map/ppermute | solution.py:30
  51.6 1.2 copy-start.1
  53.7 17.0 %collective-permute-start.5 = (bf16[68,3584]{1,0:T(8,128)(2,1)}, bf16[68,3584]{1,0:T(8,128)(2,1)}, u32[]{:S(2)}, u32[]{:S(2)}) collective-permute-start(bf16[68,3584]{1,0:T(8,128)(2,1)} %slice_bitcast_fusion), channel_id=1, source_target_pairs={{0,128},{1,385},{128,256},{129,1},{256,384},{257,129},{384,0},{385... | collective-permute-start | bytes 1462280 | tf_op jit(solution)/shard_map/ppermute | solution.py:30
  58.4 16.5 %collective-permute-start.9 = (bf16[144,1792]{1,0:T(8,128)(2,1)}, bf16[144,1792]{1,0:T(8,128)(2,1)}, u32[]{:S(2)}, u32[]{:S(2)}) collective-permute-start(bf16[144,1792]{1,0:T(8,128)(2,1)} %collective-permute-done.6.refs_1_), channel_id=1, source_target_pairs={{0,16},{1,113},{16,32},{17,1},{32,48},{33,17},{48,64},{49,33},{64,... | collective-permute-start | bytes 1548296 | tf_op jit(solution)/shard_map/ppermute | solution.py:30
  62.2 22.8 %collective-permute-start.12 = (bf16[288,1792]{1,0:T(8,128)(2,1)}, bf16[288,1792]{1,0:T(8,128)(2,1)}, u32[]{:S(2)}, u32[]{:S(2)}) collective-permute-start(bf16[288,1792]{1,0:T(8,128)(2,1)} %constant_dynamic-update-slice_fusion.2.refs_3_), channel_id=1, source_target_pairs={{0,2},{1,15},{2,4},{3,1},{4,6},{5,3},{6,8},{7,5},{8,10},{9,7},{10,... | collective-permute-start | bytes 3096584 | tf_op jit(solution)/shard_map/ppermute | solution.py:30
  65.7 19.2 %collective-permute-start.11 = (bf16[144,1792]{1,0:T(8,128)(2,1)}, bf16[144,1792]{1,0:T(8,128)(2,1)}, u32[]{:S(2)}, u32[]{:S(2)}) collective-permute-start(bf16[144,1792]{1,0:T(8,128)(2,1)} %collective-permute-done.7.refs_1_.refs_4_), channel_id=1, source_target_pairs={{0,16},{1,113},{16,32},{17,1},{32,48},{33,17},{48,64},{49,33},{64,... | collective-permute-start | bytes 1548296 | tf_op jit(solution)/shard_map/ppermute | solution.py:30
  67.7 20.1 %collective-permute-start.14 = (bf16[144,1792]{1,0:T(8,128)(2,1)}, bf16[144,1792]{1,0:T(8,128)(2,1)}, u32[]{:S(2)}, u32[]{:S(2)}) collective-permute-start(bf16[144,1792]{1,0:T(8,128)(2,1)} %collective-permute-done.7.refs_1_.refs_4_), channel_id=1, source_target_pairs={{0,2},{1,15},{2,4},{3,1},{4,6},{5,3},{6,8},{7,5},{8,10},{9,7},{10,... | collective-permute-start | bytes 1548296 | tf_op jit(solution)/shard_map/ppermute | solution.py:30
  71.2 7.5 %collective-permute-start.10 = (bf16[2,68,3584]{2,0,1:T(2,128)(2,1)}, bf16[2,68,3584]{2,0,1:T(2,128)(2,1)}, u32[]{:S(2)}, u32[]{:S(2)}) collective-permute-start(bf16[2,68,3584]{2,0,1:T(2,128)(2,1)} %collective-permute-done.1), channel_id=1, source_target_pairs={{0,1},{1,0},{2,3},{3,2},{4,5},{5,4},{6,7},{7,6},{8,9},{9,8},{10,11... | collective-permute-start | bytes 2924552 | tf_op jit(solution)/shard_map/ppermute | solution.py:30
  75.4 15.7 %collective-permute-start.16 = (bf16[144,1792]{1,0:T(8,128)(2,1)}, bf16[144,1792]{1,0:T(8,128)(2,1)}, u32[]{:S(2)}, u32[]{:S(2)}) collective-permute-start(bf16[144,1792]{1,0:T(8,128)(2,1)} %collective-permute-done.9.refs_1_.refs_5_), channel_id=1, source_target_pairs={{0,2},{1,15},{2,4},{3,1},{4,6},{5,3},{6,8},{7,5},{8,10},{9,7},{10,... | collective-permute-start | bytes 1548296 | tf_op jit(solution)/shard_map/ppermute | solution.py:30
  81.6 6.2 %collective-permute-start.13 = (bf16[68,3584]{1,0:T(8,128)(2,1)}, bf16[68,3584]{1,0:T(8,128)(2,1)}, u32[]{:S(2)}, u32[]{:S(2)}) collective-permute-start(bf16[68,3584]{1,0:T(8,128)(2,1)} %collective-permute-done.5.refs_1_.distant_ref), channel_id=1, source_target_pairs={{0,1},{1,0},{2,3},{3,2},{4,5},{5,4},{6,7},{7,6},{8,9},{9,8},{10,11... | collective-permute-start | bytes 1462280 | tf_op jit(solution)/shard_map/ppermute | solution.py:30
  85.5 2.8 %copy-start.6 = (s32[5]{0:T(128)S(1)}, s32[5]{0:T(128)}, u32[]{:S(2)}) copy-start(s32[5]{0:T(128)} %copy-done.5) | copy-start | bytes 64
  85.5 14.6 %collective-permute-start.15 = (bf16[144,1792]{1,0:T(8,128)(2,1)}, bf16[144,1792]{1,0:T(8,128)(2,1)}, u32[]{:S(2)}, u32[]{:S(2)}) collective-permute-start(bf16[144,1792]{1,0:T(8,128)(2,1)} %collective-permute-done.11.refs_1_.refs_0_), channel_id=1, source_target_pairs={{0,2},{1,15},{2,4},{3,1},{4,6},{5,3},{6,8},{7,5},{8,10},{9,7},{10,... | collective-permute-start | bytes 1548296 | tf_op jit(solution)/shard_map/ppermute | solution.py:30
  88.4 1.2 copy-start.2
  89.6 1.6 %copy-start.3 = (bf16[288,1792]{1,0:T(8,128)(2,1)S(1)}, bf16[288,1792]{1,0:T(8,128)(2,1)}, u32[]{:S(2)}) copy-start(bf16[288,1792]{1,0:T(8,128)(2,1)} %constant_dynamic-update-slice_fusion.2.refs_3_) | copy-start | bytes 3096580

commit v5 on v3

--- a/solution.py
+++ b/solution.py
@@ -73,35 +73,22 @@
     )(place, layer_rows, norm_gain.reshape(1, -1), req_len.reshape(1, -1), req_rank.reshape(1, -1))
 
 
-def line_up(place, pair, beside, distant, swapped, across):
-    rows, features = pair.shape[1:]
-
-    def body(place_ref, pair_ref, beside_ref, distant_ref, swapped_ref, across_ref, out):
-        x, c = place_ref[0], place_ref[1]
-        back = 2 * c - 1
-
-        def put(step, core, block):
-            owner = lax.rem(x + step + 4, 4) * 2 + core
-            out[pl.ds(pl.multiple_of(owner * PAD, 16), rows), :] = block
-
-        put(0, c, pair_ref[0])
-        put(0, 1 - c, pair_ref[1])
-        put(back, c, beside_ref[0])
-        put(back, 1 - c, beside_ref[1])
-        put(2, c, distant_ref[0])
-        put(-back, 1 - c, swapped_ref[0])
-        put(-back, c, swapped_ref[1])
-        put(2, 1 - c, across_ref[0])
-
-    return pl.pallas_call(
-        body,
-        out_shape=jax.ShapeDtypeStruct((8 * PAD, features), pair.dtype),
-        in_specs=[pl.BlockSpec(memory_space=pltpu.SMEM)] + [pl.BlockSpec(memory_space=pltpu.VMEM)] * 5,
+def line_up(gathered):
+    owners, rows, features = gathered.shape
+
+    def body(ref, out):
+        for i in range(owners):
+            out[i * PAD : i * PAD + rows, :] = ref[i]
+
+    return pl.pallas_call(
+        body,
+        out_shape=jax.ShapeDtypeStruct((owners * PAD, features), gathered.dtype),
+        in_specs=[pl.BlockSpec(memory_space=pltpu.VMEM)],
         out_specs=pl.BlockSpec(memory_space=pltpu.VMEM),
         compiler_params=pltpu.CompilerParams(vmem_limit_bytes=12 * MIB),
         cost_estimate=TINY,
         name="line_up",
-    )(place, pair, beside, distant, swapped, across)
+    )(gathered)
 
 
 def project(place, rows_in, near, far, rows, columns, into=None):
@@ -206,23 +193,21 @@
     b.append(along_z(b[0]))
 
     normed = normalize(place, layer_rows, after(norm_gain, a[0]), req_len, req_rank)
-    pair = jnp.stack([normed, other_core(normed)])
-    beside = along_x(pair)
-    a.append(along_z(after(a[1], pair)))
+    copies = jnp.broadcast_to(normed, (8, rows, features))
+    gathered = lax.all_to_all(copies, ("x", "core"), 0, 0, tiled=True)
+    a.append(along_z(a[1]))
     b.append(along_z(b[1]))
     near = [jnp.concatenate([a[1], b[1]], 0)]
     far = [along_y(near[0])]
-    distant = along_x(after(beside[:1], a[2]))
     a.append(along_z(a[2]))
-    b.append(along_z(after(b[2], beside)))
+    b.append(along_z(b[2]))
     near.append(jnp.concatenate([a[2], b[2]], 0))
     far.append(along_y(near[1]))
     a.append(along_z(after(a[3], far[0])))
     near += [a[3], b[3]]
-    far += [along_y(a[3]), along_y(after(b[3], distant))]
+    far += [along_y(a[3]), along_y(b[3])]
     far_4 = along_y(after(a[4], far[1], far[2]))
-    swapped, across = other_core(after(beside, a[3])), other_core(distant)
-    rows_in = line_up(place, pair, beside, distant, swapped, across)
+    rows_in = line_up(gathered)
 
     columns = 4 * width
     own_half = lax.dynamic_slice(weights, (c * half_width, 0), (half_width, features))

time: 112 us -> 117 us (1.045)
  starting transfers between devices: 66.6 us -> 60.1 us
  local copies, waits for them, and re-layouts: 2.67 us -> 7.89 us
  waiting for transfers between devices: 4.87 us -> 8.32 us
  Pallas kernels: 14.1 us -> 17.2 us
    ppermute x17 -> x12, starting transfers between devices: 66.6 us -> 48.8 us  [hop(): return lax.ppermute(value, tuple(axes), pairs)]
    all_to_all x0 -> x1, starting transfers between devices: none -> 11.3 us  [shards(): gathered = lax.all_to_all(copies, ('x', 'core'), 0, 0, tiled=True)]
    unnamed x12 -> x28, local copies, waits for them, and re-layouts: 0.09 us -> 4.08 us
    ppermute x17 -> x12, waiting for transfers between devices: 4.87 us -> 8.32 us  [hop(): return lax.ppermute(value, tuple(axes), pairs)]
    broadcast_in_dim x0 -> x1, local copies, waits for them, and re-layouts: none -> 2.23 us  [shards(): copies = jnp.broadcast_to(normed, (8, rows, features))]
    pallas_call x1, Pallas kernels: 0.82 us -> 2.59 us  [line_up(): pl.pallas_call(body, out_shape=jax.ShapeDtypeStruct((owners * PAD, featur...]
    pallas_call x2, Pallas kernels: 9.2 us -> 10.5 us  [project(): pl.pallas_call(body, grid=(owners // per,), out_shape=jax.ShapeDtypeStruc...]
  transfers between devices with their start and end apart: 17 -> 13, of which waited for: 4 -> 4; matrix products, arithmetic and copies ran while one was open for 1% -> 0% of each run, Pallas kernels for 7% -> 9%
where the time goes in v5:
time: 117 us
  starting transfers between devices  60.1 us (51%)
  blocking collectives  23 us (20%)
  Pallas kernels  17.2 us (15%)
  waiting for transfers between devices  8.32 us (7%)
  local copies, waits for them, and re-layouts  7.89 us (7%)
    ppermute x12, starting transfers between devices, hop(): return lax.ppermute(value, tuple(axes), pairs)  48.8 us
    all_to_all x1, blocking collectives, shards(): received = lax.all_to_all(gate, ('x', 'core'), 0, 0, tiled=True)  23 us
    all_to_all x1, starting transfers between devices, shards(): gathered = lax.all_to_all(copies, ('x', 'core'), 0, 0, tiled=True)  11.3 us
    pallas_call x2, Pallas kernels, project(): pl.pallas_call(body, grid=(owners // per,), out_shape=jax.ShapeDtypeStruc...  10.5 us
    ppermute x12, waiting for transfers between devices, hop(): return lax.ppermute(value, tuple(axes), pairs)  8.32 us
    unnamed x28, local copies, waits for them, and re-layouts  4.08 us
    pallas_call x1, Pallas kernels, settle(): pl.pallas_call(body, grid=(4,), out_shape=jax.ShapeDtypeStruct((rows, 4 *...  3.27 us
    pallas_call x1, Pallas kernels, line_up(): pl.pallas_call(body, out_shape=jax.ShapeDtypeStruct((owners * PAD, featur...  2.59 us
  transfers between devices with their start and end apart: 13, of which 4 were waited for; matrix products, arithmetic and copies ran while one was open for 0% of the time, Pallas kernels for 9%

profile of v5, /device:TPU:1, one launch (start us, length us, event | category | flops | bytes accessed | tf_op | source)
XLA Modules:
  0.0 116.9 jit_solution(10134981429043872565)
XLA Ops:
  0.0 1.3 %dynamic-slice_bitcast_fusion.1 = (bf16[144,1792]{1,0:T(8,128)(2,1)S(1)}, bf16[144,1792]{1,0:T(8,128)(2,1)S(1)}) fusion(bf16[3584,288]{0,1:T(8,128)(2,1)} %param.7, s32[]{:T(128)S(6)} %select_n.11, s32[]{:T(128)S(6)} %select_n.13, s32[]{:T(128)S(6)} %select_n.12), kind=kLoop, calls=%fused_computation.1 | loop fusion | bytes 2064396 | tf_op jit(solution)/shard_map/dynamic_slice | solution.py:189
  1.4 0.1 stack.23.place_ref
  1.5 0.8 normalize.1
  2.3 2.2 %broadcast_in_dim.3 = bf16[8,68,3584]{2,1,0:T(8,128)(2,1)} broadcast(bf16[68,3584]{1,0:T(8,128)(2,1)S(1)} %normalize.1), dimensions={1,2} | broadcast | bytes 4386816 | tf_op jit(solution)/shard_map/broadcast_in_dim | solution.py:196
  4.6 11.3 %all-to-all-start = ((bf16[8,68,3584]{2,1,0:T(8,128)(2,1)}), bf16[8,68,3584]{2,1,0:T(8,128)(2,1)}, u32[]{:S(2)}, u32[]{:S(2)}) async-start(bf16[8,68,3584]{2,1,0:T(8,128)(2,1)} %broadcast_in_dim.3), calls=%async_computation | async-start | bytes 8257536 | tf_op jit(solution)/shard_map/all_to_all | solution.py:197
  15.8 5.3 %collective-permute-start = (bf16[144,1792]{1,0:T(8,128)(2,1)S(1)}, bf16[144,1792]{1,0:T(8,128)(2,1)S(1)}, u32[]{:S(2)}, u32[]{:S(2)}) collective-permute-start(bf16[144,1792]{1,0:T(8,128)(2,1)S(1)} %get-tuple-element.14), channel_id=1, source_target_pairs={{0,16},{1,113},{16,32},{17,1},{32,48},{33,17},{48,64},{49,33},{64,... | collective-permute-start | bytes 1548296 | tf_op jit(solution)/shard_map/ppermute | solution.py:30
  21.2 0.0 copy-start.11
  21.2 2.3 %collective-permute-start.3 = (bf16[144,1792]{1,0:T(8,128)(2,1)S(1)}, bf16[144,1792]{1,0:T(8,128)(2,1)S(1)}, u32[]{:S(2)}, u32[]{:S(2)}) collective-permute-start(bf16[144,1792]{1,0:T(8,128)(2,1)S(1)} %get-tuple-element.13), channel_id=1, source_target_pairs={{0,16},{1,113},{16,32},{17,1},{32,48},{33,17},{48,64},{49,33},{64,... | collective-permute-start | bytes 1548296 | tf_op jit(solution)/shard_map/ppermute | solution.py:30
  23.5 3.7 %collective-permute-done = bf16[144,1792]{1,0:T(8,128)(2,1)S(1)} collective-permute-done((bf16[144,1792]{1,0:T(8,128)(2,1)S(1)}, bf16[144,1792]{1,0:T(8,128)(2,1)S(1)}, u32[]{:S(2)}, u32[]{:S(2)}) %collective-permute-start) | collective-permute-done | bytes 516128 | tf_op jit(solution)/shard_map/ppermute | solution.py:30
  27.2 5.4 %collective-permute-start.1 = (bf16[144,1792]{1,0:T(8,128)(2,1)S(1)}, bf16[144,1792]{1,0:T(8,128)(2,1)S(1)}, u32[]{:S(2)}, u32[]{:S(2)}) collective-permute-start(bf16[144,1792]{1,0:T(8,128)(2,1)S(1)} %collective-permute-done), channel_id=1, source_target_pairs={{0,16},{1,113},{16,32},{17,1},{32,48},{33,17},{48,64},{49,33},{64,... | collective-permute-start | bytes 1548296 | tf_op jit(solution)/shard_map/ppermute | solution.py:30
  32.6 0.1 collective-permute-done.3
  32.7 5.0 %collective-permute-start.6 = (bf16[144,1792]{1,0:T(8,128)(2,1)S(1)}, bf16[144,1792]{1,0:T(8,128)(2,1)S(1)}, u32[]{:S(2)}, u32[]{:S(2)}) collective-permute-start(bf16[144,1792]{1,0:T(8,128)(2,1)S(1)} %collective-permute-done.3), channel_id=1, source_target_pairs={{0,16},{1,113},{16,32},{17,1},{32,48},{33,17},{48,64},{49,33},{64,... | collective-permute-start | bytes 1548296 | tf_op jit(solution)/shard_map/ppermute | solution.py:30
  37.8 5.1 %collective-permute-start.4 = (bf16[288,1792]{1,0:T(8,128)(2,1)S(1)}, bf16[288,1792]{1,0:T(8,128)(2,1)S(1)}, u32[]{:S(2)}, u32[]{:S(2)}) collective-permute-start(bf16[288,1792]{1,0:T(8,128)(2,1)S(1)} %constant_dynamic-update-slice_fusion.refs_2_), channel_id=1, source_target_pairs={{0,2},{1,15},{2,4},{3,1},{4,6},{5,3},{6,8},{7,5},{8,10},{9,7},{10,... | collective-permute-start | bytes 3096584 | tf_op jit(solution)/shard_map/ppermute | solution.py:30
  42.9 0.0 collective-permute-done.1
  42.9 1.9 %collective-permute-start.2 = (bf16[144,1792]{1,0:T(8,128)(2,1)S(1)}, bf16[144,1792]{1,0:T(8,128)(2,1)S(1)}, u32[]{:S(2)}, u32[]{:S(2)}) collective-permute-start(bf16[144,1792]{1,0:T(8,128)(2,1)S(1)} %collective-permute-done.1), channel_id=1, source_target_pairs={{0,16},{1,113},{16,32},{17,1},{32,48},{33,17},{48,64},{49,33},{64,... | collective-permute-start | bytes 1548296 | tf_op jit(solution)/shard_map/ppermute | solution.py:30
  44.9 0.0 collective-permute-done.6
  45.0 4.3 %collective-permute-start.7 = (bf16[288,1792]{1,0:T(8,128)(2,1)S(1)}, bf16[288,1792]{1,0:T(8,128)(2,1)S(1)}, u32[]{:S(2)}, u32[]{:S(2)}) collective-permute-start(bf16[288,1792]{1,0:T(8,128)(2,1)S(1)} %constant_dynamic-update-slice_fusion.2.refs_3_), channel_id=1, source_target_pairs={{0,2},{1,15},{2,4},{3,1},{4,6},{5,3},{6,8},{7,5},{8,10},{9,7},{10,... | collective-permute-start | bytes 3096584 | tf_op jit(solution)/shard_map/ppermute | solution.py:30
  49.3 5.4 %collective-permute-start.10 = (bf16[144,1792]{1,0:T(8,128)(2,1)S(1)}, bf16[144,1792]{1,0:T(8,128)(2,1)}, u32[]{:S(2)}, u32[]{:S(2)}) collective-permute-start(bf16[144,1792]{1,0:T(8,128)(2,1)S(1)} %collective-permute-done.6), channel_id=1, source_target_pairs={{0,16},{1,113},{16,32},{17,1},{32,48},{33,17},{48,64},{49,33},{64,... | collective-permute-start | bytes 1548296 | tf_op jit(solution)/shard_map/ppermute | solution.py:30
  54.7 0.0 collective-permute-done.4.refs_6_
  54.7 0.0 copy-start
  54.8 1.0 copy-done
  55.7 0.0 collective-permute-done.2.refs_4_
  55.7 1.9 %collective-permute-start.5 = (bf16[144,1792]{1,0:T(8,128)(2,1)S(1)}, bf16[144,1792]{1,0:T(8,128)(2,1)}, u32[]{:S(2)}, u32[]{:S(2)}) collective-permute-start(bf16[144,1792]{1,0:T(8,128)(2,1)S(1)} %collective-permute-done.2.refs_4_), channel_id=1, source_target_pairs={{0,16},{1,113},{16,32},{17,1},{32,48},{33,17},{48,64},{49,33},{64,... | collective-permute-start | bytes 1548296 | tf_op jit(solution)/shard_map/ppermute | solution.py:30
  57.6 5.2 %collective-permute-start.8 = (bf16[144,1792]{1,0:T(8,128)(2,1)S(1)}, bf16[144,1792]{1,0:T(8,128)(2,1)S(1)}, u32[]{:S(2)}, u32[]{:S(2)}) collective-permute-start(bf16[144,1792]{1,0:T(8,128)(2,1)S(1)} %collective-permute-done.2.refs_4_), channel_id=1, source_target_pairs={{0,2},{1,15},{2,4},{3,1},{4,6},{5,3},{6,8},{7,5},{8,10},{9,7},{10,... | collective-permute-start | bytes 1548296 | tf_op jit(solution)/shard_map/ppermute | solution.py:30
  62.8 0.8 copy-done.4
  63.6 0.0 collective-permute-done.10.refs_5_
  63.6 1.9 %collective-permute-start.11 = (bf16[144,1792]{1,0:T(8,128)(2,1)}, bf16[144,1792]{1,0:T(8,128)(2,1)}, u32[]{:S(2)}, u32[]{:S(2)}) collective-permute-start(bf16[144,1792]{1,0:T(8,128)(2,1)} %collective-permute-done.10.refs_5_), channel_id=1, source_target_pairs={{0,2},{1,15},{2,4},{3,1},{4,6},{5,3},{6,8},{7,5},{8,10},{9,7},{10,... | collective-permute-start | bytes 1548296 | tf_op jit(solution)/shard_map/ppermute | solution.py:30
  65.5 0.8 collective-permute-done.5.refs_0_
  66.3 0.0 collective-permute-done.7.refs_7_
  66.3 1.0 copy-done.2
  67.3 3.7 %collective-permute-done.8.refs_8_ = bf16[144,1792]{1,0:T(8,128)(2,1)S(1)} collective-permute-done((bf16[144,1792]{1,0:T(8,128)(2,1)S(1)}, bf16[144,1792]{1,0:T(8,128)(2,1)S(1)}, u32[]{:S(2)}, u32[]{:S(2)}) %collective-permute-start.8) | collective-permute-done | bytes 516128 | tf_op jit(solution)/shard_map/ppermute | solution.py:30
  71.1 0.8 copy-done.6
  71.9 5.0 %collective-permute-start.9 = (bf16[144,1792]{1,0:T(8,128)(2,1)}, bf16[144,1792]{1,0:T(8,128)(2,1)}, u32[]{:S(2)}, u32[]{:S(2)}) collective-permute-start(bf16[144,1792]{1,0:T(8,128)(2,1)} %collective-permute-done.5.refs_0_), channel_id=1, source_target_pairs={{0,2},{1,15},{2,4},{3,1},{4,6},{5,3},{6,8},{7,5},{8,10},{9,7},{10,... | collective-permute-start | bytes 1548296 | tf_op jit(solution)/shard_map/ppermute | solution.py:30
  76.9 0.0 copy-done.11
  76.9 0.1 dynamic-slice_bitcast_fusion.refs_0_.refs_1_
  77.0 0.0 all-to-all-done.ref
  77.0 0.0 copy-start.1
  77.0 2.6 %line_up.1.a_ref = bf16[640,3584]{1,0:T(8,128)(2,1)S(1)} custom-call(bf16[8,68,3584]{2,1,0:T(8,128)(2,1)} %all-to-all-done.ref), custom_call_target="tpu_custom_call" | custom-call | bytes 1024 | tf_op jit(solution)/shard_map/line_up/pallas_call | solution.py:83
  79.6 0.0 collective-permute-done.11.refs_9_
  79.6 0.0 copy-done.1
  79.6 0.1 copy-done.3
  79.8 0.1 copy-done.5
  79.9 0.2 copy-done.7
  80.0 7.6 %project.2.refs_2_ = bf16[8,68,1152]{2,1,0:T(8,128)(2,1)S(1)} custom-call(s32[5]{0:T(128)S(1)} %stack.23.place_ref, bf16[640,3584]{1,0:T(8,128)(2,1)S(1)} %line_up.1.a_ref, bf16[144,3584]{1,0:T(8,128)(2,1)S(1)} %dynamic-slice_bitcast_fusion.refs_0_.refs_1_, bf16[144,3584]{1,0:T(8,128)(2,1)S(1)} %dynamic-slice_bitcast_fusion.refs_0_.refs_1_, ...), custom_call_target="tpu_custom_call" | custom-call | bytes 1024 | tf_op jit(solution)/shard_map/project/pallas_call | solution.py:131
  87.7 0.0 collective-permute-done.9.refs_1_
  87.7 2.9 %project.3 = bf16[8,68,1152]{2,1,0:T(8,128)(2,1)S(1)} custom-call(s32[5]{0:T(128)S(1)} %stack.23.place_ref, bf16[640,3584]{1,0:T(8,128)(2,1)S(1)} %line_up.1.a_ref, bf16[144,1792]{1,0:T(8,128)(2,1)} %collective-permute-done.5.refs_0_, bf16[144,1792]{1,0:T(8,128)(2,1)} %collective-permute-done.9.refs_1_, ...), custom_call_target="tpu_custom_call", output_to_operand_aliasing={{}: (4, {})} | custom-call | bytes 1024 | tf_op jit(solution)/shard_map/project/pallas_call | solution.py:131
  90.6 23.0 %all_to_all.10.ref = bf16[8,68,1152]{2,1,0:T(8,128)(2,1)S(1)} all-to-all(bf16[8,68,1152]{2,1,0:T(8,128)(2,1)S(1)} %project.3), channel_id=1, replica_groups=mesh['x'=4,'z'=8,'y'=8,'core'=2] {'x','core'}, dimensions={0} | all-to-all | bytes 2506752 | tf_op jit(solution)/shard_map/all_to_all | solution.py:216
  113.6 3.3 %settle.1 = bf16[68,9216]{1,0:T(8,128)(2,1)} custom-call(s32[5]{0:T(128)S(1)} %stack.23.place_ref, bf16[8,68,1152]{2,1,0:T(8,128)(2,1)S(1)} %all_to_all.10.ref), custom_call_target="tpu_custom_call" | custom-call | bytes 1024 | tf_op jit(solution)/shard_map/settle/pallas_call | solution.py:163
  (19 shorter events, 0.2 us)
Async XLA Ops:
  0.0 1.4 %copy-start.12 = (f32[3584]{0:T(1024)S(1)}, f32[3584]{0:T(1024)}, u32[]{:S(2)}) copy-start(f32[3584]{0:T(1024)} %param.6) | copy-start | bytes 43012
  0.0 1.5 %copy-start.9 = (s32[64]{0:T(128)S(1)}, s32[64]{0:T(128)}, u32[]{:S(2)}) copy-start(s32[64]{0:T(128)} %param.8) | copy-start | bytes 772
  0.0 1.5 %copy-start.10 = (s32[64]{0:T(128)S(1)}, s32[64]{0:T(128)}, u32[]{:S(2)}) copy-start(s32[64]{0:T(128)} %param.9) | copy-start | bytes 772
  0.0 1.5 %copy-start.8 = (bf16[68,3584]{1,0:T(8,128)(2,1)S(1)}, bf16[68,3584]{1,0:T(8,128)(2,1)}, u32[]{:S(2)}) copy-start(bf16[68,3584]{1,0:T(8,128)(2,1)} %rows_ref.1) | copy-start | bytes 1462276
  4.6 72.4 %all-to-all-start = ((bf16[8,68,3584]{2,1,0:T(8,128)(2,1)}), bf16[8,68,3584]{2,1,0:T(8,128)(2,1)}, u32[]{:S(2)}, u32[]{:S(2)}) async-start(bf16[8,68,3584]{2,1,0:T(8,128)(2,1)} %broadcast_in_dim.3), calls=%async_computation | async-start | bytes 8257536 | tf_op jit(solution)/shard_map/all_to_all | solution.py:197
  15.8 11.3 %collective-permute-start = (bf16[144,1792]{1,0:T(8,128)(2,1)S(1)}, bf16[144,1792]{1,0:T(8,128)(2,1)S(1)}, u32[]{:S(2)}, u32[]{:S(2)}) collective-permute-start(bf16[144,1792]{1,0:T(8,128)(2,1)S(1)} %get-tuple-element.14), channel_id=1, source_target_pairs={{0,16},{1,113},{16,32},{17,1},{32,48},{33,17},{48,64},{49,33},{64,... | collective-permute-start | bytes 1548296 | tf_op jit(solution)/shard_map/ppermute | solution.py:30
  21.2 55.7 %copy-start.11 = (bf16[3584,288]{0,1:T(8,128)(2,1)S(1)}, bf16[3584,288]{0,1:T(8,128)(2,1)}, u32[]{:S(2)}) copy-start(bf16[3584,288]{0,1:T(8,128)(2,1)} %param.7) | copy-start | bytes 6193156
  21.2 11.5 %collective-permute-start.3 = (bf16[144,1792]{1,0:T(8,128)(2,1)S(1)}, bf16[144,1792]{1,0:T(8,128)(2,1)S(1)}, u32[]{:S(2)}, u32[]{:S(2)}) collective-permute-start(bf16[144,1792]{1,0:T(8,128)(2,1)S(1)} %get-tuple-element.13), channel_id=1, source_target_pairs={{0,16},{1,113},{16,32},{17,1},{32,48},{33,17},{48,64},{49,33},{64,... | collective-permute-start | bytes 1548296 | tf_op jit(solution)/shard_map/ppermute | solution.py:30
  27.2 15.7 %collective-permute-start.1 = (bf16[144,1792]{1,0:T(8,128)(2,1)S(1)}, bf16[144,1792]{1,0:T(8,128)(2,1)S(1)}, u32[]{:S(2)}, u32[]{:S(2)}) collective-permute-start(bf16[144,1792]{1,0:T(8,128)(2,1)S(1)} %collective-permute-done), channel_id=1, source_target_pairs={{0,16},{1,113},{16,32},{17,1},{32,48},{33,17},{48,64},{49,33},{64,... | collective-permute-start | bytes 1548296 | tf_op jit(solution)/shard_map/ppermute | solution.py:30
  32.7 12.2 %collective-permute-start.6 = (bf16[144,1792]{1,0:T(8,128)(2,1)S(1)}, bf16[144,1792]{1,0:T(8,128)(2,1)S(1)}, u32[]{:S(2)}, u32[]{:S(2)}) collective-permute-start(bf16[144,1792]{1,0:T(8,128)(2,1)S(1)} %collective-permute-done.3), channel_id=1, source_target_pairs={{0,16},{1,113},{16,32},{17,1},{32,48},{33,17},{48,64},{49,33},{64,... | collective-permute-start | bytes 1548296 | tf_op jit(solution)/shard_map/ppermute | solution.py:30
  37.8 16.9 %collective-permute-start.4 = (bf16[288,1792]{1,0:T(8,128)(2,1)S(1)}, bf16[288,1792]{1,0:T(8,128)(2,1)S(1)}, u32[]{:S(2)}, u32[]{:S(2)}) collective-permute-start(bf16[288,1792]{1,0:T(8,128)(2,1)S(1)} %constant_dynamic-update-slice_fusion.refs_2_), channel_id=1, source_target_pairs={{0,2},{1,15},{2,4},{3,1},{4,6},{5,3},{6,8},{7,5},{8,10},{9,7},{10,... | collective-permute-start | bytes 3096584 | tf_op jit(solution)/shard_map/ppermute | solution.py:30
  42.9 12.8 %collective-permute-start.2 = (bf16[144,1792]{1,0:T(8,128)(2,1)S(1)}, bf16[144,1792]{1,0:T(8,128)(2,1)S(1)}, u32[]{:S(2)}, u32[]{:S(2)}) collective-permute-start(bf16[144,1792]{1,0:T(8,128)(2,1)S(1)} %collective-permute-done.1), channel_id=1, source_target_pairs={{0,16},{1,113},{16,32},{17,1},{32,48},{33,17},{48,64},{49,33},{64,... | collective-permute-start | bytes 1548296 | tf_op jit(solution)/shard_map/ppermute | solution.py:30
  45.0 21.3 %collective-permute-start.7 = (bf16[288,1792]{1,0:T(8,128)(2,1)S(1)}, bf16[288,1792]{1,0:T(8,128)(2,1)S(1)}, u32[]{:S(2)}, u32[]{:S(2)}) collective-permute-start(bf16[288,1792]{1,0:T(8,128)(2,1)S(1)} %constant_dynamic-update-slice_fusion.2.refs_3_), channel_id=1, source_target_pairs={{0,2},{1,15},{2,4},{3,1},{4,6},{5,3},{6,8},{7,5},{8,10},{9,7},{10,... | collective-permute-start | bytes 3096584 | tf_op jit(solution)/shard_map/ppermute | solution.py:30
  49.3 14.3 %collective-permute-start.10 = (bf16[144,1792]{1,0:T(8,128)(2,1)S(1)}, bf16[144,1792]{1,0:T(8,128)(2,1)}, u32[]{:S(2)}, u32[]{:S(2)}) collective-permute-start(bf16[144,1792]{1,0:T(8,128)(2,1)S(1)} %collective-permute-done.6), channel_id=1, source_target_pairs={{0,16},{1,113},{16,32},{17,1},{32,48},{33,17},{48,64},{49,33},{64,... | collective-permute-start | bytes 1548296 | tf_op jit(solution)/shard_map/ppermute | solution.py:30
  54.7 1.0 copy-start
  55.7 10.6 %collective-permute-start.5 = (bf16[144,1792]{1,0:T(8,128)(2,1)S(1)}, bf16[144,1792]{1,0:T(8,128)(2,1)}, u32[]{:S(2)}, u32[]{:S(2)}) collective-permute-start(bf16[144,1792]{1,0:T(8,128)(2,1)S(1)} %collective-permute-done.2.refs_4_), channel_id=1, source_target_pairs={{0,16},{1,113},{16,32},{17,1},{32,48},{33,17},{48,64},{49,33},{64,... | collective-permute-start | bytes 1548296 | tf_op jit(solution)/shard_map/ppermute | solution.py:30
  57.6 13.4 %collective-permute-start.8 = (bf16[144,1792]{1,0:T(8,128)(2,1)S(1)}, bf16[144,1792]{1,0:T(8,128)(2,1)S(1)}, u32[]{:S(2)}, u32[]{:S(2)}) collective-permute-start(bf16[144,1792]{1,0:T(8,128)(2,1)S(1)} %collective-permute-done.2.refs_4_), channel_id=1, source_target_pairs={{0,2},{1,15},{2,4},{3,1},{4,6},{5,3},{6,8},{7,5},{8,10},{9,7},{10,... | collective-permute-start | bytes 1548296 | tf_op jit(solution)/shard_map/ppermute | solution.py:30
  62.8 0.8 copy-start.4
  63.6 16.0 %collective-permute-start.11 = (bf16[144,1792]{1,0:T(8,128)(2,1)}, bf16[144,1792]{1,0:T(8,128)(2,1)}, u32[]{:S(2)}, u32[]{:S(2)}) collective-permute-start(bf16[144,1792]{1,0:T(8,128)(2,1)} %collective-permute-done.10.refs_5_), channel_id=1, source_target_pairs={{0,2},{1,15},{2,4},{3,1},{4,6},{5,3},{6,8},{7,5},{8,10},{9,7},{10,... | collective-permute-start | bytes 1548296 | tf_op jit(solution)/shard_map/ppermute | solution.py:30
  66.3 1.0 copy-start.2
  71.1 0.8 copy-start.6
  71.9 15.8 %collective-permute-start.9 = (bf16[144,1792]{1,0:T(8,128)(2,1)}, bf16[144,1792]{1,0:T(8,128)(2,1)}, u32[]{:S(2)}, u32[]{:S(2)}) collective-permute-start(bf16[144,1792]{1,0:T(8,128)(2,1)} %collective-permute-done.5.refs_0_), channel_id=1, source_target_pairs={{0,2},{1,15},{2,4},{3,1},{4,6},{5,3},{6,8},{7,5},{8,10},{9,7},{10,... | collective-permute-start | bytes 1548296 | tf_op jit(solution)/shard_map/ppermute | solution.py:30
  77.0 2.7 %copy-start.1 = (bf16[288,1792]{1,0:T(8,128)(2,1)S(1)}, bf16[288,1792]{1,0:T(8,128)(2,1)}, u32[]{:S(2)}) copy-start(bf16[288,1792]{1,0:T(8,128)(2,1)} %copy-done) | copy-start | bytes 3096580
  77.0 2.8 %copy-start.3 = (bf16[288,1792]{1,0:T(8,128)(2,1)S(1)}, bf16[288,1792]{1,0:T(8,128)(2,1)}, u32[]{:S(2)}) copy-start(bf16[288,1792]{1,0:T(8,128)(2,1)} %copy-done.2) | copy-start | bytes 3096580
  77.0 2.9 %copy-start.5 = (bf16[144,1792]{1,0:T(8,128)(2,1)S(1)}, bf16[144,1792]{1,0:T(8,128)(2,1)}, u32[]{:S(2)}) copy-start(bf16[144,1792]{1,0:T(8,128)(2,1)} %copy-done.4) | copy-start | bytes 1548292
  77.0 3.0 %copy-start.7 = (bf16[144,1792]{1,0:T(8,128)(2,1)S(1)}, bf16[144,1792]{1,0:T(8,128)(2,1)}, u32[]{:S(2)}) copy-start(bf16[144,1792]{1,0:T(8,128)(2,1)} %copy-done.6) | copy-start | bytes 1548292

commit v6 on v3

--- a/solution.py
+++ b/solution.py
@@ -50,6 +50,21 @@
     return lax.optimization_barrier((value, *others))[0]
 
 
+def mark(*seen):
+    def body(*refs):
+        refs[-1][...] = jnp.zeros_like(refs[-1])
+
+    return pl.pallas_call(
+        body,
+        out_shape=jax.ShapeDtypeStruct((8, 128), jnp.float32),
+        in_specs=[pl.BlockSpec(memory_space=pltpu.VMEM)] * len(seen),
+        out_specs=pl.BlockSpec(memory_space=pltpu.VMEM),
+        compiler_params=pltpu.CompilerParams(has_side_effects=True, vmem_limit_bytes=8 * MIB),
+        cost_estimate=pl.CostEstimate(flops=10**11, bytes_accessed=1024, transcendentals=0),
+        name="mark",
+    )(*seen)
+
+
 def normalize(place, layer_rows, norm_gain, req_len, req_rank):
     rows, features = layer_rows.shape
 
@@ -73,10 +88,10 @@
     )(place, layer_rows, norm_gain.reshape(1, -1), req_len.reshape(1, -1), req_rank.reshape(1, -1))
 
 
-def line_up(place, pair, beside, distant, swapped, across):
+def line_up(place, pair, beside, distant, swapped):
     rows, features = pair.shape[1:]
 
-    def body(place_ref, pair_ref, beside_ref, distant_ref, swapped_ref, across_ref, out):
+    def body(place_ref, pair_ref, beside_ref, distant_ref, swapped_ref, out):
         x, c = place_ref[0], place_ref[1]
         back = 2 * c - 1
 
@@ -91,26 +106,26 @@
         put(2, c, distant_ref[0])
         put(-back, 1 - c, swapped_ref[0])
         put(-back, c, swapped_ref[1])
-        put(2, 1 - c, across_ref[0])
+        put(2, 1 - c, swapped_ref[2])
 
     return pl.pallas_call(
         body,
         out_shape=jax.ShapeDtypeStruct((8 * PAD, features), pair.dtype),
-        in_specs=[pl.BlockSpec(memory_space=pltpu.SMEM)] + [pl.BlockSpec(memory_space=pltpu.VMEM)] * 5,
+        in_specs=[pl.BlockSpec(memory_space=pltpu.SMEM)] + [pl.BlockSpec(memory_space=pltpu.VMEM)] * 4,
         out_specs=pl.BlockSpec(memory_space=pltpu.VMEM),
         compiler_params=pltpu.CompilerParams(vmem_limit_bytes=12 * MIB),
         cost_estimate=TINY,
         name="line_up",
-    )(place, pair, beside, distant, swapped, across)
-
-
-def project(place, rows_in, near, far, rows, columns, into=None):
+    )(place, pair, beside, distant, swapped)
+
+
+def project(place, rows_in, near, far, rows, columns, start, lead, into=None):
     total, features = rows_in.shape
     half = features // 2
     owners = total // PAD
     given = list(near) + [w for w in far if w is not None]
-    made = sum(w.shape[0] for w in near)
-    span = columns if into is None else -(-made // 128) * 128
+    end = start + lead + sum(w.shape[0] for w in near)
+    span = columns if into is None else -(-end // 128) * 128
     per = 4
     block = per * PAD
 
@@ -129,6 +144,9 @@
             else:
                 w_first.append(ref[...])
                 w_second.append(rest.pop(0)[...])
+        if lead:
+            w_first.insert(0, w_first[0][:lead])
+            w_second.insert(0, w_second[0][:lead])
         contract = (((1,), (1,)), ((), ()))
         gate = lax.dot_general(a_first, jnp.concatenate(w_first, 0), contract, preferred_element_type=jnp.float32)
         gate += lax.dot_general(a_second, jnp.concatenate(w_second, 0), contract, preferred_element_type=jnp.float32)
@@ -136,7 +154,7 @@
         if into is not None:
             out[...] = refs[len(given)][...]
         for i in range(per):
-            out[i, :, :made] = act[i * PAD : i * PAD + rows]
+            out[i, :, start:end] = act[i * PAD : i * PAD + rows]
 
     whole = pl.BlockSpec(memory_space=pltpu.VMEM)
     part = pl.BlockSpec((per, rows, span), lambda i: (i, 0, 0))
@@ -165,8 +183,8 @@
         def take(core, k, n=1):
             return ref[core, :, k * half : (k + n) * half]
 
-        parts = [take(0, 6, 2), take(0, 4, 2), take(0, 2, 2), take(0, 1), take(1, 1)]
-        for k in (2, 4, 6):
+        parts = [take(0, 1, 2), take(0, 6, 2), take(0, 4, 2), take(0, 3), take(1, 3)]
+        for k in (4, 6, 1):
             parts += [take(1, k + 1), take(1, k)]
         parts += [take(0, 0), take(1, 0)]
         line = jnp.concatenate([p.astype(jnp.float32) for p in parts], axis=1)
@@ -204,30 +222,45 @@
     a, b = [own(c)], [own(1 - c)]
     a.append(along_z(a[0]))
     b.append(along_z(b[0]))
-
     normed = normalize(place, layer_rows, after(norm_gain, a[0]), req_len, req_rank)
     pair = jnp.stack([normed, other_core(normed)])
     beside = along_x(pair)
-    a.append(along_z(after(a[1], pair)))
+
+    a.append(along_z(a[1]))
+    point = mark(a[1])
+    b[1] = after(b[1], point)
     b.append(along_z(b[1]))
     near = [jnp.concatenate([a[1], b[1]], 0)]
     far = [along_y(near[0])]
-    distant = along_x(after(beside[:1], a[2]))
+
     a.append(along_z(a[2]))
-    b.append(along_z(after(b[2], beside)))
+    point = mark(point, a[2], beside)
+    distant = along_x(after(beside[:1], point))
+    b[2] = after(b[2], point)
+    b.append(along_z(b[2]))
     near.append(jnp.concatenate([a[2], b[2]], 0))
     far.append(along_y(near[1]))
-    a.append(along_z(after(a[3], far[0])))
+
+    a.append(along_z(a[3]))
+    point = mark(point, a[3], distant, far[0])
+    swapped = other_core(after(jnp.concatenate([beside, distant], 0), point))
     near += [a[3], b[3]]
-    far += [along_y(a[3]), along_y(after(b[3], distant))]
-    far_4 = along_y(after(a[4], far[1], far[2]))
-    swapped, across = other_core(after(beside, a[3])), other_core(distant)
-    rows_in = line_up(place, pair, beside, distant, swapped, across)
-
+    far += [along_y(after(a[3], point)), along_y(after(b[3], point))]
+
+    near.append(a[4])
+    far.append(along_y(a[4]))
+    point = mark(point, a[4], far[1])
+    rows_in = line_up(place, pair, beside, after(distant, point), swapped)
+
+    own_half = lax.dynamic_slice(weights, (c * half_width, 0), (half_width, features))
     columns = 4 * width
-    own_half = lax.dynamic_slice(weights, (c * half_width, 0), (half_width, features))
-    gate = project(place, after(rows_in, a[4]), [own_half, own_half] + near, [None, None] + far, rows, columns)
-    gate = project(place, rows_in, a[4:], [far_4], rows, columns, gate)
+    begin = half_width * 3 // 128 * 128
+    gate = project(
+        place, rows_in, [own_half] + near[:2], [None] + far[:2], rows, columns, begin, half_width * 3 - begin
+    )
+    begin = half_width // 128 * 128
+    gate = project(place, rows_in, near[2:4], far[2:4], rows, columns, begin, half_width - begin, gate)
+    gate = project(place, rows_in, near[4:], far[4:], rows, columns, 0, 0, gate)
     received = lax.all_to_all(gate, ("x", "core"), 0, 0, tiled=True)
     return settle(place, received, width)
 

time: 112 us -> 107 us (0.955)
  starting transfers between devices: 66.6 us -> 60 us
  Pallas kernels: 14.1 us -> 15.7 us
    ppermute x17 -> x16, starting transfers between devices: 66.6 us -> 60 us  [hop(): return lax.ppermute(value, tuple(axes), pairs)]
    pallas_call x2 -> x3, Pallas kernels: 9.2 us -> 10.3 us  [project(): pl.pallas_call(body, grid=(owners // per,), out_shape=jax.ShapeDtypeStruc...]
    ppermute x17 -> x16, waiting for transfers between devices: 4.87 us -> 5.02 us  [hop(): return lax.ppermute(value, tuple(axes), pairs)]
  transfers between devices with their start and end apart: 17 -> 16, of which waited for: 4 -> 4; matrix products, arithmetic and copies ran while one was open for 1% -> 1% of each run, Pallas kernels for 7% -> 9%
where the time goes in v6:
time: 107 us; the launch traced here: 106 us
  starting transfers between devices  60 us (56%)
  blocking collectives  21.8 us (20%)
  Pallas kernels  15.7 us (15%)
  waiting for transfers between devices  5.02 us (5%)
  local copies, waits for them, and re-layouts  2.96 us (3%)
    ppermute x16, starting transfers between devices, hop(): return lax.ppermute(value, tuple(axes), pairs)  60 us
    all_to_all x1, blocking collectives, shards(): received = lax.all_to_all(gate, ('x', 'core'), 0, 0, tiled=True)  21.8 us
    pallas_call x3, Pallas kernels, project(): pl.pallas_call(body, grid=(owners // per,), out_shape=jax.ShapeDtypeStruc...  10.3 us
    ppermute x16, waiting for transfers between devices, hop(): return lax.ppermute(value, tuple(axes), pairs)  5.02 us
    pallas_call x1, Pallas kernels, settle(): pl.pallas_call(body, grid=(4,), out_shape=jax.ShapeDtypeStruct((rows, 4 *...  3.22 us
  transfers between devices with their start and end apart: 16, of which 4 were waited for; matrix products, arithmetic and copies ran while one was open for 1% of the time, Pallas kernels for 9%

profile of v6, /device:TPU:1, one launch (start us, length us, event | category | flops | bytes accessed | tf_op | source)
XLA Modules:
  0.0 106.2 jit_solution(10542372662782618045)
XLA Ops:
  0.0 1.3 %dynamic-slice_bitcast_fusion.1 = (bf16[144,1792]{1,0:T(8,128)(2,1)S(1)}, bf16[144,1792]{1,0:T(8,128)(2,1)S(1)}) fusion(bf16[3584,288]{0,1:T(8,128)(2,1)} %param.7, s32[]{:T(128)S(6)} %select_n.11, s32[]{:T(128)S(6)} %select_n.13, s32[]{:T(128)S(6)} %select_n.12), kind=kLoop, calls=%fused_computation.3 | loop fusion | bytes 2064396 | tf_op jit(solution)/shard_map/dynamic_slice | solution.py:220
  1.4 0.1 stack.32.place_ref
  1.5 0.8 normalize.1
  2.3 8.8 %collective-permute-start = (bf16[68,3584]{1,0:T(8,128)(2,1)S(1)}, bf16[68,3584]{1,0:T(8,128)(2,1)S(1)}, u32[]{:S(2)}, u32[]{:S(2)}) collective-permute-start(bf16[68,3584]{1,0:T(8,128)(2,1)S(1)} %normalize.1), channel_id=1, source_target_pairs={{0,1},{1,0},{2,3},{3,2},{4,5},{5,4},{6,7},{7,6},{8,9},{9,8},{10,11... | collective-permute-start | bytes 1462280 | tf_op jit(solution)/shard_map/ppermute | solution.py:30
  11.1 5.3 %collective-permute-start.2 = (bf16[144,1792]{1,0:T(8,128)(2,1)S(1)}, bf16[144,1792]{1,0:T(8,128)(2,1)S(1)}, u32[]{:S(2)}, u32[]{:S(2)}) collective-permute-start(bf16[144,1792]{1,0:T(8,128)(2,1)S(1)} %get-tuple-element.22), channel_id=1, source_target_pairs={{0,16},{1,113},{16,32},{17,1},{32,48},{33,17},{48,64},{49,33},{64,... | collective-permute-start | bytes 1548296 | tf_op jit(solution)/shard_map/ppermute | solution.py:30
  16.4 2.2 %collective-permute-start.6 = (bf16[144,1792]{1,0:T(8,128)(2,1)S(1)}, bf16[144,1792]{1,0:T(8,128)(2,1)S(1)}, u32[]{:S(2)}, u32[]{:S(2)}) collective-permute-start(bf16[144,1792]{1,0:T(8,128)(2,1)S(1)} %get-tuple-element.21), channel_id=1, source_target_pairs={{0,16},{1,113},{16,32},{17,1},{32,48},{33,17},{48,64},{49,33},{64,... | collective-permute-start | bytes 1548296 | tf_op jit(solution)/shard_map/ppermute | solution.py:30
  18.6 0.0 collective-permute-done
  18.6 0.1 pad_maximum_fusion.1.pair_ref
  18.7 0.8 copy.8
  19.5 4.4 %collective-permute-start.1 = (bf16[2,68,3584]{2,0,1:T(2,128)(2,1)S(1)}, bf16[2,68,3584]{2,0,1:T(2,128)(2,1)S(1)}, u32[]{:S(2)}, u32[]{:S(2)}) collective-permute-start(bf16[2,68,3584]{2,0,1:T(2,128)(2,1)S(1)} %copy.8), channel_id=1, source_target_pairs={{0,128},{1,385},{128,256},{129,1},{256,384},{257,129},{384,0},{385... | collective-permute-start | bytes 2924552 | tf_op jit(solution)/shard_map/ppermute | solution.py:30
  23.9 0.0 collective-permute-done.2.refs_0_
  23.9 3.9 %collective-permute-start.3 = (bf16[144,1792]{1,0:T(8,128)(2,1)S(1)}, bf16[144,1792]{1,0:T(8,128)(2,1)S(1)}, u32[]{:S(2)}, u32[]{:S(2)}) collective-permute-start(bf16[144,1792]{1,0:T(8,128)(2,1)S(1)} %collective-permute-done.2.refs_0_), channel_id=1, source_target_pairs={{0,16},{1,113},{16,32},{17,1},{32,48},{33,17},{48,64},{49,33},{64,... | collective-permute-start | bytes 1548296 | tf_op jit(solution)/shard_map/ppermute | solution.py:30
  27.8 0.2 collective-permute-done.6
  28.0 5.3 %collective-permute-start.9 = (bf16[144,1792]{1,0:T(8,128)(2,1)S(1)}, bf16[144,1792]{1,0:T(8,128)(2,1)S(1)}, u32[]{:S(2)}, u32[]{:S(2)}) collective-permute-start(bf16[144,1792]{1,0:T(8,128)(2,1)S(1)} %collective-permute-done.6), channel_id=1, source_target_pairs={{0,16},{1,113},{16,32},{17,1},{32,48},{33,17},{48,64},{49,33},{64,... | collective-permute-start | bytes 1548296 | tf_op jit(solution)/shard_map/ppermute | solution.py:30
  33.4 0.0 copy-start
  33.4 5.1 %collective-permute-start.7 = (bf16[288,1792]{1,0:T(8,128)(2,1)S(1)}, bf16[288,1792]{1,0:T(8,128)(2,1)S(1)}, u32[]{:S(2)}, u32[]{:S(2)}) collective-permute-start(bf16[288,1792]{1,0:T(8,128)(2,1)S(1)} %constant_dynamic-update-slice_fusion.refs_1_), channel_id=1, source_target_pairs={{0,2},{1,15},{2,4},{3,1},{4,6},{5,3},{6,8},{7,5},{8,10},{9,7},{10,... | collective-permute-start | bytes 3096584 | tf_op jit(solution)/shard_map/ppermute | solution.py:30
  38.5 0.0 collective-permute-done.3.refs_1_
  38.5 1.9 %collective-permute-start.5 = (bf16[144,1792]{1,0:T(8,128)(2,1)S(1)}, bf16[144,1792]{1,0:T(8,128)(2,1)S(1)}, u32[]{:S(2)}, u32[]{:S(2)}) collective-permute-start(bf16[144,1792]{1,0:T(8,128)(2,1)S(1)} %collective-permute-done.3.refs_1_), channel_id=1, source_target_pairs={{0,16},{1,113},{16,32},{17,1},{32,48},{33,17},{48,64},{49,33},{64,... | collective-permute-start | bytes 1548296 | tf_op jit(solution)/shard_map/ppermute | solution.py:30
  40.4 0.0 collective-permute-done.1
  40.4 0.1 copy.12.refs_2_.beside_ref
  40.6 0.0 copy-start.5
  40.6 4.2 %collective-permute-start.4 = (bf16[1,68,3584]{2,1,0:T(8,128)(2,1)S(1)}, bf16[1,68,3584]{2,1,0:T(8,128)(2,1)S(1)}, u32[]{:S(2)}, u32[]{:S(2)}) collective-permute-start(bf16[1,68,3584]{2,1,0:T(8,128)(2,1)S(1)} %slice.4), channel_id=1, source_target_pairs={{0,128},{1,385},{128,256},{129,1},{256,384},{257,129},{384,0},{385... | collective-permute-start | bytes 1462280 | tf_op jit(solution)/shard_map/ppermute | solution.py:30
  44.9 0.1 dynamic-slice_bitcast_fusion.refs_0_
  45.0 0.0 collective-permute-done.9
  45.0 1.9 %collective-permute-start.13 = (bf16[144,1792]{1,0:T(8,128)(2,1)S(1)}, bf16[144,1792]{1,0:T(8,128)(2,1)S(1)}, u32[]{:S(2)}, u32[]{:S(2)}) collective-permute-start(bf16[144,1792]{1,0:T(8,128)(2,1)S(1)} %collective-permute-done.9), channel_id=1, source_target_pairs={{0,16},{1,113},{16,32},{17,1},{32,48},{33,17},{48,64},{49,33},{64,... | collective-permute-start | bytes 1548296 | tf_op jit(solution)/shard_map/ppermute | solution.py:30
  47.0 3.5 %collective-permute-start.10 = (bf16[288,1792]{1,0:T(8,128)(2,1)S(1)}, bf16[288,1792]{1,0:T(8,128)(2,1)S(1)}, u32[]{:S(2)}, u32[]{:S(2)}) collective-permute-start(bf16[288,1792]{1,0:T(8,128)(2,1)S(1)} %constant_dynamic-update-slice_fusion.2.refs_2_), channel_id=1, source_target_pairs={{0,2},{1,15},{2,4},{3,1},{4,6},{5,3},{6,8},{7,5},{8,10},{9,7},{10,... | collective-permute-start | bytes 3096584 | tf_op jit(solution)/shard_map/ppermute | solution.py:30
  50.5 0.0 collective-permute-done.5.refs_1_.refs_0_
  50.5 1.9 %collective-permute-start.8 = (bf16[144,1792]{1,0:T(8,128)(2,1)S(1)}, bf16[144,1792]{1,0:T(8,128)(2,1)S(1)}, u32[]{:S(2)}, u32[]{:S(2)}) collective-permute-start(bf16[144,1792]{1,0:T(8,128)(2,1)S(1)} %collective-permute-done.5.refs_1_.refs_0_), channel_id=1, source_target_pairs={{0,16},{1,113},{16,32},{17,1},{32,48},{33,17},{48,64},{49,33},{64,... | collective-permute-start | bytes 1548296 | tf_op jit(solution)/shard_map/ppermute | solution.py:30
  52.4 0.1 pad_maximum_fusion
  52.6 2.4 %collective-permute-start.11 = (bf16[3,68,3584]{2,1,0:T(8,128)(2,1)S(1)}, bf16[3,68,3584]{2,1,0:T(8,128)(2,1)S(1)}, u32[]{:S(2)}, u32[]{:S(2)}) collective-permute-start(bf16[3,68,3584]{2,1,0:T(8,128)(2,1)S(1)} %pad_maximum_fusion), channel_id=1, source_target_pairs={{0,1},{1,0},{2,3},{3,2},{4,5},{5,4},{6,7},{7,6},{8,9},{9,8},{10,11... | collective-permute-start | bytes 4386824 | tf_op jit(solution)/shard_map/ppermute | solution.py:30
  55.0 3.3 %collective-permute-start.14 = (bf16[144,1792]{1,0:T(8,128)(2,1)S(1)}, bf16[144,1792]{1,0:T(8,128)(2,1)S(1)}, u32[]{:S(2)}, u32[]{:S(2)}) collective-permute-start(bf16[144,1792]{1,0:T(8,128)(2,1)S(1)} %collective-permute-done.5.refs_1_.refs_0_), channel_id=1, source_target_pairs={{0,2},{1,15},{2,4},{3,1},{4,6},{5,3},{6,8},{7,5},{8,10},{9,7},{10,... | collective-permute-start | bytes 1548296 | tf_op jit(solution)/shard_map/ppermute | solution.py:30
  58.3 0.0 collective-permute-done.13.refs_1_
  58.3 2.3 %collective-permute-start.15 = (bf16[144,1792]{1,0:T(8,128)(2,1)S(1)}, bf16[144,1792]{1,0:T(8,128)(2,1)S(1)}, u32[]{:S(2)}, u32[]{:S(2)}) collective-permute-start(bf16[144,1792]{1,0:T(8,128)(2,1)S(1)} %collective-permute-done.13.refs_1_), channel_id=1, source_target_pairs={{0,2},{1,15},{2,4},{3,1},{4,6},{5,3},{6,8},{7,5},{8,10},{9,7},{10,... | collective-permute-start | bytes 1548296 | tf_op jit(solution)/shard_map/ppermute | solution.py:30
  60.6 0.1 collective-permute-done.8.refs_1_.refs_0_
  60.7 3.6 %collective-permute-start.12 = (bf16[144,1792]{1,0:T(8,128)(2,1)S(1)}, bf16[144,1792]{1,0:T(8,128)(2,1)S(1)}, u32[]{:S(2)}, u32[]{:S(2)}) collective-permute-start(bf16[144,1792]{1,0:T(8,128)(2,1)S(1)} %collective-permute-done.8.refs_1_.refs_0_), channel_id=1, source_target_pairs={{0,2},{1,15},{2,4},{3,1},{4,6},{5,3},{6,8},{7,5},{8,10},{9,7},{10,... | collective-permute-start | bytes 1548296 | tf_op jit(solution)/shard_map/ppermute | solution.py:30
  64.3 0.0 collective-permute-done.10.refs_2_.refs_4_
  64.3 0.6 mark.7
  64.9 0.0 collective-permute-done.11.swapped_ref
  64.9 0.8 line_up.1.a_ref
  65.7 0.4 copy-done.1
  66.1 4.7 %project.3.refs_4_ = bf16[8,68,1152]{2,1,0:T(8,128)(2,1)S(1)} custom-call(s32[5]{0:T(128)S(1)} %stack.32.place_ref, bf16[640,3584]{1,0:T(8,128)(2,1)S(1)} %line_up.1.a_ref, bf16[144,3584]{1,0:T(8,128)(2,1)S(1)} %dynamic-slice_bitcast_fusion.refs_0_, bf16[288,1792]{1,0:T(8,128)(2,1)S(1)} %copy-done.1, ...), custom_call_target="tpu_custom_call" | custom-call | bytes 1024 | tf_op jit(solution)/shard_map/project/pallas_call | solution.py:162
  70.8 0.0 collective-permute-done.14.refs_2_
  70.8 2.9 %collective-permute-done.15.refs_3_ = bf16[144,1792]{1,0:T(8,128)(2,1)S(1)} collective-permute-done((bf16[144,1792]{1,0:T(8,128)(2,1)S(1)}, bf16[144,1792]{1,0:T(8,128)(2,1)S(1)}, u32[]{:S(2)}, u32[]{:S(2)}) %collective-permute-start.15) | collective-permute-done | bytes 516128 | tf_op jit(solution)/shard_map/ppermute | solution.py:30
  73.7 3.4 %project.4.refs_2_ = bf16[8,68,1152]{2,1,0:T(8,128)(2,1)S(1)} custom-call(s32[5]{0:T(128)S(1)} %stack.32.place_ref, bf16[640,3584]{1,0:T(8,128)(2,1)S(1)} %line_up.1.a_ref, bf16[144,1792]{1,0:T(8,128)(2,1)S(1)} %collective-permute-done.5.refs_1_.refs_0_, bf16[144,1792]{1,0:T(8,128)(2,1)S(1)} %collective-permute-done.13.refs_1_, ...), custom_call_target="tpu_custom_call", output_to_operand_aliasing={{}: (6, {})} | custom-call | bytes 1024 | tf_op jit(solution)/shard_map/project/pallas_call | solution.py:162
  77.1 1.8 %collective-permute-done.12.refs_1_ = bf16[144,1792]{1,0:T(8,128)(2,1)S(1)} collective-permute-done((bf16[144,1792]{1,0:T(8,128)(2,1)S(1)}, bf16[144,1792]{1,0:T(8,128)(2,1)S(1)}, u32[]{:S(2)}, u32[]{:S(2)}) %collective-permute-start.12) | collective-permute-done | bytes 516128 | tf_op jit(solution)/shard_map/ppermute | solution.py:30
  78.9 2.2 %project.5 = bf16[8,68,1152]{2,1,0:T(8,128)(2,1)S(1)} custom-call(s32[5]{0:T(128)S(1)} %stack.32.place_ref, bf16[640,3584]{1,0:T(8,128)(2,1)S(1)} %line_up.1.a_ref, bf16[144,1792]{1,0:T(8,128)(2,1)S(1)} %collective-permute-done.8.refs_1_.refs_0_, bf16[144,1792]{1,0:T(8,128)(2,1)S(1)} %collective-permute-done.12.refs_1_, ...), custom_call_target="tpu_custom_call", output_to_operand_aliasing={{}: (4, {})} | custom-call | bytes 1024 | tf_op jit(solution)/shard_map/project/pallas_call | solution.py:162
  81.1 21.8 %all_to_all.5.ref = bf16[8,68,1152]{2,1,0:T(8,128)(2,1)S(1)} all-to-all(bf16[8,68,1152]{2,1,0:T(8,128)(2,1)S(1)} %project.5), channel_id=1, replica_groups=mesh['x'=4,'z'=8,'y'=8,'core'=2] {'x','core'}, dimensions={0} | all-to-all | bytes 2506752 | tf_op jit(solution)/shard_map/all_to_all | solution.py:264
  102.9 3.2 %settle.1 = bf16[68,9216]{1,0:T(8,128)(2,1)} custom-call(s32[5]{0:T(128)S(1)} %stack.32.place_ref, bf16[8,68,1152]{2,1,0:T(8,128)(2,1)S(1)} %all_to_all.5.ref), custom_call_target="tpu_custom_call" | custom-call | bytes 1024 | tf_op jit(solution)/shard_map/settle/pallas_call | solution.py:194
  (22 shorter events, 0.2 us)
Async XLA Ops:
  0.0 1.4 %copy-start.6 = (f32[3584]{0:T(1024)S(1)}, f32[3584]{0:T(1024)}, u32[]{:S(2)}) copy-start(f32[3584]{0:T(1024)} %param.6) | copy-start | bytes 43012
  0.0 1.5 %copy-start.3 = (s32[64]{0:T(128)S(1)}, s32[64]{0:T(128)}, u32[]{:S(2)}) copy-start(s32[64]{0:T(128)} %param.8) | copy-start | bytes 772
  0.0 1.5 %copy-start.4 = (s32[64]{0:T(128)S(1)}, s32[64]{0:T(128)}, u32[]{:S(2)}) copy-start(s32[64]{0:T(128)} %param.9) | copy-start | bytes 772
  0.0 1.5 %copy-start.2 = (bf16[68,3584]{1,0:T(8,128)(2,1)S(1)}, bf16[68,3584]{1,0:T(8,128)(2,1)}, u32[]{:S(2)}) copy-start(bf16[68,3584]{1,0:T(8,128)(2,1)} %rows_ref.1) | copy-start | bytes 1462276
  2.3 16.3 %collective-permute-start = (bf16[68,3584]{1,0:T(8,128)(2,1)S(1)}, bf16[68,3584]{1,0:T(8,128)(2,1)S(1)}, u32[]{:S(2)}, u32[]{:S(2)}) collective-permute-start(bf16[68,3584]{1,0:T(8,128)(2,1)S(1)} %normalize.1), channel_id=1, source_target_pairs={{0,1},{1,0},{2,3},{3,2},{4,5},{5,4},{6,7},{7,6},{8,9},{9,8},{10,11... | collective-permute-start | bytes 1462280 | tf_op jit(solution)/shard_map/ppermute | solution.py:30
  11.1 12.8 %collective-permute-start.2 = (bf16[144,1792]{1,0:T(8,128)(2,1)S(1)}, bf16[144,1792]{1,0:T(8,128)(2,1)S(1)}, u32[]{:S(2)}, u32[]{:S(2)}) collective-permute-start(bf16[144,1792]{1,0:T(8,128)(2,1)S(1)} %get-tuple-element.22), channel_id=1, source_target_pairs={{0,16},{1,113},{16,32},{17,1},{32,48},{33,17},{48,64},{49,33},{64,... | collective-permute-start | bytes 1548296 | tf_op jit(solution)/shard_map/ppermute | solution.py:30
  16.4 11.5 %collective-permute-start.6 = (bf16[144,1792]{1,0:T(8,128)(2,1)S(1)}, bf16[144,1792]{1,0:T(8,128)(2,1)S(1)}, u32[]{:S(2)}, u32[]{:S(2)}) collective-permute-start(bf16[144,1792]{1,0:T(8,128)(2,1)S(1)} %get-tuple-element.21), channel_id=1, source_target_pairs={{0,16},{1,113},{16,32},{17,1},{32,48},{33,17},{48,64},{49,33},{64,... | collective-permute-start | bytes 1548296 | tf_op jit(solution)/shard_map/ppermute | solution.py:30
  19.5 20.9 %collective-permute-start.1 = (bf16[2,68,3584]{2,0,1:T(2,128)(2,1)S(1)}, bf16[2,68,3584]{2,0,1:T(2,128)(2,1)S(1)}, u32[]{:S(2)}, u32[]{:S(2)}) collective-permute-start(bf16[2,68,3584]{2,0,1:T(2,128)(2,1)S(1)} %copy.8), channel_id=1, source_target_pairs={{0,128},{1,385},{128,256},{129,1},{256,384},{257,129},{384,0},{385... | collective-permute-start | bytes 2924552 | tf_op jit(solution)/shard_map/ppermute | solution.py:30
  23.9 14.6 %collective-permute-start.3 = (bf16[144,1792]{1,0:T(8,128)(2,1)S(1)}, bf16[144,1792]{1,0:T(8,128)(2,1)S(1)}, u32[]{:S(2)}, u32[]{:S(2)}) collective-permute-start(bf16[144,1792]{1,0:T(8,128)(2,1)S(1)} %collective-permute-done.2.refs_0_), channel_id=1, source_target_pairs={{0,16},{1,113},{16,32},{17,1},{32,48},{33,17},{48,64},{49,33},{64,... | collective-permute-start | bytes 1548296 | tf_op jit(solution)/shard_map/ppermute | solution.py:30
  28.0 17.0 %collective-permute-start.9 = (bf16[144,1792]{1,0:T(8,128)(2,1)S(1)}, bf16[144,1792]{1,0:T(8,128)(2,1)S(1)}, u32[]{:S(2)}, u32[]{:S(2)}) collective-permute-start(bf16[144,1792]{1,0:T(8,128)(2,1)S(1)} %collective-permute-done.6), channel_id=1, source_target_pairs={{0,16},{1,113},{16,32},{17,1},{32,48},{33,17},{48,64},{49,33},{64,... | collective-permute-start | bytes 1548296 | tf_op jit(solution)/shard_map/ppermute | solution.py:30
  33.4 7.2 %copy-start = (bf16[288,1792]{1,0:T(8,128)(2,1)}, bf16[288,1792]{1,0:T(8,128)(2,1)S(1)}, u32[]{:S(2)}) copy-start(bf16[288,1792]{1,0:T(8,128)(2,1)S(1)} %constant_dynamic-update-slice_fusion.refs_1_) | copy-start | bytes 3096580
  33.4 19.0 %collective-permute-start.7 = (bf16[288,1792]{1,0:T(8,128)(2,1)S(1)}, bf16[288,1792]{1,0:T(8,128)(2,1)S(1)}, u32[]{:S(2)}, u32[]{:S(2)}) collective-permute-start(bf16[288,1792]{1,0:T(8,128)(2,1)S(1)} %constant_dynamic-update-slice_fusion.refs_1_), channel_id=1, source_target_pairs={{0,2},{1,15},{2,4},{3,1},{4,6},{5,3},{6,8},{7,5},{8,10},{9,7},{10,... | collective-permute-start | bytes 3096584 | tf_op jit(solution)/shard_map/ppermute | solution.py:30
  38.5 12.0 %collective-permute-start.5 = (bf16[144,1792]{1,0:T(8,128)(2,1)S(1)}, bf16[144,1792]{1,0:T(8,128)(2,1)S(1)}, u32[]{:S(2)}, u32[]{:S(2)}) collective-permute-start(bf16[144,1792]{1,0:T(8,128)(2,1)S(1)} %collective-permute-done.3.refs_1_), channel_id=1, source_target_pairs={{0,16},{1,113},{16,32},{17,1},{32,48},{33,17},{48,64},{49,33},{64,... | collective-permute-start | bytes 1548296 | tf_op jit(solution)/shard_map/ppermute | solution.py:30
  40.6 4.3 %copy-start.5 = (bf16[3584,288]{0,1:T(8,128)(2,1)S(1)}, bf16[3584,288]{0,1:T(8,128)(2,1)}, u32[]{:S(2)}) copy-start(bf16[3584,288]{0,1:T(8,128)(2,1)} %param.7) | copy-start | bytes 6193156
  40.6 11.8 %collective-permute-start.4 = (bf16[1,68,3584]{2,1,0:T(8,128)(2,1)S(1)}, bf16[1,68,3584]{2,1,0:T(8,128)(2,1)S(1)}, u32[]{:S(2)}, u32[]{:S(2)}) collective-permute-start(bf16[1,68,3584]{2,1,0:T(8,128)(2,1)S(1)} %slice.4), channel_id=1, source_target_pairs={{0,128},{1,385},{128,256},{129,1},{256,384},{257,129},{384,0},{385... | collective-permute-start | bytes 1462280 | tf_op jit(solution)/shard_map/ppermute | solution.py:30
  45.0 13.3 %collective-permute-start.13 = (bf16[144,1792]{1,0:T(8,128)(2,1)S(1)}, bf16[144,1792]{1,0:T(8,128)(2,1)S(1)}, u32[]{:S(2)}, u32[]{:S(2)}) collective-permute-start(bf16[144,1792]{1,0:T(8,128)(2,1)S(1)} %collective-permute-done.9), channel_id=1, source_target_pairs={{0,16},{1,113},{16,32},{17,1},{32,48},{33,17},{48,64},{49,33},{64,... | collective-permute-start | bytes 1548296 | tf_op jit(solution)/shard_map/ppermute | solution.py:30
  47.0 17.3 %collective-permute-start.10 = (bf16[288,1792]{1,0:T(8,128)(2,1)S(1)}, bf16[288,1792]{1,0:T(8,128)(2,1)S(1)}, u32[]{:S(2)}, u32[]{:S(2)}) collective-permute-start(bf16[288,1792]{1,0:T(8,128)(2,1)S(1)} %constant_dynamic-update-slice_fusion.2.refs_2_), channel_id=1, source_target_pairs={{0,2},{1,15},{2,4},{3,1},{4,6},{5,3},{6,8},{7,5},{8,10},{9,7},{10,... | collective-permute-start | bytes 3096584 | tf_op jit(solution)/shard_map/ppermute | solution.py:30
  50.5 10.2 %collective-permute-start.8 = (bf16[144,1792]{1,0:T(8,128)(2,1)S(1)}, bf16[144,1792]{1,0:T(8,128)(2,1)S(1)}, u32[]{:S(2)}, u32[]{:S(2)}) collective-permute-start(bf16[144,1792]{1,0:T(8,128)(2,1)S(1)} %collective-permute-done.5.refs_1_.refs_0_), channel_id=1, source_target_pairs={{0,16},{1,113},{16,32},{17,1},{32,48},{33,17},{48,64},{49,33},{64,... | collective-permute-start | bytes 1548296 | tf_op jit(solution)/shard_map/ppermute | solution.py:30
  52.6 12.3 %collective-permute-start.11 = (bf16[3,68,3584]{2,1,0:T(8,128)(2,1)S(1)}, bf16[3,68,3584]{2,1,0:T(8,128)(2,1)S(1)}, u32[]{:S(2)}, u32[]{:S(2)}) collective-permute-start(bf16[3,68,3584]{2,1,0:T(8,128)(2,1)S(1)} %pad_maximum_fusion), channel_id=1, source_target_pairs={{0,1},{1,0},{2,3},{3,2},{4,5},{5,4},{6,7},{7,6},{8,9},{9,8},{10,11... | collective-permute-start | bytes 4386824 | tf_op jit(solution)/shard_map/ppermute | solution.py:30
  55.0 15.8 %collective-permute-start.14 = (bf16[144,1792]{1,0:T(8,128)(2,1)S(1)}, bf16[144,1792]{1,0:T(8,128)(2,1)S(1)}, u32[]{:S(2)}, u32[]{:S(2)}) collective-permute-start(bf16[144,1792]{1,0:T(8,128)(2,1)S(1)} %collective-permute-done.5.refs_1_.refs_0_), channel_id=1, source_target_pairs={{0,2},{1,15},{2,4},{3,1},{4,6},{5,3},{6,8},{7,5},{8,10},{9,7},{10,... | collective-permute-start | bytes 1548296 | tf_op jit(solution)/shard_map/ppermute | solution.py:30
  58.3 15.4 %collective-permute-start.15 = (bf16[144,1792]{1,0:T(8,128)(2,1)S(1)}, bf16[144,1792]{1,0:T(8,128)(2,1)S(1)}, u32[]{:S(2)}, u32[]{:S(2)}) collective-permute-start(bf16[144,1792]{1,0:T(8,128)(2,1)S(1)} %collective-permute-done.13.refs_1_), channel_id=1, source_target_pairs={{0,2},{1,15},{2,4},{3,1},{4,6},{5,3},{6,8},{7,5},{8,10},{9,7},{10,... | collective-permute-start | bytes 1548296 | tf_op jit(solution)/shard_map/ppermute | solution.py:30
  60.7 18.3 %collective-permute-start.12 = (bf16[144,1792]{1,0:T(8,128)(2,1)S(1)}, bf16[144,1792]{1,0:T(8,128)(2,1)S(1)}, u32[]{:S(2)}, u32[]{:S(2)}) collective-permute-start(bf16[144,1792]{1,0:T(8,128)(2,1)S(1)} %collective-permute-done.8.refs_1_.refs_0_), channel_id=1, source_target_pairs={{0,2},{1,15},{2,4},{3,1},{4,6},{5,3},{6,8},{7,5},{8,10},{9,7},{10,... | collective-permute-start | bytes 1548296 | tf_op jit(solution)/shard_map/ppermute | solution.py:30
  64.9 1.2 %copy-start.1 = (bf16[288,1792]{1,0:T(8,128)(2,1)S(1)}, bf16[288,1792]{1,0:T(8,128)(2,1)}, u32[]{:S(2)}) copy-start(bf16[288,1792]{1,0:T(8,128)(2,1)} %copy-done) | copy-start | bytes 3096580

commit v7 on v6

--- a/solution.py
+++ b/solution.py
@@ -86,6 +86,24 @@
         cost_estimate=TINY,
         name="normalize",
     )(place, layer_rows, norm_gain.reshape(1, -1), req_len.reshape(1, -1), req_rank.reshape(1, -1))
+
+
+def pair_up(one, other):
+    rows, features = one.shape
+
+    def body(one_ref, other_ref, out):
+        out[0] = one_ref[...]
+        out[1] = other_ref[...]
+
+    return pl.pallas_call(
+        body,
+        out_shape=jax.ShapeDtypeStruct((2, rows, features), one.dtype),
+        in_specs=[pl.BlockSpec(memory_space=pltpu.VMEM)] * 2,
+        out_specs=pl.BlockSpec(memory_space=pltpu.VMEM),
+        compiler_params=pltpu.CompilerParams(vmem_limit_bytes=8 * MIB),
+        cost_estimate=TINY,
+        name="pair_up",
+    )(one, other)
 
 
 def line_up(place, pair, beside, distant, swapped):
@@ -223,7 +241,7 @@
     a.append(along_z(a[0]))
     b.append(along_z(b[0]))
     normed = normalize(place, layer_rows, after(norm_gain, a[0]), req_len, req_rank)
-    pair = jnp.stack([normed, other_core(normed)])
+    pair = pair_up(normed, other_core(normed))
     beside = along_x(pair)
 
     a.append(along_z(a[1]))

time: 107 us -> 106 us (level)
  transfers between devices with their start and end apart: 16 -> 16, of which waited for: 4 -> 2; matrix products, arithmetic and copies ran while one was open for 1% -> 1% of each run, Pallas kernels for 9% -> 10%
where the time goes in v7:
time: 106 us; the launch traced here: 105 us
  starting transfers between devices  59.1 us (56%)
  blocking collectives  22.8 us (22%)
  Pallas kernels  15.8 us (15%)
  waiting for transfers between devices  4.09 us (4%)
  local copies, waits for them, and re-layouts  2.97 us (3%)
    ppermute x16, starting transfers between devices, hop(): return lax.ppermute(value, tuple(axes), pairs)  59.1 us
    all_to_all x1, blocking collectives, shards(): received = lax.all_to_all(gate, ('x', 'core'), 0, 0, tiled=True)  22.8 us
    pallas_call x3, Pallas kernels, project(): pl.pallas_call(body, grid=(owners // per,), out_shape=jax.ShapeDtypeStruc...  10.3 us
    ppermute x16, waiting for transfers between devices, hop(): return lax.ppermute(value, tuple(axes), pairs)  4.09 us
    pallas_call x1, Pallas kernels, settle(): pl.pallas_call(body, grid=(4,), out_shape=jax.ShapeDtypeStruct((rows, 4 *...  3.22 us
  transfers between devices with their start and end apart: 16, of which 2 were waited for; matrix products, arithmetic and copies ran while one was open for 1% of the time, Pallas kernels for 10%

profile of v7, /device:TPU:1, one launch (start us, length us, event | category | flops | bytes accessed | tf_op | source)
XLA Modules:
  0.0 105.3 jit_solution(9825204166805651521)
XLA Ops:
  0.0 1.3 %dynamic-slice_bitcast_fusion.1 = (bf16[144,1792]{1,0:T(8,128)(2,1)S(1)}, bf16[144,1792]{1,0:T(8,128)(2,1)S(1)}) fusion(bf16[3584,288]{0,1:T(8,128)(2,1)} %param.7, s32[]{:T(128)S(6)} %select_n.11, s32[]{:T(128)S(6)} %select_n.13, s32[]{:T(128)S(6)} %select_n.12), kind=kLoop, calls=%fused_computation.2 | loop fusion | bytes 2064396 | tf_op jit(solution)/shard_map/dynamic_slice | solution.py:238
  1.4 11.5 %collective-permute-start.2 = (bf16[144,1792]{1,0:T(8,128)(2,1)S(1)}, bf16[144,1792]{1,0:T(8,128)(2,1)S(1)}, u32[]{:S(2)}, u32[]{:S(2)}) collective-permute-start(bf16[144,1792]{1,0:T(8,128)(2,1)S(1)} %get-tuple-element.22), channel_id=1, source_target_pairs={{0,16},{1,113},{16,32},{17,1},{32,48},{33,17},{48,64},{49,33},{64,... | collective-permute-start | bytes 1548296 | tf_op jit(solution)/shard_map/ppermute | solution.py:30
  12.9 0.1 stack.23.place_ref
  13.0 0.8 normalize.1.one_ref
  13.8 1.9 %collective-permute-start = (bf16[68,3584]{1,0:T(8,128)(2,1)S(1)}, bf16[68,3584]{1,0:T(8,128)(2,1)S(1)}, u32[]{:S(2)}, u32[]{:S(2)}) collective-permute-start(bf16[68,3584]{1,0:T(8,128)(2,1)S(1)} %normalize.1.one_ref), channel_id=1, source_target_pairs={{0,1},{1,0},{2,3},{3,2},{4,5},{5,4},{6,7},{7,6},{8,9},{9,8},{10,11... | collective-permute-start | bytes 1462280 | tf_op jit(solution)/shard_map/ppermute | solution.py:30
  15.8 2.6 %collective-permute-start.6 = (bf16[144,1792]{1,0:T(8,128)(2,1)S(1)}, bf16[144,1792]{1,0:T(8,128)(2,1)S(1)}, u32[]{:S(2)}, u32[]{:S(2)}) collective-permute-start(bf16[144,1792]{1,0:T(8,128)(2,1)S(1)} %get-tuple-element.21), channel_id=1, source_target_pairs={{0,16},{1,113},{16,32},{17,1},{32,48},{33,17},{48,64},{49,33},{64,... | collective-permute-start | bytes 1548296 | tf_op jit(solution)/shard_map/ppermute | solution.py:30
  18.4 0.0 collective-permute-done.other_ref
  18.4 0.1 pair_up.1.pair_ref
  18.5 0.8 copy.8
  19.2 4.4 %collective-permute-start.1 = (bf16[2,68,3584]{2,0,1:T(2,128)(2,1)S(1)}, bf16[2,68,3584]{2,0,1:T(2,128)(2,1)S(1)}, u32[]{:S(2)}, u32[]{:S(2)}) collective-permute-start(bf16[2,68,3584]{2,0,1:T(2,128)(2,1)S(1)} %copy.8), channel_id=1, source_target_pairs={{0,128},{1,385},{128,256},{129,1},{256,384},{257,129},{384,0},{385... | collective-permute-start | bytes 2924552 | tf_op jit(solution)/shard_map/ppermute | solution.py:30
  23.6 0.0 collective-permute-done.2.refs_0_
  23.6 3.6 %collective-permute-start.3 = (bf16[144,1792]{1,0:T(8,128)(2,1)S(1)}, bf16[144,1792]{1,0:T(8,128)(2,1)S(1)}, u32[]{:S(2)}, u32[]{:S(2)}) collective-permute-start(bf16[144,1792]{1,0:T(8,128)(2,1)S(1)} %collective-permute-done.2.refs_0_), channel_id=1, source_target_pairs={{0,16},{1,113},{16,32},{17,1},{32,48},{33,17},{48,64},{49,33},{64,... | collective-permute-start | bytes 1548296 | tf_op jit(solution)/shard_map/ppermute | solution.py:30
  27.3 0.0 collective-permute-done.6
  27.3 2.2 %collective-permute-start.9 = (bf16[144,1792]{1,0:T(8,128)(2,1)S(1)}, bf16[144,1792]{1,0:T(8,128)(2,1)S(1)}, u32[]{:S(2)}, u32[]{:S(2)}) collective-permute-start(bf16[144,1792]{1,0:T(8,128)(2,1)S(1)} %collective-permute-done.6), channel_id=1, source_target_pairs={{0,16},{1,113},{16,32},{17,1},{32,48},{33,17},{48,64},{49,33},{64,... | collective-permute-start | bytes 1548296 | tf_op jit(solution)/shard_map/ppermute | solution.py:30
  29.6 0.0 copy-start
  29.6 5.1 %collective-permute-start.7 = (bf16[288,1792]{1,0:T(8,128)(2,1)S(1)}, bf16[288,1792]{1,0:T(8,128)(2,1)S(1)}, u32[]{:S(2)}, u32[]{:S(2)}) collective-permute-start(bf16[288,1792]{1,0:T(8,128)(2,1)S(1)} %constant_dynamic-update-slice_fusion.refs_1_), channel_id=1, source_target_pairs={{0,2},{1,15},{2,4},{3,1},{4,6},{5,3},{6,8},{7,5},{8,10},{9,7},{10,... | collective-permute-start | bytes 3096584 | tf_op jit(solution)/shard_map/ppermute | solution.py:30
  34.7 0.0 collective-permute-done.3.refs_1_
  34.7 3.9 %collective-permute-start.5 = (bf16[144,1792]{1,0:T(8,128)(2,1)S(1)}, bf16[144,1792]{1,0:T(8,128)(2,1)S(1)}, u32[]{:S(2)}, u32[]{:S(2)}) collective-permute-start(bf16[144,1792]{1,0:T(8,128)(2,1)S(1)} %collective-permute-done.3.refs_1_), channel_id=1, source_target_pairs={{0,16},{1,113},{16,32},{17,1},{32,48},{33,17},{48,64},{49,33},{64,... | collective-permute-start | bytes 1548296 | tf_op jit(solution)/shard_map/ppermute | solution.py:30
  38.6 0.0 collective-permute-done.1
  38.6 0.1 copy.12.refs_2_.beside_ref
  38.7 0.0 copy-start.5
  38.8 3.3 %collective-permute-start.4 = (bf16[1,68,3584]{2,1,0:T(8,128)(2,1)S(1)}, bf16[1,68,3584]{2,1,0:T(8,128)(2,1)S(1)}, u32[]{:S(2)}, u32[]{:S(2)}) collective-permute-start(bf16[1,68,3584]{2,1,0:T(8,128)(2,1)S(1)} %slice.4), channel_id=1, source_target_pairs={{0,128},{1,385},{128,256},{129,1},{256,384},{257,129},{384,0},{385... | collective-permute-start | bytes 1462280 | tf_op jit(solution)/shard_map/ppermute | solution.py:30
  42.1 0.1 dynamic-slice_bitcast_fusion.refs_0_
  42.2 0.0 collective-permute-done.9
  42.2 2.2 %collective-permute-start.13 = (bf16[144,1792]{1,0:T(8,128)(2,1)S(1)}, bf16[144,1792]{1,0:T(8,128)(2,1)S(1)}, u32[]{:S(2)}, u32[]{:S(2)}) collective-permute-start(bf16[144,1792]{1,0:T(8,128)(2,1)S(1)} %collective-permute-done.9), channel_id=1, source_target_pairs={{0,16},{1,113},{16,32},{17,1},{32,48},{33,17},{48,64},{49,33},{64,... | collective-permute-start | bytes 1548296 | tf_op jit(solution)/shard_map/ppermute | solution.py:30
  44.5 4.5 %collective-permute-start.10 = (bf16[288,1792]{1,0:T(8,128)(2,1)S(1)}, bf16[288,1792]{1,0:T(8,128)(2,1)S(1)}, u32[]{:S(2)}, u32[]{:S(2)}) collective-permute-start(bf16[288,1792]{1,0:T(8,128)(2,1)S(1)} %constant_dynamic-update-slice_fusion.2.refs_2_), channel_id=1, source_target_pairs={{0,2},{1,15},{2,4},{3,1},{4,6},{5,3},{6,8},{7,5},{8,10},{9,7},{10,... | collective-permute-start | bytes 3096584 | tf_op jit(solution)/shard_map/ppermute | solution.py:30
  49.0 0.0 collective-permute-done.5.refs_1_.refs_0_
  49.0 2.0 %collective-permute-start.8 = (bf16[144,1792]{1,0:T(8,128)(2,1)S(1)}, bf16[144,1792]{1,0:T(8,128)(2,1)S(1)}, u32[]{:S(2)}, u32[]{:S(2)}) collective-permute-start(bf16[144,1792]{1,0:T(8,128)(2,1)S(1)} %collective-permute-done.5.refs_1_.refs_0_), channel_id=1, source_target_pairs={{0,16},{1,113},{16,32},{17,1},{32,48},{33,17},{48,64},{49,33},{64,... | collective-permute-start | bytes 1548296 | tf_op jit(solution)/shard_map/ppermute | solution.py:30
  51.0 0.0 collective-permute-done.7.refs_3_
  51.0 0.0 collective-permute-done.4.refs_2_.distant_ref
  51.1 0.1 pad_maximum_fusion
  51.2 1.9 %collective-permute-start.11 = (bf16[3,68,3584]{2,1,0:T(8,128)(2,1)S(1)}, bf16[3,68,3584]{2,1,0:T(8,128)(2,1)S(1)}, u32[]{:S(2)}, u32[]{:S(2)}) collective-permute-start(bf16[3,68,3584]{2,1,0:T(8,128)(2,1)S(1)} %pad_maximum_fusion), channel_id=1, source_target_pairs={{0,1},{1,0},{2,3},{3,2},{4,5},{5,4},{6,7},{7,6},{8,9},{9,8},{10,11... | collective-permute-start | bytes 4386824 | tf_op jit(solution)/shard_map/ppermute | solution.py:30
  53.2 4.0 %collective-permute-start.14 = (bf16[144,1792]{1,0:T(8,128)(2,1)S(1)}, bf16[144,1792]{1,0:T(8,128)(2,1)S(1)}, u32[]{:S(2)}, u32[]{:S(2)}) collective-permute-start(bf16[144,1792]{1,0:T(8,128)(2,1)S(1)} %collective-permute-done.5.refs_1_.refs_0_), channel_id=1, source_target_pairs={{0,2},{1,15},{2,4},{3,1},{4,6},{5,3},{6,8},{7,5},{8,10},{9,7},{10,... | collective-permute-start | bytes 1548296 | tf_op jit(solution)/shard_map/ppermute | solution.py:30
  57.2 0.0 collective-permute-done.13.refs_1_
  57.2 3.0 %collective-permute-start.15 = (bf16[144,1792]{1,0:T(8,128)(2,1)S(1)}, bf16[144,1792]{1,0:T(8,128)(2,1)S(1)}, u32[]{:S(2)}, u32[]{:S(2)}) collective-permute-start(bf16[144,1792]{1,0:T(8,128)(2,1)S(1)} %collective-permute-done.13.refs_1_), channel_id=1, source_target_pairs={{0,2},{1,15},{2,4},{3,1},{4,6},{5,3},{6,8},{7,5},{8,10},{9,7},{10,... | collective-permute-start | bytes 1548296 | tf_op jit(solution)/shard_map/ppermute | solution.py:30
  60.2 0.0 collective-permute-done.8.refs_1_.refs_0_
  60.2 3.0 %collective-permute-start.12 = (bf16[144,1792]{1,0:T(8,128)(2,1)S(1)}, bf16[144,1792]{1,0:T(8,128)(2,1)S(1)}, u32[]{:S(2)}, u32[]{:S(2)}) collective-permute-start(bf16[144,1792]{1,0:T(8,128)(2,1)S(1)} %collective-permute-done.8.refs_1_.refs_0_), channel_id=1, source_target_pairs={{0,2},{1,15},{2,4},{3,1},{4,6},{5,3},{6,8},{7,5},{8,10},{9,7},{10,... | collective-permute-start | bytes 1548296 | tf_op jit(solution)/shard_map/ppermute | solution.py:30
  63.2 0.6 mark.7
  63.7 0.0 collective-permute-done.11.swapped_ref
  63.7 0.8 line_up.1.a_ref
  64.6 0.4 copy-done.1
  65.0 4.7 %project.3.refs_4_ = bf16[8,68,1152]{2,1,0:T(8,128)(2,1)S(1)} custom-call(s32[5]{0:T(128)S(1)} %stack.23.place_ref, bf16[640,3584]{1,0:T(8,128)(2,1)S(1)} %line_up.1.a_ref, bf16[144,3584]{1,0:T(8,128)(2,1)S(1)} %dynamic-slice_bitcast_fusion.refs_0_, bf16[288,1792]{1,0:T(8,128)(2,1)S(1)} %copy-done.1, ...), custom_call_target="tpu_custom_call" | custom-call | bytes 1024 | tf_op jit(solution)/shard_map/project/pallas_call | solution.py:180
  69.7 1.9 %collective-permute-done.15.refs_3_ = bf16[144,1792]{1,0:T(8,128)(2,1)S(1)} collective-permute-done((bf16[144,1792]{1,0:T(8,128)(2,1)S(1)}, bf16[144,1792]{1,0:T(8,128)(2,1)S(1)}, u32[]{:S(2)}, u32[]{:S(2)}) %collective-permute-start.15) | collective-permute-done | bytes 516128 | tf_op jit(solution)/shard_map/ppermute | solution.py:30
  71.6 3.4 %project.4.refs_2_ = bf16[8,68,1152]{2,1,0:T(8,128)(2,1)S(1)} custom-call(s32[5]{0:T(128)S(1)} %stack.23.place_ref, bf16[640,3584]{1,0:T(8,128)(2,1)S(1)} %line_up.1.a_ref, bf16[144,1792]{1,0:T(8,128)(2,1)S(1)} %collective-permute-done.5.refs_1_.refs_0_, bf16[144,1792]{1,0:T(8,128)(2,1)S(1)} %collective-permute-done.13.refs_1_, ...), custom_call_target="tpu_custom_call", output_to_operand_aliasing={{}: (6, {})} | custom-call | bytes 1024 | tf_op jit(solution)/shard_map/project/pallas_call | solution.py:180
  75.0 2.1 %collective-permute-done.12.refs_1_ = bf16[144,1792]{1,0:T(8,128)(2,1)S(1)} collective-permute-done((bf16[144,1792]{1,0:T(8,128)(2,1)S(1)}, bf16[144,1792]{1,0:T(8,128)(2,1)S(1)}, u32[]{:S(2)}, u32[]{:S(2)}) %collective-permute-start.12) | collective-permute-done | bytes 516128 | tf_op jit(solution)/shard_map/ppermute | solution.py:30
  77.1 2.2 %project.5 = bf16[8,68,1152]{2,1,0:T(8,128)(2,1)S(1)} custom-call(s32[5]{0:T(128)S(1)} %stack.23.place_ref, bf16[640,3584]{1,0:T(8,128)(2,1)S(1)} %line_up.1.a_ref, bf16[144,1792]{1,0:T(8,128)(2,1)S(1)} %collective-permute-done.8.refs_1_.refs_0_, bf16[144,1792]{1,0:T(8,128)(2,1)S(1)} %collective-permute-done.12.refs_1_, ...), custom_call_target="tpu_custom_call", output_to_operand_aliasing={{}: (4, {})} | custom-call | bytes 1024 | tf_op jit(solution)/shard_map/project/pallas_call | solution.py:180
  79.3 22.8 %all_to_all.5.ref = bf16[8,68,1152]{2,1,0:T(8,128)(2,1)S(1)} all-to-all(bf16[8,68,1152]{2,1,0:T(8,128)(2,1)S(1)} %project.5), channel_id=1, replica_groups=mesh['x'=4,'z'=8,'y'=8,'core'=2] {'x','core'}, dimensions={0} | all-to-all | bytes 2506752 | tf_op jit(solution)/shard_map/all_to_all | solution.py:282
  102.1 3.2 %settle.1 = bf16[68,9216]{1,0:T(8,128)(2,1)} custom-call(s32[5]{0:T(128)S(1)} %stack.23.place_ref, bf16[8,68,1152]{2,1,0:T(8,128)(2,1)S(1)} %all_to_all.5.ref), custom_call_target="tpu_custom_call" | custom-call | bytes 1024 | tf_op jit(solution)/shard_map/settle/pallas_call | solution.py:212
  (22 shorter events, 0.2 us)
Async XLA Ops:
  0.0 12.9 %copy-start.6 = (f32[3584]{0:T(1024)S(1)}, f32[3584]{0:T(1024)}, u32[]{:S(2)}) copy-start(f32[3584]{0:T(1024)} %param.6) | copy-start | bytes 43012
  0.0 13.0 %copy-start.3 = (s32[64]{0:T(128)S(1)}, s32[64]{0:T(128)}, u32[]{:S(2)}) copy-start(s32[64]{0:T(128)} %param.8) | copy-start | bytes 772
  0.0 13.0 %copy-start.4 = (s32[64]{0:T(128)S(1)}, s32[64]{0:T(128)}, u32[]{:S(2)}) copy-start(s32[64]{0:T(128)} %param.9) | copy-start | bytes 772
  0.0 13.0 %copy-start.2 = (bf16[68,3584]{1,0:T(8,128)(2,1)S(1)}, bf16[68,3584]{1,0:T(8,128)(2,1)}, u32[]{:S(2)}) copy-start(bf16[68,3584]{1,0:T(8,128)(2,1)} %rows_ref.1) | copy-start | bytes 1462276
  1.4 22.2 %collective-permute-start.2 = (bf16[144,1792]{1,0:T(8,128)(2,1)S(1)}, bf16[144,1792]{1,0:T(8,128)(2,1)S(1)}, u32[]{:S(2)}, u32[]{:S(2)}) collective-permute-start(bf16[144,1792]{1,0:T(8,128)(2,1)S(1)} %get-tuple-element.22), channel_id=1, source_target_pairs={{0,16},{1,113},{16,32},{17,1},{32,48},{33,17},{48,64},{49,33},{64,... | collective-permute-start | bytes 1548296 | tf_op jit(solution)/shard_map/ppermute | solution.py:30
  13.8 4.5 %collective-permute-start = (bf16[68,3584]{1,0:T(8,128)(2,1)S(1)}, bf16[68,3584]{1,0:T(8,128)(2,1)S(1)}, u32[]{:S(2)}, u32[]{:S(2)}) collective-permute-start(bf16[68,3584]{1,0:T(8,128)(2,1)S(1)} %normalize.1.one_ref), channel_id=1, source_target_pairs={{0,1},{1,0},{2,3},{3,2},{4,5},{5,4},{6,7},{7,6},{8,9},{9,8},{10,11... | collective-permute-start | bytes 1462280 | tf_op jit(solution)/shard_map/ppermute | solution.py:30
  15.8 11.5 %collective-permute-start.6 = (bf16[144,1792]{1,0:T(8,128)(2,1)S(1)}, bf16[144,1792]{1,0:T(8,128)(2,1)S(1)}, u32[]{:S(2)}, u32[]{:S(2)}) collective-permute-start(bf16[144,1792]{1,0:T(8,128)(2,1)S(1)} %get-tuple-element.21), channel_id=1, source_target_pairs={{0,16},{1,113},{16,32},{17,1},{32,48},{33,17},{48,64},{49,33},{64,... | collective-permute-start | bytes 1548296 | tf_op jit(solution)/shard_map/ppermute | solution.py:30
  19.2 19.4 %collective-permute-start.1 = (bf16[2,68,3584]{2,0,1:T(2,128)(2,1)S(1)}, bf16[2,68,3584]{2,0,1:T(2,128)(2,1)S(1)}, u32[]{:S(2)}, u32[]{:S(2)}) collective-permute-start(bf16[2,68,3584]{2,0,1:T(2,128)(2,1)S(1)} %copy.8), channel_id=1, source_target_pairs={{0,128},{1,385},{128,256},{129,1},{256,384},{257,129},{384,0},{385... | collective-permute-start | bytes 2924552 | tf_op jit(solution)/shard_map/ppermute | solution.py:30
  23.6 11.1 %collective-permute-start.3 = (bf16[144,1792]{1,0:T(8,128)(2,1)S(1)}, bf16[144,1792]{1,0:T(8,128)(2,1)S(1)}, u32[]{:S(2)}, u32[]{:S(2)}) collective-permute-start(bf16[144,1792]{1,0:T(8,128)(2,1)S(1)} %collective-permute-done.2.refs_0_), channel_id=1, source_target_pairs={{0,16},{1,113},{16,32},{17,1},{32,48},{33,17},{48,64},{49,33},{64,... | collective-permute-start | bytes 1548296 | tf_op jit(solution)/shard_map/ppermute | solution.py:30
  27.3 14.9 %collective-permute-start.9 = (bf16[144,1792]{1,0:T(8,128)(2,1)S(1)}, bf16[144,1792]{1,0:T(8,128)(2,1)S(1)}, u32[]{:S(2)}, u32[]{:S(2)}) collective-permute-start(bf16[144,1792]{1,0:T(8,128)(2,1)S(1)} %collective-permute-done.6), channel_id=1, source_target_pairs={{0,16},{1,113},{16,32},{17,1},{32,48},{33,17},{48,64},{49,33},{64,... | collective-permute-start | bytes 1548296 | tf_op jit(solution)/shard_map/ppermute | solution.py:30
  29.6 9.2 %copy-start = (bf16[288,1792]{1,0:T(8,128)(2,1)}, bf16[288,1792]{1,0:T(8,128)(2,1)S(1)}, u32[]{:S(2)}) copy-start(bf16[288,1792]{1,0:T(8,128)(2,1)S(1)} %constant_dynamic-update-slice_fusion.refs_1_) | copy-start | bytes 3096580
  29.6 21.5 %collective-permute-start.7 = (bf16[288,1792]{1,0:T(8,128)(2,1)S(1)}, bf16[288,1792]{1,0:T(8,128)(2,1)S(1)}, u32[]{:S(2)}, u32[]{:S(2)}) collective-permute-start(bf16[288,1792]{1,0:T(8,128)(2,1)S(1)} %constant_dynamic-update-slice_fusion.refs_1_), channel_id=1, source_target_pairs={{0,2},{1,15},{2,4},{3,1},{4,6},{5,3},{6,8},{7,5},{8,10},{9,7},{10,... | collective-permute-start | bytes 3096584 | tf_op jit(solution)/shard_map/ppermute | solution.py:30
  34.7 14.3 %collective-permute-start.5 = (bf16[144,1792]{1,0:T(8,128)(2,1)S(1)}, bf16[144,1792]{1,0:T(8,128)(2,1)S(1)}, u32[]{:S(2)}, u32[]{:S(2)}) collective-permute-start(bf16[144,1792]{1,0:T(8,128)(2,1)S(1)} %collective-permute-done.3.refs_1_), channel_id=1, source_target_pairs={{0,16},{1,113},{16,32},{17,1},{32,48},{33,17},{48,64},{49,33},{64,... | collective-permute-start | bytes 1548296 | tf_op jit(solution)/shard_map/ppermute | solution.py:30
  38.7 3.4 %copy-start.5 = (bf16[3584,288]{0,1:T(8,128)(2,1)S(1)}, bf16[3584,288]{0,1:T(8,128)(2,1)}, u32[]{:S(2)}) copy-start(bf16[3584,288]{0,1:T(8,128)(2,1)} %param.7) | copy-start | bytes 6193156
  38.8 12.2 %collective-permute-start.4 = (bf16[1,68,3584]{2,1,0:T(8,128)(2,1)S(1)}, bf16[1,68,3584]{2,1,0:T(8,128)(2,1)S(1)}, u32[]{:S(2)}, u32[]{:S(2)}) collective-permute-start(bf16[1,68,3584]{2,1,0:T(8,128)(2,1)S(1)} %slice.4), channel_id=1, source_target_pairs={{0,128},{1,385},{128,256},{129,1},{256,384},{257,129},{384,0},{385... | collective-permute-start | bytes 1462280 | tf_op jit(solution)/shard_map/ppermute | solution.py:30
  42.2 14.9 %collective-permute-start.13 = (bf16[144,1792]{1,0:T(8,128)(2,1)S(1)}, bf16[144,1792]{1,0:T(8,128)(2,1)S(1)}, u32[]{:S(2)}, u32[]{:S(2)}) collective-permute-start(bf16[144,1792]{1,0:T(8,128)(2,1)S(1)} %collective-permute-done.9), channel_id=1, source_target_pairs={{0,16},{1,113},{16,32},{17,1},{32,48},{33,17},{48,64},{49,33},{64,... | collective-permute-start | bytes 1548296 | tf_op jit(solution)/shard_map/ppermute | solution.py:30
  44.5 18.7 %collective-permute-start.10 = (bf16[288,1792]{1,0:T(8,128)(2,1)S(1)}, bf16[288,1792]{1,0:T(8,128)(2,1)S(1)}, u32[]{:S(2)}, u32[]{:S(2)}) collective-permute-start(bf16[288,1792]{1,0:T(8,128)(2,1)S(1)} %constant_dynamic-update-slice_fusion.2.refs_2_), channel_id=1, source_target_pairs={{0,2},{1,15},{2,4},{3,1},{4,6},{5,3},{6,8},{7,5},{8,10},{9,7},{10,... | collective-permute-start | bytes 3096584 | tf_op jit(solution)/shard_map/ppermute | solution.py:30
  49.0 11.2 %collective-permute-start.8 = (bf16[144,1792]{1,0:T(8,128)(2,1)S(1)}, bf16[144,1792]{1,0:T(8,128)(2,1)S(1)}, u32[]{:S(2)}, u32[]{:S(2)}) collective-permute-start(bf16[144,1792]{1,0:T(8,128)(2,1)S(1)} %collective-permute-done.5.refs_1_.refs_0_), channel_id=1, source_target_pairs={{0,16},{1,113},{16,32},{17,1},{32,48},{33,17},{48,64},{49,33},{64,... | collective-permute-start | bytes 1548296 | tf_op jit(solution)/shard_map/ppermute | solution.py:30
  51.2 12.5 %collective-permute-start.11 = (bf16[3,68,3584]{2,1,0:T(8,128)(2,1)S(1)}, bf16[3,68,3584]{2,1,0:T(8,128)(2,1)S(1)}, u32[]{:S(2)}, u32[]{:S(2)}) collective-permute-start(bf16[3,68,3584]{2,1,0:T(8,128)(2,1)S(1)} %pad_maximum_fusion), channel_id=1, source_target_pairs={{0,1},{1,0},{2,3},{3,2},{4,5},{5,4},{6,7},{7,6},{8,9},{9,8},{10,11... | collective-permute-start | bytes 4386824 | tf_op jit(solution)/shard_map/ppermute | solution.py:30
  53.2 16.5 %collective-permute-start.14 = (bf16[144,1792]{1,0:T(8,128)(2,1)S(1)}, bf16[144,1792]{1,0:T(8,128)(2,1)S(1)}, u32[]{:S(2)}, u32[]{:S(2)}) collective-permute-start(bf16[144,1792]{1,0:T(8,128)(2,1)S(1)} %collective-permute-done.5.refs_1_.refs_0_), channel_id=1, source_target_pairs={{0,2},{1,15},{2,4},{3,1},{4,6},{5,3},{6,8},{7,5},{8,10},{9,7},{10,... | collective-permute-start | bytes 1548296 | tf_op jit(solution)/shard_map/ppermute | solution.py:30
  57.2 14.4 %collective-permute-start.15 = (bf16[144,1792]{1,0:T(8,128)(2,1)S(1)}, bf16[144,1792]{1,0:T(8,128)(2,1)S(1)}, u32[]{:S(2)}, u32[]{:S(2)}) collective-permute-start(bf16[144,1792]{1,0:T(8,128)(2,1)S(1)} %collective-permute-done.13.refs_1_), channel_id=1, source_target_pairs={{0,2},{1,15},{2,4},{3,1},{4,6},{5,3},{6,8},{7,5},{8,10},{9,7},{10,... | collective-permute-start | bytes 1548296 | tf_op jit(solution)/shard_map/ppermute | solution.py:30
  60.2 17.0 %collective-permute-start.12 = (bf16[144,1792]{1,0:T(8,128)(2,1)S(1)}, bf16[144,1792]{1,0:T(8,128)(2,1)S(1)}, u32[]{:S(2)}, u32[]{:S(2)}) collective-permute-start(bf16[144,1792]{1,0:T(8,128)(2,1)S(1)} %collective-permute-done.8.refs_1_.refs_0_), channel_id=1, source_target_pairs={{0,2},{1,15},{2,4},{3,1},{4,6},{5,3},{6,8},{7,5},{8,10},{9,7},{10,... | collective-permute-start | bytes 1548296 | tf_op jit(solution)/shard_map/ppermute | solution.py:30
  63.7 1.2 %copy-start.1 = (bf16[288,1792]{1,0:T(8,128)(2,1)S(1)}, bf16[288,1792]{1,0:T(8,128)(2,1)}, u32[]{:S(2)}) copy-start(bf16[288,1792]{1,0:T(8,128)(2,1)} %copy-done) | copy-start | bytes 3096580

commit v8 on v7

--- a/solution.py
+++ b/solution.py
@@ -60,7 +60,7 @@
         in_specs=[pl.BlockSpec(memory_space=pltpu.VMEM)] * len(seen),
         out_specs=pl.BlockSpec(memory_space=pltpu.VMEM),
         compiler_params=pltpu.CompilerParams(has_side_effects=True, vmem_limit_bytes=8 * MIB),
-        cost_estimate=pl.CostEstimate(flops=10**11, bytes_accessed=1024, transcendentals=0),
+        cost_estimate=pl.CostEstimate(flops=int(2e10), bytes_accessed=1024, transcendentals=0),
         name="mark",
     )(*seen)
 
@@ -255,9 +255,10 @@
     point = mark(point, a[2], beside)
     distant = along_x(after(beside[:1], point))
     b[2] = after(b[2], point)
-    b.append(along_z(b[2]))
     near.append(jnp.concatenate([a[2], b[2]], 0))
     far.append(along_y(near[1]))
+    point = mark(point, b[2][:16, :128])
+    b.append(along_z(after(b[2], point)))
 
     a.append(along_z(a[3]))
     point = mark(point, a[3], distant, far[0])
@@ -270,7 +271,8 @@
     point = mark(point, a[4], far[1])
     rows_in = line_up(place, pair, beside, after(distant, point), swapped)
 
-    own_half = lax.dynamic_slice(weights, (c * half_width, 0), (half_width, features))
+    later = point[0, 0].astype(jnp.int32)
+    own_half = lax.dynamic_slice(weights, (c * half_width + later, 0), (half_width, features))
     columns = 4 * width
     begin = half_width * 3 // 128 * 128
     gate = project(

time: 106 us -> 112 us (1.057)
  Pallas kernels: 15.8 us -> 20.6 us
  waiting for transfers between devices: 4.09 us -> 0.04 us
  local copies, waits for them, and re-layouts: 2.97 us -> 5.91 us
  other arithmetic: 0.15 us -> 1.28 us
    ppermute x16, waiting for transfers between devices: 4.09 us -> 0.04 us  [hop(): return lax.ppermute(value, tuple(axes), pairs)]
    pallas_call x4 -> x5, Pallas kernels: 0.59 us -> 2.65 us  [mark(): pl.pallas_call(body, out_shape=jax.ShapeDtypeStruct((8, 128), jnp.float32...]
    pallas_call x3, Pallas kernels: 10.3 us -> 12 us  [project(): pl.pallas_call(body, grid=(owners // per,), out_shape=jax.ShapeDtypeStruc...]
    dynamic_slice x1, local copies, waits for them, and re-layouts: 0.08 us -> 1.52 us  [shards(): lax.dynamic_slice(weights, (c * half_width + later, 0), (half_width, feat...]
    concatenate x1, other arithmetic: 0.15 us -> 1.28 us  [shards(): swapped = other_core(after(jnp.concatenate([beside, distant], 0), point))]
  transfers between devices with their start and end apart: 16 -> 16, of which waited for: 2 -> 0; matrix products, arithmetic and copies ran while one was open for 1% -> 4% of each run, Pallas kernels for 10% -> 13%
where the time goes in v8:
time: 112 us; the launch traced here: 111 us
  starting transfers between devices  59.2 us (53%)
  blocking collectives  22.8 us (20%)
  Pallas kernels  20.6 us (18%)
  local copies, waits for them, and re-layouts  5.91 us (5%)
  other arithmetic  1.28 us (1%)
  between operations  1.17 us (1%)
    ppermute x16, starting transfers between devices, hop(): return lax.ppermute(value, tuple(axes), pairs)  59.2 us
    all_to_all x1, blocking collectives, shards(): received = lax.all_to_all(gate, ('x', 'core'), 0, 0, tiled=True)  22.8 us
    pallas_call x3, Pallas kernels, project(): pl.pallas_call(body, grid=(owners // per,), out_shape=jax.ShapeDtypeStruc...  12 us
    pallas_call x1, Pallas kernels, settle(): pl.pallas_call(body, grid=(4,), out_shape=jax.ShapeDtypeStruct((rows, 4 *...  3.22 us
    pallas_call x5, Pallas kernels, mark(): pl.pallas_call(body, out_shape=jax.ShapeDtypeStruct((8, 128), jnp.float32...  2.65 us
  transfers between devices with their start and end apart: 16, of which 0 were waited for; matrix products, arithmetic and copies ran while one was open for 4% of the time, Pallas kernels for 13%

profile of v8, /device:TPU:1, one launch (start us, length us, event | category | flops | bytes accessed | tf_op | source)
XLA Modules:
  0.0 110.9 jit_solution(10808392602603358273)
XLA Ops:
  0.0 1.3 %dynamic-slice_bitcast_fusion.1 = (bf16[144,1792]{1,0:T(8,128)(2,1)S(1)}, bf16[144,1792]{1,0:T(8,128)(2,1)S(1)}) fusion(bf16[3584,288]{0,1:T(8,128)(2,1)} %param.7, s32[]{:T(128)S(6)} %select_n.13, s32[]{:T(128)S(6)} %select_n.15, s32[]{:T(128)S(6)} %select_n.14), kind=kLoop, calls=%fused_computation.2 | loop fusion | bytes 2064396 | tf_op jit(solution)/shard_map/dynamic_slice | solution.py:238
  1.4 11.5 %collective-permute-start.2 = (bf16[144,1792]{1,0:T(8,128)(2,1)S(1)}, bf16[144,1792]{1,0:T(8,128)(2,1)S(1)}, u32[]{:S(2)}, u32[]{:S(2)}) collective-permute-start(bf16[144,1792]{1,0:T(8,128)(2,1)S(1)} %get-tuple-element.24), channel_id=1, source_target_pairs={{0,16},{1,113},{16,32},{17,1},{32,48},{33,17},{48,64},{49,33},{64,... | collective-permute-start | bytes 1548296 | tf_op jit(solution)/shard_map/ppermute | solution.py:30
  12.9 0.1 stack.23.place_ref
  13.0 0.8 normalize.1.one_ref
  13.8 1.9 %collective-permute-start = (bf16[68,3584]{1,0:T(8,128)(2,1)S(1)}, bf16[68,3584]{1,0:T(8,128)(2,1)S(1)}, u32[]{:S(2)}, u32[]{:S(2)}) collective-permute-start(bf16[68,3584]{1,0:T(8,128)(2,1)S(1)} %normalize.1.one_ref), channel_id=1, source_target_pairs={{0,1},{1,0},{2,3},{3,2},{4,5},{5,4},{6,7},{7,6},{8,9},{9,8},{10,11... | collective-permute-start | bytes 1462280 | tf_op jit(solution)/shard_map/ppermute | solution.py:30
  15.8 2.6 %collective-permute-start.5 = (bf16[144,1792]{1,0:T(8,128)(2,1)S(1)}, bf16[144,1792]{1,0:T(8,128)(2,1)S(1)}, u32[]{:S(2)}, u32[]{:S(2)}) collective-permute-start(bf16[144,1792]{1,0:T(8,128)(2,1)S(1)} %get-tuple-element.23), channel_id=1, source_target_pairs={{0,16},{1,113},{16,32},{17,1},{32,48},{33,17},{48,64},{49,33},{64,... | collective-permute-start | bytes 1548296 | tf_op jit(solution)/shard_map/ppermute | solution.py:30
  18.4 0.1 pair_up.1.pair_ref
  18.4 0.8 copy.8
  19.2 4.4 %collective-permute-start.1 = (bf16[2,68,3584]{2,0,1:T(2,128)(2,1)S(1)}, bf16[2,68,3584]{2,0,1:T(2,128)(2,1)S(1)}, u32[]{:S(2)}, u32[]{:S(2)}) collective-permute-start(bf16[2,68,3584]{2,0,1:T(2,128)(2,1)S(1)} %copy.8), channel_id=1, source_target_pairs={{0,128},{1,385},{128,256},{129,1},{256,384},{257,129},{384,0},{385... | collective-permute-start | bytes 2924552 | tf_op jit(solution)/shard_map/ppermute | solution.py:30
  23.6 0.0 collective-permute-done.2.refs_0_
  23.6 3.6 %collective-permute-start.3 = (bf16[144,1792]{1,0:T(8,128)(2,1)S(1)}, bf16[144,1792]{1,0:T(8,128)(2,1)S(1)}, u32[]{:S(2)}, u32[]{:S(2)}) collective-permute-start(bf16[144,1792]{1,0:T(8,128)(2,1)S(1)} %collective-permute-done.2.refs_0_), channel_id=1, source_target_pairs={{0,16},{1,113},{16,32},{17,1},{32,48},{33,17},{48,64},{49,33},{64,... | collective-permute-start | bytes 1548296 | tf_op jit(solution)/shard_map/ppermute | solution.py:30
  27.3 0.0 collective-permute-done.5
  27.3 2.2 %collective-permute-start.6 = (bf16[144,1792]{1,0:T(8,128)(2,1)S(1)}, bf16[144,1792]{1,0:T(8,128)(2,1)S(1)}, u32[]{:S(2)}, u32[]{:S(2)}) collective-permute-start(bf16[144,1792]{1,0:T(8,128)(2,1)S(1)} %collective-permute-done.5), channel_id=1, source_target_pairs={{0,16},{1,113},{16,32},{17,1},{32,48},{33,17},{48,64},{49,33},{64,... | collective-permute-start | bytes 1548296 | tf_op jit(solution)/shard_map/ppermute | solution.py:30
  29.6 0.0 copy-start
  29.6 5.1 %collective-permute-start.8 = (bf16[288,1792]{1,0:T(8,128)(2,1)S(1)}, bf16[288,1792]{1,0:T(8,128)(2,1)S(1)}, u32[]{:S(2)}, u32[]{:S(2)}) collective-permute-start(bf16[288,1792]{1,0:T(8,128)(2,1)S(1)} %constant_dynamic-update-slice_fusion.refs_1_), channel_id=1, source_target_pairs={{0,2},{1,15},{2,4},{3,1},{4,6},{5,3},{6,8},{7,5},{8,10},{9,7},{10,... | collective-permute-start | bytes 3096584 | tf_op jit(solution)/shard_map/ppermute | solution.py:30
  34.7 3.9 %collective-permute-start.7 = (bf16[144,1792]{1,0:T(8,128)(2,1)S(1)}, bf16[144,1792]{1,0:T(8,128)(2,1)}, u32[]{:S(2)}, u32[]{:S(2)}) collective-permute-start(bf16[144,1792]{1,0:T(8,128)(2,1)S(1)} %collective-permute-done.3.refs_1_), channel_id=1, source_target_pairs={{0,16},{1,113},{16,32},{17,1},{32,48},{33,17},{48,64},{49,33},{64,... | collective-permute-start | bytes 1548296 | tf_op jit(solution)/shard_map/ppermute | solution.py:30
  38.7 0.1 copy.12.refs_2_.beside_ref
  38.8 3.1 %collective-permute-start.4 = (bf16[1,68,3584]{2,1,0:T(8,128)(2,1)S(1)}, bf16[1,68,3584]{2,1,0:T(8,128)(2,1)S(1)}, u32[]{:S(2)}, u32[]{:S(2)}) collective-permute-start(bf16[1,68,3584]{2,1,0:T(8,128)(2,1)S(1)} %slice.12), channel_id=1, source_target_pairs={{0,128},{1,385},{128,256},{129,1},{256,384},{257,129},{384,0},{385... | collective-permute-start | bytes 1462280 | tf_op jit(solution)/shard_map/ppermute | solution.py:30
  42.0 0.0 collective-permute-done.6
  42.0 4.1 %collective-permute-start.10 = (bf16[288,1792]{1,0:T(8,128)(2,1)S(1)}, bf16[288,1792]{1,0:T(8,128)(2,1)S(1)}, u32[]{:S(2)}, u32[]{:S(2)}) collective-permute-start(bf16[288,1792]{1,0:T(8,128)(2,1)S(1)} %constant_dynamic-update-slice_fusion.2.refs_2_), channel_id=1, source_target_pairs={{0,2},{1,15},{2,4},{3,1},{4,6},{5,3},{6,8},{7,5},{8,10},{9,7},{10,... | collective-permute-start | bytes 3096584 | tf_op jit(solution)/shard_map/ppermute | solution.py:30
  46.2 2.8 %collective-permute-start.13 = (bf16[144,1792]{1,0:T(8,128)(2,1)S(1)}, bf16[144,1792]{1,0:T(8,128)(2,1)}, u32[]{:S(2)}, u32[]{:S(2)}) collective-permute-start(bf16[144,1792]{1,0:T(8,128)(2,1)S(1)} %collective-permute-done.6), channel_id=1, source_target_pairs={{0,16},{1,113},{16,32},{17,1},{32,48},{33,17},{48,64},{49,33},{64,... | collective-permute-start | bytes 1548296 | tf_op jit(solution)/shard_map/ppermute | solution.py:30
  49.0 0.0 collective-permute-done.7.refs_1_.refs_0_
  49.0 1.9 %collective-permute-start.9 = (bf16[144,1792]{1,0:T(8,128)(2,1)}, bf16[144,1792]{1,0:T(8,128)(2,1)}, u32[]{:S(2)}, u32[]{:S(2)}) collective-permute-start(bf16[144,1792]{1,0:T(8,128)(2,1)} %collective-permute-done.7.refs_1_.refs_0_), channel_id=1, source_target_pairs={{0,16},{1,113},{16,32},{17,1},{32,48},{33,17},{48,64},{49,33},{64,... | collective-permute-start | bytes 1548296 | tf_op jit(solution)/shard_map/ppermute | solution.py:30
  50.9 0.0 collective-permute-done.8.refs_3_
  51.0 1.2 %mark.8.refs_0_ = f32[8,128]{1,0:T(8,128)S(1)} custom-call(f32[8,128]{1,0:T(8,128)S(1)} %mark.7.refs_0_, bf16[144,1792]{1,0:T(8,128)(2,1)} %collective-permute-done.7.refs_1_.refs_0_, bf16[1,68,3584]{2,1,0:T(8,128)(2,1)S(1)} %collective-permute-done.4.refs_2_.distant_ref, bf16[288,1792]{1,0:T(8,128)(2,1)S(1)} %collective-permute-done.8.refs_3_), custom_call_target="tpu_custom_call" | custom-call | flops 20000000000 | bytes 1024 | tf_op jit(solution)/shard_map/mark/pallas_call | solution.py:57
  52.2 1.0 copy-done.4
  53.2 1.3 %pad_maximum_fusion = bf16[3,68,3584]{2,1,0:T(8,128)(2,1)} fusion(bf16[1,68,3584]{2,1,0:T(8,128)(2,1)S(1)} %collective-permute-done.4.refs_2_.distant_ref, bf16[2,68,3584]{2,1,0:T(8,128)(2,1)S(1)} %copy.12.refs_2_.beside_ref), kind=kLoop, calls=%fused_computation | loop fusion | flops 731136 | bytes 2924544 | tf_op jit(solution)/shard_map/concatenate | solution.py:265
  54.4 1.9 %collective-permute-start.11 = (bf16[3,68,3584]{2,1,0:T(8,128)(2,1)}, bf16[3,68,3584]{2,1,0:T(8,128)(2,1)}, u32[]{:S(2)}, u32[]{:S(2)}) collective-permute-start(bf16[3,68,3584]{2,1,0:T(8,128)(2,1)} %pad_maximum_fusion), channel_id=1, source_target_pairs={{0,1},{1,0},{2,3},{3,2},{4,5},{5,4},{6,7},{7,6},{8,9},{9,8},{10,11... | collective-permute-start | bytes 4386824 | tf_op jit(solution)/shard_map/ppermute | solution.py:30
  56.4 4.1 %collective-permute-start.14 = (bf16[144,1792]{1,0:T(8,128)(2,1)}, bf16[144,1792]{1,0:T(8,128)(2,1)}, u32[]{:S(2)}, u32[]{:S(2)}) collective-permute-start(bf16[144,1792]{1,0:T(8,128)(2,1)} %collective-permute-done.7.refs_1_.refs_0_), channel_id=1, source_target_pairs={{0,2},{1,15},{2,4},{3,1},{4,6},{5,3},{6,8},{7,5},{8,10},{9,7},{10,... | collective-permute-start | bytes 1548296 | tf_op jit(solution)/shard_map/ppermute | solution.py:30
  60.5 0.0 collective-permute-done.13.refs_1_
  60.5 3.0 %collective-permute-start.15 = (bf16[144,1792]{1,0:T(8,128)(2,1)}, bf16[144,1792]{1,0:T(8,128)(2,1)}, u32[]{:S(2)}, u32[]{:S(2)}) collective-permute-start(bf16[144,1792]{1,0:T(8,128)(2,1)} %collective-permute-done.13.refs_1_), channel_id=1, source_target_pairs={{0,2},{1,15},{2,4},{3,1},{4,6},{5,3},{6,8},{7,5},{8,10},{9,7},{10,... | collective-permute-start | bytes 1548296 | tf_op jit(solution)/shard_map/ppermute | solution.py:30
  63.5 0.0 collective-permute-done.9.refs_1_.refs_0_
  63.5 3.0 %collective-permute-start.12 = (bf16[144,1792]{1,0:T(8,128)(2,1)}, bf16[144,1792]{1,0:T(8,128)(2,1)}, u32[]{:S(2)}, u32[]{:S(2)}) collective-permute-start(bf16[144,1792]{1,0:T(8,128)(2,1)} %collective-permute-done.9.refs_1_.refs_0_), channel_id=1, source_target_pairs={{0,2},{1,15},{2,4},{3,1},{4,6},{5,3},{6,8},{7,5},{8,10},{9,7},{10,... | collective-permute-start | bytes 1548296 | tf_op jit(solution)/shard_map/ppermute | solution.py:30
  66.5 1.4 %mark.9 = f32[8,128]{1,0:T(8,128)S(1)} custom-call(f32[8,128]{1,0:T(8,128)S(1)} %mark.8.refs_0_, bf16[144,1792]{1,0:T(8,128)(2,1)} %collective-permute-done.9.refs_1_.refs_0_, bf16[288,1792]{1,0:T(8,128)(2,1)S(1)} %collective-permute-done.10.refs_2_.refs_4_), custom_call_target="tpu_custom_call" | custom-call | flops 20000000000 | bytes 1024 | tf_op jit(solution)/shard_map/mark/pallas_call | solution.py:57
  67.9 0.5 slice.11
  69.1 1.5 %dynamic-slice_bitcast_fusion.refs_0_ = bf16[144,3584]{1,0:T(8,128)(2,1)S(1)} fusion(bf16[3584,288]{0,1:T(8,128)(2,1)} %param.7, s32[]{:T(128)S(6)} %select_n.16), kind=kLoop, calls=%fused_computation.1 | loop fusion | bytes 2064388 | tf_op jit(solution)/shard_map/dynamic_slice | solution.py:275
  70.6 0.0 copy-start.1
  70.6 0.0 collective-permute-done.11.swapped_ref
  70.6 1.8 %line_up.1.a_ref = bf16[640,3584]{1,0:T(8,128)(2,1)S(1)} custom-call(s32[5]{0:T(128)S(1)} %stack.23.place_ref, bf16[2,68,3584]{2,1,0:T(8,128)(2,1)S(1)} %pair_up.1.pair_ref, bf16[2,68,3584]{2,1,0:T(8,128)(2,1)S(1)} %copy.12.refs_2_.beside_ref, bf16[1,68,3584]{2,1,0:T(8,128)(2,1)S(1)} %copy-done.3, bf16[3,68,3584]{2,1,0:T(8,128)(2,1)} %collective-permute-done.11.swapped_ref), custom_call_target="tpu_custom_call" | custom-call | bytes 1024 | tf_op jit(solution)/shard_map/line_up/pallas_call | solution.py:129
  72.5 0.1 copy-done.5
  72.6 0.3 copy-done.7
  72.9 4.7 %project.3.refs_4_ = bf16[8,68,1152]{2,1,0:T(8,128)(2,1)S(1)} custom-call(s32[5]{0:T(128)S(1)} %stack.23.place_ref, bf16[640,3584]{1,0:T(8,128)(2,1)S(1)} %line_up.1.a_ref, bf16[144,3584]{1,0:T(8,128)(2,1)S(1)} %dynamic-slice_bitcast_fusion.refs_0_, bf16[288,1792]{1,0:T(8,128)(2,1)S(1)} %copy-done.1, ...), custom_call_target="tpu_custom_call" | custom-call | bytes 1024 | tf_op jit(solution)/shard_map/project/pallas_call | solution.py:180
  77.6 0.0 collective-permute-done.14.refs_2_
  77.6 4.4 %project.4.refs_2_ = bf16[8,68,1152]{2,1,0:T(8,128)(2,1)S(1)} custom-call(s32[5]{0:T(128)S(1)} %stack.23.place_ref, bf16[640,3584]{1,0:T(8,128)(2,1)S(1)} %line_up.1.a_ref, bf16[144,1792]{1,0:T(8,128)(2,1)} %collective-permute-done.7.refs_1_.refs_0_, bf16[144,1792]{1,0:T(8,128)(2,1)} %collective-permute-done.13.refs_1_, ...), custom_call_target="tpu_custom_call", output_to_operand_aliasing={{}: (6, {})} | custom-call | bytes 1024 | tf_op jit(solution)/shard_map/project/pallas_call | solution.py:180
  82.0 0.0 collective-permute-done.12.refs_1_
  82.0 2.9 %project.5 = bf16[8,68,1152]{2,1,0:T(8,128)(2,1)S(1)} custom-call(s32[5]{0:T(128)S(1)} %stack.23.place_ref, bf16[640,3584]{1,0:T(8,128)(2,1)S(1)} %line_up.1.a_ref, bf16[144,1792]{1,0:T(8,128)(2,1)} %collective-permute-done.9.refs_1_.refs_0_, bf16[144,1792]{1,0:T(8,128)(2,1)} %collective-permute-done.12.refs_1_, ...), custom_call_target="tpu_custom_call", output_to_operand_aliasing={{}: (4, {})} | custom-call | bytes 1024 | tf_op jit(solution)/shard_map/project/pallas_call | solution.py:180
  84.9 22.8 %all_to_all.5.ref = bf16[8,68,1152]{2,1,0:T(8,128)(2,1)S(1)} all-to-all(bf16[8,68,1152]{2,1,0:T(8,128)(2,1)S(1)} %project.5), channel_id=1, replica_groups=mesh['x'=4,'z'=8,'y'=8,'core'=2] {'x','core'}, dimensions={0} | all-to-all | bytes 2506752 | tf_op jit(solution)/shard_map/all_to_all | solution.py:284
  107.7 3.2 %settle.1 = bf16[68,9216]{1,0:T(8,128)(2,1)} custom-call(s32[5]{0:T(128)S(1)} %stack.23.place_ref, bf16[8,68,1152]{2,1,0:T(8,128)(2,1)S(1)} %all_to_all.5.ref), custom_call_target="tpu_custom_call" | custom-call | bytes 1024 | tf_op jit(solution)/shard_map/settle/pallas_call | solution.py:212
  (35 shorter events, 0.3 us)
Async XLA Ops:
  0.0 12.9 %copy-start.11 = (f32[3584]{0:T(1024)S(1)}, f32[3584]{0:T(1024)}, u32[]{:S(2)}) copy-start(f32[3584]{0:T(1024)} %param.6) | copy-start | bytes 43012
  0.0 13.0 %copy-start.8 = (bf16[68,3584]{1,0:T(8,128)(2,1)S(1)}, bf16[68,3584]{1,0:T(8,128)(2,1)}, u32[]{:S(2)}) copy-start(bf16[68,3584]{1,0:T(8,128)(2,1)} %rows_ref.1) | copy-start | bytes 1462276
  0.0 13.0 %copy-start.9 = (s32[64]{0:T(128)S(1)}, s32[64]{0:T(128)}, u32[]{:S(2)}) copy-start(s32[64]{0:T(128)} %param.8) | copy-start | bytes 772
  0.0 13.0 %copy-start.10 = (s32[64]{0:T(128)S(1)}, s32[64]{0:T(128)}, u32[]{:S(2)}) copy-start(s32[64]{0:T(128)} %param.9) | copy-start | bytes 772
  1.4 22.2 %collective-permute-start.2 = (bf16[144,1792]{1,0:T(8,128)(2,1)S(1)}, bf16[144,1792]{1,0:T(8,128)(2,1)S(1)}, u32[]{:S(2)}, u32[]{:S(2)}) collective-permute-start(bf16[144,1792]{1,0:T(8,128)(2,1)S(1)} %get-tuple-element.24), channel_id=1, source_target_pairs={{0,16},{1,113},{16,32},{17,1},{32,48},{33,17},{48,64},{49,33},{64,... | collective-permute-start | bytes 1548296 | tf_op jit(solution)/shard_map/ppermute | solution.py:30
  13.8 4.5 %collective-permute-start = (bf16[68,3584]{1,0:T(8,128)(2,1)S(1)}, bf16[68,3584]{1,0:T(8,128)(2,1)S(1)}, u32[]{:S(2)}, u32[]{:S(2)}) collective-permute-start(bf16[68,3584]{1,0:T(8,128)(2,1)S(1)} %normalize.1.one_ref), channel_id=1, source_target_pairs={{0,1},{1,0},{2,3},{3,2},{4,5},{5,4},{6,7},{7,6},{8,9},{9,8},{10,11... | collective-permute-start | bytes 1462280 | tf_op jit(solution)/shard_map/ppermute | solution.py:30
  15.8 11.5 %collective-permute-start.5 = (bf16[144,1792]{1,0:T(8,128)(2,1)S(1)}, bf16[144,1792]{1,0:T(8,128)(2,1)S(1)}, u32[]{:S(2)}, u32[]{:S(2)}) collective-permute-start(bf16[144,1792]{1,0:T(8,128)(2,1)S(1)} %get-tuple-element.23), channel_id=1, source_target_pairs={{0,16},{1,113},{16,32},{17,1},{32,48},{33,17},{48,64},{49,33},{64,... | collective-permute-start | bytes 1548296 | tf_op jit(solution)/shard_map/ppermute | solution.py:30
  19.2 19.4 %collective-permute-start.1 = (bf16[2,68,3584]{2,0,1:T(2,128)(2,1)S(1)}, bf16[2,68,3584]{2,0,1:T(2,128)(2,1)S(1)}, u32[]{:S(2)}, u32[]{:S(2)}) collective-permute-start(bf16[2,68,3584]{2,0,1:T(2,128)(2,1)S(1)} %copy.8), channel_id=1, source_target_pairs={{0,128},{1,385},{128,256},{129,1},{256,384},{257,129},{384,0},{385... | collective-permute-start | bytes 2924552 | tf_op jit(solution)/shard_map/ppermute | solution.py:30
  23.6 11.1 %collective-permute-start.3 = (bf16[144,1792]{1,0:T(8,128)(2,1)S(1)}, bf16[144,1792]{1,0:T(8,128)(2,1)S(1)}, u32[]{:S(2)}, u32[]{:S(2)}) collective-permute-start(bf16[144,1792]{1,0:T(8,128)(2,1)S(1)} %collective-permute-done.2.refs_0_), channel_id=1, source_target_pairs={{0,16},{1,113},{16,32},{17,1},{32,48},{33,17},{48,64},{49,33},{64,... | collective-permute-start | bytes 1548296 | tf_op jit(solution)/shard_map/ppermute | solution.py:30
  27.3 14.7 %collective-permute-start.6 = (bf16[144,1792]{1,0:T(8,128)(2,1)S(1)}, bf16[144,1792]{1,0:T(8,128)(2,1)S(1)}, u32[]{:S(2)}, u32[]{:S(2)}) collective-permute-start(bf16[144,1792]{1,0:T(8,128)(2,1)S(1)} %collective-permute-done.5), channel_id=1, source_target_pairs={{0,16},{1,113},{16,32},{17,1},{32,48},{33,17},{48,64},{49,33},{64,... | collective-permute-start | bytes 1548296 | tf_op jit(solution)/shard_map/ppermute | solution.py:30
  29.6 9.2 %copy-start = (bf16[288,1792]{1,0:T(8,128)(2,1)}, bf16[288,1792]{1,0:T(8,128)(2,1)S(1)}, u32[]{:S(2)}) copy-start(bf16[288,1792]{1,0:T(8,128)(2,1)S(1)} %constant_dynamic-update-slice_fusion.refs_1_) | copy-start | bytes 3096580
  29.6 21.4 %collective-permute-start.8 = (bf16[288,1792]{1,0:T(8,128)(2,1)S(1)}, bf16[288,1792]{1,0:T(8,128)(2,1)S(1)}, u32[]{:S(2)}, u32[]{:S(2)}) collective-permute-start(bf16[288,1792]{1,0:T(8,128)(2,1)S(1)} %constant_dynamic-update-slice_fusion.refs_1_), channel_id=1, source_target_pairs={{0,2},{1,15},{2,4},{3,1},{4,6},{5,3},{6,8},{7,5},{8,10},{9,7},{10,... | collective-permute-start | bytes 3096584 | tf_op jit(solution)/shard_map/ppermute | solution.py:30
  34.7 14.3 %collective-permute-start.7 = (bf16[144,1792]{1,0:T(8,128)(2,1)S(1)}, bf16[144,1792]{1,0:T(8,128)(2,1)}, u32[]{:S(2)}, u32[]{:S(2)}) collective-permute-start(bf16[144,1792]{1,0:T(8,128)(2,1)S(1)} %collective-permute-done.3.refs_1_), channel_id=1, source_target_pairs={{0,16},{1,113},{16,32},{17,1},{32,48},{33,17},{48,64},{49,33},{64,... | collective-permute-start | bytes 1548296 | tf_op jit(solution)/shard_map/ppermute | solution.py:30
  38.8 12.1 %collective-permute-start.4 = (bf16[1,68,3584]{2,1,0:T(8,128)(2,1)S(1)}, bf16[1,68,3584]{2,1,0:T(8,128)(2,1)S(1)}, u32[]{:S(2)}, u32[]{:S(2)}) collective-permute-start(bf16[1,68,3584]{2,1,0:T(8,128)(2,1)S(1)} %slice.12), channel_id=1, source_target_pairs={{0,128},{1,385},{128,256},{129,1},{256,384},{257,129},{384,0},{385... | collective-permute-start | bytes 1462280 | tf_op jit(solution)/shard_map/ppermute | solution.py:30
  42.0 24.4 %collective-permute-start.10 = (bf16[288,1792]{1,0:T(8,128)(2,1)S(1)}, bf16[288,1792]{1,0:T(8,128)(2,1)S(1)}, u32[]{:S(2)}, u32[]{:S(2)}) collective-permute-start(bf16[288,1792]{1,0:T(8,128)(2,1)S(1)} %constant_dynamic-update-slice_fusion.2.refs_2_), channel_id=1, source_target_pairs={{0,2},{1,15},{2,4},{3,1},{4,6},{5,3},{6,8},{7,5},{8,10},{9,7},{10,... | collective-permute-start | bytes 3096584 | tf_op jit(solution)/shard_map/ppermute | solution.py:30
  46.2 14.3 %collective-permute-start.13 = (bf16[144,1792]{1,0:T(8,128)(2,1)S(1)}, bf16[144,1792]{1,0:T(8,128)(2,1)}, u32[]{:S(2)}, u32[]{:S(2)}) collective-permute-start(bf16[144,1792]{1,0:T(8,128)(2,1)S(1)} %collective-permute-done.6), channel_id=1, source_target_pairs={{0,16},{1,113},{16,32},{17,1},{32,48},{33,17},{48,64},{49,33},{64,... | collective-permute-start | bytes 1548296 | tf_op jit(solution)/shard_map/ppermute | solution.py:30
  49.0 14.5 %collective-permute-start.9 = (bf16[144,1792]{1,0:T(8,128)(2,1)}, bf16[144,1792]{1,0:T(8,128)(2,1)}, u32[]{:S(2)}, u32[]{:S(2)}) collective-permute-start(bf16[144,1792]{1,0:T(8,128)(2,1)} %collective-permute-done.7.refs_1_.refs_0_), channel_id=1, source_target_pairs={{0,16},{1,113},{16,32},{17,1},{32,48},{33,17},{48,64},{49,33},{64,... | collective-permute-start | bytes 1548296 | tf_op jit(solution)/shard_map/ppermute | solution.py:30
  51.0 1.2 %copy-start.2 = (bf16[1,68,3584]{2,1,0:T(8,128)(2,1)}, bf16[1,68,3584]{2,1,0:T(8,128)(2,1)S(1)}, u32[]{:S(2)}) copy-start(bf16[1,68,3584]{2,1,0:T(8,128)(2,1)S(1)} %collective-permute-done.4.refs_2_.distant_ref) | copy-start | bytes 1462276
  52.2 1.0 copy-start.4
  54.4 16.2 %collective-permute-start.11 = (bf16[3,68,3584]{2,1,0:T(8,128)(2,1)}, bf16[3,68,3584]{2,1,0:T(8,128)(2,1)}, u32[]{:S(2)}, u32[]{:S(2)}) collective-permute-start(bf16[3,68,3584]{2,1,0:T(8,128)(2,1)} %pad_maximum_fusion), channel_id=1, source_target_pairs={{0,1},{1,0},{2,3},{3,2},{4,5},{5,4},{6,7},{7,6},{8,9},{9,8},{10,11... | collective-permute-start | bytes 4386824 | tf_op jit(solution)/shard_map/ppermute | solution.py:30
  56.4 21.2 %collective-permute-start.14 = (bf16[144,1792]{1,0:T(8,128)(2,1)}, bf16[144,1792]{1,0:T(8,128)(2,1)}, u32[]{:S(2)}, u32[]{:S(2)}) collective-permute-start(bf16[144,1792]{1,0:T(8,128)(2,1)} %collective-permute-done.7.refs_1_.refs_0_), channel_id=1, source_target_pairs={{0,2},{1,15},{2,4},{3,1},{4,6},{5,3},{6,8},{7,5},{8,10},{9,7},{10,... | collective-permute-start | bytes 1548296 | tf_op jit(solution)/shard_map/ppermute | solution.py:30
  60.5 17.1 %collective-permute-start.15 = (bf16[144,1792]{1,0:T(8,128)(2,1)}, bf16[144,1792]{1,0:T(8,128)(2,1)}, u32[]{:S(2)}, u32[]{:S(2)}) collective-permute-start(bf16[144,1792]{1,0:T(8,128)(2,1)} %collective-permute-done.13.refs_1_), channel_id=1, source_target_pairs={{0,2},{1,15},{2,4},{3,1},{4,6},{5,3},{6,8},{7,5},{8,10},{9,7},{10,... | collective-permute-start | bytes 1548296 | tf_op jit(solution)/shard_map/ppermute | solution.py:30
  63.5 18.6 %collective-permute-start.12 = (bf16[144,1792]{1,0:T(8,128)(2,1)}, bf16[144,1792]{1,0:T(8,128)(2,1)}, u32[]{:S(2)}, u32[]{:S(2)}) collective-permute-start(bf16[144,1792]{1,0:T(8,128)(2,1)} %collective-permute-done.9.refs_1_.refs_0_), channel_id=1, source_target_pairs={{0,2},{1,15},{2,4},{3,1},{4,6},{5,3},{6,8},{7,5},{8,10},{9,7},{10,... | collective-permute-start | bytes 1548296 | tf_op jit(solution)/shard_map/ppermute | solution.py:30
  66.5 1.4 %copy-start.6 = (bf16[288,1792]{1,0:T(8,128)(2,1)}, bf16[288,1792]{1,0:T(8,128)(2,1)S(1)}, u32[]{:S(2)}) copy-start(bf16[288,1792]{1,0:T(8,128)(2,1)S(1)} %collective-permute-done.10.refs_2_.refs_4_) | copy-start | bytes 3096580
  69.0 1.6 %copy-start.3 = (bf16[1,68,3584]{2,1,0:T(8,128)(2,1)S(1)}, bf16[1,68,3584]{2,1,0:T(8,128)(2,1)}, u32[]{:S(2)}) copy-start(bf16[1,68,3584]{2,1,0:T(8,128)(2,1)} %copy-done.2) | copy-start | bytes 1462276
  70.6 1.9 %copy-start.1 = (bf16[288,1792]{1,0:T(8,128)(2,1)S(1)}, bf16[288,1792]{1,0:T(8,128)(2,1)}, u32[]{:S(2)}) copy-start(bf16[288,1792]{1,0:T(8,128)(2,1)} %copy-done) | copy-start | bytes 3096580
  70.6 2.0 %copy-start.5 = (bf16[288,1792]{1,0:T(8,128)(2,1)S(1)}, bf16[288,1792]{1,0:T(8,128)(2,1)}, u32[]{:S(2)}) copy-start(bf16[288,1792]{1,0:T(8,128)(2,1)} %copy-done.4) | copy-start | bytes 3096580
  70.6 2.3 %copy-start.7 = (bf16[288,1792]{1,0:T(8,128)(2,1)S(1)}, bf16[288,1792]{1,0:T(8,128)(2,1)}, u32[]{:S(2)}) copy-start(bf16[288,1792]{1,0:T(8,128)(2,1)} %copy-done.6) | copy-start | bytes 3096580

commit v9 on v8

--- a/solution.py
+++ b/solution.py
@@ -60,7 +60,7 @@
         in_specs=[pl.BlockSpec(memory_space=pltpu.VMEM)] * len(seen),
         out_specs=pl.BlockSpec(memory_space=pltpu.VMEM),
         compiler_params=pltpu.CompilerParams(has_side_effects=True, vmem_limit_bytes=8 * MIB),
-        cost_estimate=pl.CostEstimate(flops=int(2e10), bytes_accessed=1024, transcendentals=0),
+        cost_estimate=pl.CostEstimate(flops=12 * 10**9, bytes_accessed=1024, transcendentals=0),
         name="mark",
     )(*seen)
 
@@ -246,6 +246,8 @@
 
     a.append(along_z(a[1]))
     point = mark(a[1])
+    later = point[0, 0].astype(jnp.int32)
+    own_half = lax.dynamic_slice(weights, (c * half_width + later, 0), (half_width, features))
     b[1] = after(b[1], point)
     b.append(along_z(b[1]))
     near = [jnp.concatenate([a[1], b[1]], 0)]
@@ -271,8 +273,6 @@
     point = mark(point, a[4], far[1])
     rows_in = line_up(place, pair, beside, after(distant, point), swapped)
 
-    later = point[0, 0].astype(jnp.int32)
-    own_half = lax.dynamic_slice(weights, (c * half_width + later, 0), (half_width, features))
     columns = 4 * width
     begin = half_width * 3 // 128 * 128
     gate = project(

time: 112 us -> 113 us (level)
  local copies, waits for them, and re-layouts: 5.91 us -> 10.3 us
  waiting for transfers between devices: 0.04 us -> 3.02 us
  starting transfers between devices: 59.2 us -> 56.3 us
  Pallas kernels: 20.6 us -> 17.9 us
  other arithmetic: 1.28 us -> 0.15 us
    ppermute x16, waiting for transfers between devices: 0.04 us -> 3.02 us  [hop(): return lax.ppermute(value, tuple(axes), pairs)]
    ppermute x16, starting transfers between devices: 59.2 us -> 56.3 us  [hop(): return lax.ppermute(value, tuple(axes), pairs)]
    pallas_call x3, Pallas kernels: 12 us -> 10.3 us  [project(): pl.pallas_call(body, grid=(owners // per,), out_shape=jax.ShapeDtypeStruc...]
    dynamic_slice x1, local copies, waits for them, and re-layouts: 1.52 us -> 0.25 us  [shards(): lax.dynamic_slice(weights, (c * half_width + later, 0), (half_width, feat...]
    ppermute x1, local copies, waits for them, and re-layouts: 0.1 us -> 1.3 us  [hop(): return lax.ppermute(value, tuple(axes), pairs)]
    concatenate x1, other arithmetic: 1.28 us -> 0.15 us  [shards(): swapped = other_core(after(jnp.concatenate([beside, distant], 0), point))]
  transfers between devices with their start and end apart: 16 -> 16, of which waited for: 0 -> 2; matrix products, arithmetic and copies ran while one was open for 4% -> 8% of each run, Pallas kernels for 13% -> 11%
where the time goes in v9:
time: 113 us; the launch traced here: 112 us
  starting transfers between devices  56.3 us (50%)
  blocking collectives  23.5 us (21%)
  Pallas kernels  17.9 us (16%)
  local copies, waits for them, and re-layouts  10.3 us (9%)
  waiting for transfers between devices  3.02 us (3%)
    ppermute x16, starting transfers between devices, hop(): return lax.ppermute(value, tuple(axes), pairs)  56.3 us
    all_to_all x1, blocking collectives, shards(): received = lax.all_to_all(gate, ('x', 'core'), 0, 0, tiled=True)  23.5 us
    pallas_call x3, Pallas kernels, project(): pl.pallas_call(body, grid=(owners // per,), out_shape=jax.ShapeDtypeStruc...  10.3 us
    pallas_call x1, Pallas kernels, settle(): pl.pallas_call(body, grid=(4,), out_shape=jax.ShapeDtypeStruct((rows, 4 *...  3.22 us
    ppermute x16, waiting for transfers between devices, hop(): return lax.ppermute(value, tuple(axes), pairs)  3.02 us
    pallas_call x5, Pallas kernels, mark(): pl.pallas_call(body, out_shape=jax.ShapeDtypeStruct((8, 128), jnp.float32...  2.69 us
  transfers between devices with their start and end apart: 16, of which 2 were waited for; matrix products, arithmetic and copies ran while one was open for 8% of the time, Pallas kernels for 11%

profile of v9, /device:TPU:1, one launch (start us, length us, event | category | flops | bytes accessed | tf_op | source)
XLA Modules:
  0.0 112.2 jit_solution(10017032441373114979)
XLA Ops:
  0.0 1.3 %dynamic-slice_bitcast_fusion.1 = (bf16[144,1792]{1,0:T(8,128)(2,1)S(1)}, bf16[144,1792]{1,0:T(8,128)(2,1)S(1)}) fusion(bf16[3584,288]{0,1:T(8,128)(2,1)} %param.7, s32[]{:T(128)S(6)} %select_n.13, s32[]{:T(128)S(6)} %select_n.15, s32[]{:T(128)S(6)} %select_n.14), kind=kLoop, calls=%fused_computation.2 | loop fusion | bytes 2064396 | tf_op jit(solution)/shard_map/dynamic_slice | solution.py:238
  1.4 11.5 %collective-permute-start.2 = (bf16[144,1792]{1,0:T(8,128)(2,1)S(1)}, bf16[144,1792]{1,0:T(8,128)(2,1)}, u32[]{:S(2)}, u32[]{:S(2)}) collective-permute-start(bf16[144,1792]{1,0:T(8,128)(2,1)S(1)} %get-tuple-element.24), channel_id=1, source_target_pairs={{0,16},{1,113},{16,32},{17,1},{32,48},{33,17},{48,64},{49,33},{64,... | collective-permute-start | bytes 1548296 | tf_op jit(solution)/shard_map/ppermute | solution.py:30
  12.9 0.1 stack.23.place_ref
  13.0 0.8 normalize.1.one_ref
  13.8 1.9 %collective-permute-start = (bf16[68,3584]{1,0:T(8,128)(2,1)S(1)}, bf16[68,3584]{1,0:T(8,128)(2,1)S(1)}, u32[]{:S(2)}, u32[]{:S(2)}) collective-permute-start(bf16[68,3584]{1,0:T(8,128)(2,1)S(1)} %normalize.1.one_ref), channel_id=1, source_target_pairs={{0,1},{1,0},{2,3},{3,2},{4,5},{5,4},{6,7},{7,6},{8,9},{9,8},{10,11... | collective-permute-start | bytes 1462280 | tf_op jit(solution)/shard_map/ppermute | solution.py:30
  15.8 2.6 %collective-permute-start.5 = (bf16[144,1792]{1,0:T(8,128)(2,1)S(1)}, bf16[144,1792]{1,0:T(8,128)(2,1)}, u32[]{:S(2)}, u32[]{:S(2)}) collective-permute-start(bf16[144,1792]{1,0:T(8,128)(2,1)S(1)} %get-tuple-element.23), channel_id=1, source_target_pairs={{0,16},{1,113},{16,32},{17,1},{32,48},{33,17},{48,64},{49,33},{64,... | collective-permute-start | bytes 1548296 | tf_op jit(solution)/shard_map/ppermute | solution.py:30
  18.4 0.1 pair_up.1.pair_ref
  18.5 1.7 %copy.8 = bf16[2,68,3584]{2,0,1:T(2,128)(2,1)} copy(bf16[2,68,3584]{2,1,0:T(8,128)(2,1)S(1)} %pair_up.1.pair_ref) | data formatting | bytes 1949696 | tf_op jit(solution)/shard_map/pair_up/pallas_call | solution.py:98
  20.2 4.4 %collective-permute-start.1 = (bf16[2,68,3584]{2,0,1:T(2,128)(2,1)}, bf16[2,68,3584]{2,0,1:T(2,128)(2,1)}, u32[]{:S(2)}, u32[]{:S(2)}) collective-permute-start(bf16[2,68,3584]{2,0,1:T(2,128)(2,1)} %copy.8), channel_id=1, source_target_pairs={{0,128},{1,385},{128,256},{129,1},{256,384},{257,129},{384,0},{385... | collective-permute-start | bytes 2924552 | tf_op jit(solution)/shard_map/ppermute | solution.py:30
  24.5 3.6 %collective-permute-start.3 = (bf16[144,1792]{1,0:T(8,128)(2,1)}, bf16[144,1792]{1,0:T(8,128)(2,1)}, u32[]{:S(2)}, u32[]{:S(2)}) collective-permute-start(bf16[144,1792]{1,0:T(8,128)(2,1)} %collective-permute-done.2.refs_0_), channel_id=1, source_target_pairs={{0,16},{1,113},{16,32},{17,1},{32,48},{33,17},{48,64},{49,33},{64,... | collective-permute-start | bytes 1548296 | tf_op jit(solution)/shard_map/ppermute | solution.py:30
  28.2 1.1 mark.5.refs_0_
  29.2 0.6 slice.11
  30.5 0.0 collective-permute-done.5
  30.5 2.2 %collective-permute-start.6 = (bf16[144,1792]{1,0:T(8,128)(2,1)}, bf16[144,1792]{1,0:T(8,128)(2,1)}, u32[]{:S(2)}, u32[]{:S(2)}) collective-permute-start(bf16[144,1792]{1,0:T(8,128)(2,1)} %collective-permute-done.5), channel_id=1, source_target_pairs={{0,16},{1,113},{16,32},{17,1},{32,48},{33,17},{48,64},{49,33},{64,... | collective-permute-start | bytes 1548296 | tf_op jit(solution)/shard_map/ppermute | solution.py:30
  32.7 1.1 constant_dynamic-update-slice_fusion.1
  33.7 1.1 constant_dynamic-update-slice_fusion.refs_1_
  34.8 5.1 %collective-permute-start.8 = (bf16[288,1792]{1,0:T(8,128)(2,1)S(1)}, bf16[288,1792]{1,0:T(8,128)(2,1)S(1)}, u32[]{:S(2)}, u32[]{:S(2)}) collective-permute-start(bf16[288,1792]{1,0:T(8,128)(2,1)S(1)} %constant_dynamic-update-slice_fusion.refs_1_), channel_id=1, source_target_pairs={{0,2},{1,15},{2,4},{3,1},{4,6},{5,3},{6,8},{7,5},{8,10},{9,7},{10,... | collective-permute-start | bytes 3096584 | tf_op jit(solution)/shard_map/ppermute | solution.py:30
  39.9 0.0 collective-permute-done.3.refs_1_
  39.9 2.2 %collective-permute-start.7 = (bf16[144,1792]{1,0:T(8,128)(2,1)}, bf16[144,1792]{1,0:T(8,128)(2,1)S(1)}, u32[]{:S(2)}, u32[]{:S(2)}) collective-permute-start(bf16[144,1792]{1,0:T(8,128)(2,1)} %collective-permute-done.3.refs_1_), channel_id=1, source_target_pairs={{0,16},{1,113},{16,32},{17,1},{32,48},{33,17},{48,64},{49,33},{64,... | collective-permute-start | bytes 1548296 | tf_op jit(solution)/shard_map/ppermute | solution.py:30
  42.1 1.1 constant_dynamic-update-slice_fusion.3
  43.2 0.0 collective-permute-done.1
  43.2 1.3 %copy.12.refs_2_.beside_ref = bf16[2,68,3584]{2,1,0:T(8,128)(2,1)S(1)} copy(bf16[2,68,3584]{2,0,1:T(2,128)(2,1)} %collective-permute-done.1) | data formatting | bytes 1949696 | tf_op jit(solution)/shard_map/ppermute | solution.py:30
  44.5 1.0 mark.6.refs_0_
  45.6 2.5 %collective-permute-start.4 = (bf16[1,68,3584]{2,1,0:T(8,128)(2,1)S(1)}, bf16[1,68,3584]{2,1,0:T(8,128)(2,1)S(1)}, u32[]{:S(2)}, u32[]{:S(2)}) collective-permute-start(bf16[1,68,3584]{2,1,0:T(8,128)(2,1)S(1)} %slice.12), channel_id=1, source_target_pairs={{0,128},{1,385},{128,256},{129,1},{256,384},{257,129},{384,0},{385... | collective-permute-start | bytes 1462280 | tf_op jit(solution)/shard_map/ppermute | solution.py:30
  48.1 0.0 collective-permute-done.6
  48.1 0.7 slice.10.refs_1_
  48.8 1.1 constant_dynamic-update-slice_fusion.2.refs_2_
  49.8 3.0 %collective-permute-start.10 = (bf16[288,1792]{1,0:T(8,128)(2,1)S(1)}, bf16[288,1792]{1,0:T(8,128)(2,1)S(1)}, u32[]{:S(2)}, u32[]{:S(2)}) collective-permute-start(bf16[288,1792]{1,0:T(8,128)(2,1)S(1)} %constant_dynamic-update-slice_fusion.2.refs_2_), channel_id=1, source_target_pairs={{0,2},{1,15},{2,4},{3,1},{4,6},{5,3},{6,8},{7,5},{8,10},{9,7},{10,... | collective-permute-start | bytes 3096584 | tf_op jit(solution)/shard_map/ppermute | solution.py:30
  52.8 3.4 %collective-permute-start.13 = (bf16[144,1792]{1,0:T(8,128)(2,1)}, bf16[144,1792]{1,0:T(8,128)(2,1)S(1)}, u32[]{:S(2)}, u32[]{:S(2)}) collective-permute-start(bf16[144,1792]{1,0:T(8,128)(2,1)} %collective-permute-done.6), channel_id=1, source_target_pairs={{0,16},{1,113},{16,32},{17,1},{32,48},{33,17},{48,64},{49,33},{64,... | collective-permute-start | bytes 1548296 | tf_op jit(solution)/shard_map/ppermute | solution.py:30
  56.2 0.0 collective-permute-done.7.refs_1_.refs_0_
  56.2 1.9 %collective-permute-start.9 = (bf16[144,1792]{1,0:T(8,128)(2,1)S(1)}, bf16[144,1792]{1,0:T(8,128)(2,1)S(1)}, u32[]{:S(2)}, u32[]{:S(2)}) collective-permute-start(bf16[144,1792]{1,0:T(8,128)(2,1)S(1)} %collective-permute-done.7.refs_1_.refs_0_), channel_id=1, source_target_pairs={{0,16},{1,113},{16,32},{17,1},{32,48},{33,17},{48,64},{49,33},{64,... | collective-permute-start | bytes 1548296 | tf_op jit(solution)/shard_map/ppermute | solution.py:30
  58.2 0.0 collective-permute-done.8.refs_3_
  58.2 0.0 copy-start.3
  58.2 0.1 pad_maximum_fusion
  58.4 3.5 %collective-permute-start.11 = (bf16[3,68,3584]{2,1,0:T(8,128)(2,1)S(1)}, bf16[3,68,3584]{2,1,0:T(8,128)(2,1)S(1)}, u32[]{:S(2)}, u32[]{:S(2)}) collective-permute-start(bf16[3,68,3584]{2,1,0:T(8,128)(2,1)S(1)} %pad_maximum_fusion), channel_id=1, source_target_pairs={{0,1},{1,0},{2,3},{3,2},{4,5},{5,4},{6,7},{7,6},{8,9},{9,8},{10,11... | collective-permute-start | bytes 4386824 | tf_op jit(solution)/shard_map/ppermute | solution.py:30
  61.9 0.2 dynamic-slice_bitcast_fusion.refs_0_
  62.1 3.3 %collective-permute-start.14 = (bf16[144,1792]{1,0:T(8,128)(2,1)S(1)}, bf16[144,1792]{1,0:T(8,128)(2,1)S(1)}, u32[]{:S(2)}, u32[]{:S(2)}) collective-permute-start(bf16[144,1792]{1,0:T(8,128)(2,1)S(1)} %collective-permute-done.7.refs_1_.refs_0_), channel_id=1, source_target_pairs={{0,2},{1,15},{2,4},{3,1},{4,6},{5,3},{6,8},{7,5},{8,10},{9,7},{10,... | collective-permute-start | bytes 1548296 | tf_op jit(solution)/shard_map/ppermute | solution.py:30
  65.4 2.3 %collective-permute-start.15 = (bf16[144,1792]{1,0:T(8,128)(2,1)S(1)}, bf16[144,1792]{1,0:T(8,128)(2,1)S(1)}, u32[]{:S(2)}, u32[]{:S(2)}) collective-permute-start(bf16[144,1792]{1,0:T(8,128)(2,1)S(1)} %collective-permute-done.13.refs_1_), channel_id=1, source_target_pairs={{0,2},{1,15},{2,4},{3,1},{4,6},{5,3},{6,8},{7,5},{8,10},{9,7},{10,... | collective-permute-start | bytes 1548296 | tf_op jit(solution)/shard_map/ppermute | solution.py:30
  67.8 0.9 collective-permute-done.9.refs_1_.refs_0_
  68.7 3.0 %collective-permute-start.12 = (bf16[144,1792]{1,0:T(8,128)(2,1)S(1)}, bf16[144,1792]{1,0:T(8,128)(2,1)S(1)}, u32[]{:S(2)}, u32[]{:S(2)}) collective-permute-start(bf16[144,1792]{1,0:T(8,128)(2,1)S(1)} %collective-permute-done.9.refs_1_.refs_0_), channel_id=1, source_target_pairs={{0,2},{1,15},{2,4},{3,1},{4,6},{5,3},{6,8},{7,5},{8,10},{9,7},{10,... | collective-permute-start | bytes 1548296 | tf_op jit(solution)/shard_map/ppermute | solution.py:30
  71.7 0.6 mark.9
  72.3 0.8 line_up.1.a_ref
  73.1 4.7 %project.3.refs_4_ = bf16[8,68,1152]{2,1,0:T(8,128)(2,1)S(1)} custom-call(s32[5]{0:T(128)S(1)} %stack.23.place_ref, bf16[640,3584]{1,0:T(8,128)(2,1)S(1)} %line_up.1.a_ref, bf16[144,3584]{1,0:T(8,128)(2,1)S(1)} %dynamic-slice_bitcast_fusion.refs_0_, bf16[288,1792]{1,0:T(8,128)(2,1)S(1)} %constant_dynamic-update-slice_fusion.refs_1_, ...), custom_call_target="tpu_custom_call" | custom-call | bytes 1024 | tf_op jit(solution)/shard_map/project/pallas_call | solution.py:180
  77.8 3.4 %project.4.refs_2_ = bf16[8,68,1152]{2,1,0:T(8,128)(2,1)S(1)} custom-call(s32[5]{0:T(128)S(1)} %stack.23.place_ref, bf16[640,3584]{1,0:T(8,128)(2,1)S(1)} %line_up.1.a_ref, bf16[144,1792]{1,0:T(8,128)(2,1)S(1)} %collective-permute-done.7.refs_1_.refs_0_, bf16[144,1792]{1,0:T(8,128)(2,1)S(1)} %collective-permute-done.13.refs_1_, ...), custom_call_target="tpu_custom_call", output_to_operand_aliasing={{}: (6, {})} | custom-call | bytes 1024 | tf_op jit(solution)/shard_map/project/pallas_call | solution.py:180
  81.3 2.0 %collective-permute-done.12.refs_1_ = bf16[144,1792]{1,0:T(8,128)(2,1)S(1)} collective-permute-done((bf16[144,1792]{1,0:T(8,128)(2,1)S(1)}, bf16[144,1792]{1,0:T(8,128)(2,1)S(1)}, u32[]{:S(2)}, u32[]{:S(2)}) %collective-permute-start.12) | collective-permute-done | bytes 516128 | tf_op jit(solution)/shard_map/ppermute | solution.py:30
  83.3 2.2 %project.5 = bf16[8,68,1152]{2,1,0:T(8,128)(2,1)S(1)} custom-call(s32[5]{0:T(128)S(1)} %stack.23.place_ref, bf16[640,3584]{1,0:T(8,128)(2,1)S(1)} %line_up.1.a_ref, bf16[144,1792]{1,0:T(8,128)(2,1)S(1)} %collective-permute-done.9.refs_1_.refs_0_, bf16[144,1792]{1,0:T(8,128)(2,1)S(1)} %collective-permute-done.12.refs_1_, ...), custom_call_target="tpu_custom_call", output_to_operand_aliasing={{}: (4, {})} | custom-call | bytes 1024 | tf_op jit(solution)/shard_map/project/pallas_call | solution.py:180
  85.5 23.5 %all_to_all.5.ref = bf16[8,68,1152]{2,1,0:T(8,128)(2,1)S(1)} all-to-all(bf16[8,68,1152]{2,1,0:T(8,128)(2,1)S(1)} %project.5), channel_id=1, replica_groups=mesh['x'=4,'z'=8,'y'=8,'core'=2] {'x','core'}, dimensions={0} | all-to-all | bytes 2506752 | tf_op jit(solution)/shard_map/all_to_all | solution.py:284
  109.0 3.2 %settle.1 = bf16[68,9216]{1,0:T(8,128)(2,1)} custom-call(s32[5]{0:T(128)S(1)} %stack.23.place_ref, bf16[8,68,1152]{2,1,0:T(8,128)(2,1)S(1)} %all_to_all.5.ref), custom_call_target="tpu_custom_call" | custom-call | bytes 1024 | tf_op jit(solution)/shard_map/settle/pallas_call | solution.py:212
  (21 shorter events, 0.1 us)
Async XLA Ops:
  0.0 12.9 %copy-start.4 = (f32[3584]{0:T(1024)S(1)}, f32[3584]{0:T(1024)}, u32[]{:S(2)}) copy-start(f32[3584]{0:T(1024)} %param.6) | copy-start | bytes 43012
  0.0 13.0 %copy-start.1 = (s32[64]{0:T(128)S(1)}, s32[64]{0:T(128)}, u32[]{:S(2)}) copy-start(s32[64]{0:T(128)} %param.8) | copy-start | bytes 772
  0.0 13.0 %copy-start.2 = (s32[64]{0:T(128)S(1)}, s32[64]{0:T(128)}, u32[]{:S(2)}) copy-start(s32[64]{0:T(128)} %param.9) | copy-start | bytes 772
  0.0 13.0 %copy-start = (bf16[68,3584]{1,0:T(8,128)(2,1)S(1)}, bf16[68,3584]{1,0:T(8,128)(2,1)}, u32[]{:S(2)}) copy-start(bf16[68,3584]{1,0:T(8,128)(2,1)} %rows_ref.1) | copy-start | bytes 1462276
  1.4 23.2 %collective-permute-start.2 = (bf16[144,1792]{1,0:T(8,128)(2,1)S(1)}, bf16[144,1792]{1,0:T(8,128)(2,1)}, u32[]{:S(2)}, u32[]{:S(2)}) collective-permute-start(bf16[144,1792]{1,0:T(8,128)(2,1)S(1)} %get-tuple-element.24), channel_id=1, source_target_pairs={{0,16},{1,113},{16,32},{17,1},{32,48},{33,17},{48,64},{49,33},{64,... | collective-permute-start | bytes 1548296 | tf_op jit(solution)/shard_map/ppermute | solution.py:30
  13.8 4.5 %collective-permute-start = (bf16[68,3584]{1,0:T(8,128)(2,1)S(1)}, bf16[68,3584]{1,0:T(8,128)(2,1)S(1)}, u32[]{:S(2)}, u32[]{:S(2)}) collective-permute-start(bf16[68,3584]{1,0:T(8,128)(2,1)S(1)} %normalize.1.one_ref), channel_id=1, source_target_pairs={{0,1},{1,0},{2,3},{3,2},{4,5},{5,4},{6,7},{7,6},{8,9},{9,8},{10,11... | collective-permute-start | bytes 1462280 | tf_op jit(solution)/shard_map/ppermute | solution.py:30
  15.8 14.7 %collective-permute-start.5 = (bf16[144,1792]{1,0:T(8,128)(2,1)S(1)}, bf16[144,1792]{1,0:T(8,128)(2,1)}, u32[]{:S(2)}, u32[]{:S(2)}) collective-permute-start(bf16[144,1792]{1,0:T(8,128)(2,1)S(1)} %get-tuple-element.23), channel_id=1, source_target_pairs={{0,16},{1,113},{16,32},{17,1},{32,48},{33,17},{48,64},{49,33},{64,... | collective-permute-start | bytes 1548296 | tf_op jit(solution)/shard_map/ppermute | solution.py:30
  20.2 23.1 %collective-permute-start.1 = (bf16[2,68,3584]{2,0,1:T(2,128)(2,1)}, bf16[2,68,3584]{2,0,1:T(2,128)(2,1)}, u32[]{:S(2)}, u32[]{:S(2)}) collective-permute-start(bf16[2,68,3584]{2,0,1:T(2,128)(2,1)} %copy.8), channel_id=1, source_target_pairs={{0,128},{1,385},{128,256},{129,1},{256,384},{257,129},{384,0},{385... | collective-permute-start | bytes 2924552 | tf_op jit(solution)/shard_map/ppermute | solution.py:30
  24.5 15.4 %collective-permute-start.3 = (bf16[144,1792]{1,0:T(8,128)(2,1)}, bf16[144,1792]{1,0:T(8,128)(2,1)}, u32[]{:S(2)}, u32[]{:S(2)}) collective-permute-start(bf16[144,1792]{1,0:T(8,128)(2,1)} %collective-permute-done.2.refs_0_), channel_id=1, source_target_pairs={{0,16},{1,113},{16,32},{17,1},{32,48},{33,17},{48,64},{49,33},{64,... | collective-permute-start | bytes 1548296 | tf_op jit(solution)/shard_map/ppermute | solution.py:30
  30.5 17.6 %collective-permute-start.6 = (bf16[144,1792]{1,0:T(8,128)(2,1)}, bf16[144,1792]{1,0:T(8,128)(2,1)}, u32[]{:S(2)}, u32[]{:S(2)}) collective-permute-start(bf16[144,1792]{1,0:T(8,128)(2,1)} %collective-permute-done.5), channel_id=1, source_target_pairs={{0,16},{1,113},{16,32},{17,1},{32,48},{33,17},{48,64},{49,33},{64,... | collective-permute-start | bytes 1548296 | tf_op jit(solution)/shard_map/ppermute | solution.py:30
  34.8 23.4 %collective-permute-start.8 = (bf16[288,1792]{1,0:T(8,128)(2,1)S(1)}, bf16[288,1792]{1,0:T(8,128)(2,1)S(1)}, u32[]{:S(2)}, u32[]{:S(2)}) collective-permute-start(bf16[288,1792]{1,0:T(8,128)(2,1)S(1)} %constant_dynamic-update-slice_fusion.refs_1_), channel_id=1, source_target_pairs={{0,2},{1,15},{2,4},{3,1},{4,6},{5,3},{6,8},{7,5},{8,10},{9,7},{10,... | collective-permute-start | bytes 3096584 | tf_op jit(solution)/shard_map/ppermute | solution.py:30
  39.9 16.3 %collective-permute-start.7 = (bf16[144,1792]{1,0:T(8,128)(2,1)}, bf16[144,1792]{1,0:T(8,128)(2,1)S(1)}, u32[]{:S(2)}, u32[]{:S(2)}) collective-permute-start(bf16[144,1792]{1,0:T(8,128)(2,1)} %collective-permute-done.3.refs_1_), channel_id=1, source_target_pairs={{0,16},{1,113},{16,32},{17,1},{32,48},{33,17},{48,64},{49,33},{64,... | collective-permute-start | bytes 1548296 | tf_op jit(solution)/shard_map/ppermute | solution.py:30
  45.6 12.6 %collective-permute-start.4 = (bf16[1,68,3584]{2,1,0:T(8,128)(2,1)S(1)}, bf16[1,68,3584]{2,1,0:T(8,128)(2,1)S(1)}, u32[]{:S(2)}, u32[]{:S(2)}) collective-permute-start(bf16[1,68,3584]{2,1,0:T(8,128)(2,1)S(1)} %slice.12), channel_id=1, source_target_pairs={{0,128},{1,385},{128,256},{129,1},{256,384},{257,129},{384,0},{385... | collective-permute-start | bytes 1462280 | tf_op jit(solution)/shard_map/ppermute | solution.py:30
  49.8 21.8 %collective-permute-start.10 = (bf16[288,1792]{1,0:T(8,128)(2,1)S(1)}, bf16[288,1792]{1,0:T(8,128)(2,1)S(1)}, u32[]{:S(2)}, u32[]{:S(2)}) collective-permute-start(bf16[288,1792]{1,0:T(8,128)(2,1)S(1)} %constant_dynamic-update-slice_fusion.2.refs_2_), channel_id=1, source_target_pairs={{0,2},{1,15},{2,4},{3,1},{4,6},{5,3},{6,8},{7,5},{8,10},{9,7},{10,... | collective-permute-start | bytes 3096584 | tf_op jit(solution)/shard_map/ppermute | solution.py:30
  52.8 12.6 %collective-permute-start.13 = (bf16[144,1792]{1,0:T(8,128)(2,1)}, bf16[144,1792]{1,0:T(8,128)(2,1)S(1)}, u32[]{:S(2)}, u32[]{:S(2)}) collective-permute-start(bf16[144,1792]{1,0:T(8,128)(2,1)} %collective-permute-done.6), channel_id=1, source_target_pairs={{0,16},{1,113},{16,32},{17,1},{32,48},{33,17},{48,64},{49,33},{64,... | collective-permute-start | bytes 1548296 | tf_op jit(solution)/shard_map/ppermute | solution.py:30
  56.2 12.5 %collective-permute-start.9 = (bf16[144,1792]{1,0:T(8,128)(2,1)S(1)}, bf16[144,1792]{1,0:T(8,128)(2,1)S(1)}, u32[]{:S(2)}, u32[]{:S(2)}) collective-permute-start(bf16[144,1792]{1,0:T(8,128)(2,1)S(1)} %collective-permute-done.7.refs_1_.refs_0_), channel_id=1, source_target_pairs={{0,16},{1,113},{16,32},{17,1},{32,48},{33,17},{48,64},{49,33},{64,... | collective-permute-start | bytes 1548296 | tf_op jit(solution)/shard_map/ppermute | solution.py:30
  58.2 3.7 %copy-start.3 = (bf16[3584,288]{0,1:T(8,128)(2,1)S(1)}, bf16[3584,288]{0,1:T(8,128)(2,1)}, u32[]{:S(2)}) copy-start(bf16[3584,288]{0,1:T(8,128)(2,1)} %param.7) | copy-start | bytes 6193156
  58.4 13.9 %collective-permute-start.11 = (bf16[3,68,3584]{2,1,0:T(8,128)(2,1)S(1)}, bf16[3,68,3584]{2,1,0:T(8,128)(2,1)S(1)}, u32[]{:S(2)}, u32[]{:S(2)}) collective-permute-start(bf16[3,68,3584]{2,1,0:T(8,128)(2,1)S(1)} %pad_maximum_fusion), channel_id=1, source_target_pairs={{0,1},{1,0},{2,3},{3,2},{4,5},{5,4},{6,7},{7,6},{8,9},{9,8},{10,11... | collective-permute-start | bytes 4386824 | tf_op jit(solution)/shard_map/ppermute | solution.py:30
  62.1 15.7 %collective-permute-start.14 = (bf16[144,1792]{1,0:T(8,128)(2,1)S(1)}, bf16[144,1792]{1,0:T(8,128)(2,1)S(1)}, u32[]{:S(2)}, u32[]{:S(2)}) collective-permute-start(bf16[144,1792]{1,0:T(8,128)(2,1)S(1)} %collective-permute-done.7.refs_1_.refs_0_), channel_id=1, source_target_pairs={{0,2},{1,15},{2,4},{3,1},{4,6},{5,3},{6,8},{7,5},{8,10},{9,7},{10,... | collective-permute-start | bytes 1548296 | tf_op jit(solution)/shard_map/ppermute | solution.py:30
  65.4 12.4 %collective-permute-start.15 = (bf16[144,1792]{1,0:T(8,128)(2,1)S(1)}, bf16[144,1792]{1,0:T(8,128)(2,1)S(1)}, u32[]{:S(2)}, u32[]{:S(2)}) collective-permute-start(bf16[144,1792]{1,0:T(8,128)(2,1)S(1)} %collective-permute-done.13.refs_1_), channel_id=1, source_target_pairs={{0,2},{1,15},{2,4},{3,1},{4,6},{5,3},{6,8},{7,5},{8,10},{9,7},{10,... | collective-permute-start | bytes 1548296 | tf_op jit(solution)/shard_map/ppermute | solution.py:30
  68.7 14.6 %collective-permute-start.12 = (bf16[144,1792]{1,0:T(8,128)(2,1)S(1)}, bf16[144,1792]{1,0:T(8,128)(2,1)S(1)}, u32[]{:S(2)}, u32[]{:S(2)}) collective-permute-start(bf16[144,1792]{1,0:T(8,128)(2,1)S(1)} %collective-permute-done.9.refs_1_.refs_0_), channel_id=1, source_target_pairs={{0,2},{1,15},{2,4},{3,1},{4,6},{5,3},{6,8},{7,5},{8,10},{9,7},{10,... | collective-permute-start | bytes 1548296 | tf_op jit(solution)/shard_map/ppermute | solution.py:30

commit v10 on v9

--- a/solution.py
+++ b/solution.py
@@ -60,7 +60,7 @@
         in_specs=[pl.BlockSpec(memory_space=pltpu.VMEM)] * len(seen),
         out_specs=pl.BlockSpec(memory_space=pltpu.VMEM),
         compiler_params=pltpu.CompilerParams(has_side_effects=True, vmem_limit_bytes=8 * MIB),
-        cost_estimate=pl.CostEstimate(flops=12 * 10**9, bytes_accessed=1024, transcendentals=0),
+        cost_estimate=pl.CostEstimate(flops=14 * 10**9, bytes_accessed=1024, transcendentals=0),
         name="mark",
     )(*seen)
 
@@ -246,8 +246,6 @@
 
     a.append(along_z(a[1]))
     point = mark(a[1])
-    later = point[0, 0].astype(jnp.int32)
-    own_half = lax.dynamic_slice(weights, (c * half_width + later, 0), (half_width, features))
     b[1] = after(b[1], point)
     b.append(along_z(b[1]))
     near = [jnp.concatenate([a[1], b[1]], 0)]
@@ -273,6 +271,7 @@
     point = mark(point, a[4], far[1])
     rows_in = line_up(place, pair, beside, after(distant, point), swapped)
 
+    own_half = lax.dynamic_slice(weights, (c * half_width, 0), (half_width, features))
     columns = 4 * width
     begin = half_width * 3 // 128 * 128
     gate = project(

time: 113 us -> 105 us (0.929)
  local copies, waits for them, and re-layouts: 10.3 us -> 2.57 us
  starting transfers between devices: 56.3 us -> 59.3 us
  Pallas kernels: 17.9 us -> 15.8 us
  waiting for transfers between devices: 3.02 us -> 1.56 us
    ppermute x16, starting transfers between devices: 56.3 us -> 59.3 us  [hop(): return lax.ppermute(value, tuple(axes), pairs)]
    pallas_call x5, Pallas kernels: 2.69 us -> 0.61 us  [mark(): pl.pallas_call(body, out_shape=jax.ShapeDtypeStruct((8, 128), jnp.float32...]
    unnamed x12, local copies, waits for them, and re-layouts: 2.18 us -> 0.09 us
    ppermute x16, waiting for transfers between devices: 3.02 us -> 1.56 us  [hop(): return lax.ppermute(value, tuple(axes), pairs)]
    ppermute x1, local copies, waits for them, and re-layouts: 1.3 us -> 0.1 us  [hop(): return lax.ppermute(value, tuple(axes), pairs)]
  transfers between devices with their start and end apart: 16 -> 16, of which waited for: 2 -> 2; matrix products, arithmetic and copies ran while one was open for 8% -> 1% of each run, Pallas kernels for 11% -> 10%
where the time goes in v10:
time: 105 us; the launch traced here: 104 us
  starting transfers between devices  59.3 us (56%)
  blocking collectives  24.4 us (23%)
  Pallas kernels  15.8 us (15%)
  local copies, waits for them, and re-layouts  2.57 us (2%)
  waiting for transfers between devices  1.56 us (1%)
    ppermute x16, starting transfers between devices, hop(): return lax.ppermute(value, tuple(axes), pairs)  59.3 us
    all_to_all x1, blocking collectives, shards(): received = lax.all_to_all(gate, ('x', 'core'), 0, 0, tiled=True)  24.4 us
    pallas_call x3, Pallas kernels, project(): pl.pallas_call(body, grid=(owners // per,), out_shape=jax.ShapeDtypeStruc...  10.3 us
    pallas_call x1, Pallas kernels, settle(): pl.pallas_call(body, grid=(4,), out_shape=jax.ShapeDtypeStruct((rows, 4 *...  3.22 us
  transfers between devices with their start and end apart: 16, of which 2 were waited for; matrix products, arithmetic and copies ran while one was open for 1% of the time, Pallas kernels for 10%

profile of v10, /device:TPU:1, one launch (start us, length us, event | category | flops | bytes accessed | tf_op | source)
XLA Modules:
  0.0 104.2 jit_solution(5615164563838142249)
XLA Ops:
  0.0 1.3 %dynamic-slice_bitcast_fusion.1 = (bf16[144,1792]{1,0:T(8,128)(2,1)S(1)}, bf16[144,1792]{1,0:T(8,128)(2,1)S(1)}) fusion(bf16[3584,288]{0,1:T(8,128)(2,1)} %param.7, s32[]{:T(128)S(6)} %select_n.11, s32[]{:T(128)S(6)} %select_n.13, s32[]{:T(128)S(6)} %select_n.12), kind=kLoop, calls=%fused_computation.2 | loop fusion | bytes 2064396 | tf_op jit(solution)/shard_map/dynamic_slice | solution.py:238
  1.4 11.5 %collective-permute-start.2 = (bf16[144,1792]{1,0:T(8,128)(2,1)S(1)}, bf16[144,1792]{1,0:T(8,128)(2,1)S(1)}, u32[]{:S(2)}, u32[]{:S(2)}) collective-permute-start(bf16[144,1792]{1,0:T(8,128)(2,1)S(1)} %get-tuple-element.24), channel_id=1, source_target_pairs={{0,16},{1,113},{16,32},{17,1},{32,48},{33,17},{48,64},{49,33},{64,... | collective-permute-start | bytes 1548296 | tf_op jit(solution)/shard_map/ppermute | solution.py:30
  12.9 0.1 stack.23.place_ref
  13.0 0.8 normalize.1.one_ref
  13.8 1.9 %collective-permute-start = (bf16[68,3584]{1,0:T(8,128)(2,1)S(1)}, bf16[68,3584]{1,0:T(8,128)(2,1)S(1)}, u32[]{:S(2)}, u32[]{:S(2)}) collective-permute-start(bf16[68,3584]{1,0:T(8,128)(2,1)S(1)} %normalize.1.one_ref), channel_id=1, source_target_pairs={{0,1},{1,0},{2,3},{3,2},{4,5},{5,4},{6,7},{7,6},{8,9},{9,8},{10,11... | collective-permute-start | bytes 1462280 | tf_op jit(solution)/shard_map/ppermute | solution.py:30
  15.8 2.6 %collective-permute-start.5 = (bf16[144,1792]{1,0:T(8,128)(2,1)S(1)}, bf16[144,1792]{1,0:T(8,128)(2,1)S(1)}, u32[]{:S(2)}, u32[]{:S(2)}) collective-permute-start(bf16[144,1792]{1,0:T(8,128)(2,1)S(1)} %get-tuple-element.23), channel_id=1, source_target_pairs={{0,16},{1,113},{16,32},{17,1},{32,48},{33,17},{48,64},{49,33},{64,... | collective-permute-start | bytes 1548296 | tf_op jit(solution)/shard_map/ppermute | solution.py:30
  18.4 0.0 collective-permute-done.other_ref
  18.4 0.1 pair_up.1.pair_ref
  18.5 0.8 copy.8
  19.2 4.4 %collective-permute-start.1 = (bf16[2,68,3584]{2,0,1:T(2,128)(2,1)S(1)}, bf16[2,68,3584]{2,0,1:T(2,128)(2,1)S(1)}, u32[]{:S(2)}, u32[]{:S(2)}) collective-permute-start(bf16[2,68,3584]{2,0,1:T(2,128)(2,1)S(1)} %copy.8), channel_id=1, source_target_pairs={{0,128},{1,385},{128,256},{129,1},{256,384},{257,129},{384,0},{385... | collective-permute-start | bytes 2924552 | tf_op jit(solution)/shard_map/ppermute | solution.py:30
  23.6 0.0 collective-permute-done.2.refs_0_
  23.6 3.6 %collective-permute-start.3 = (bf16[144,1792]{1,0:T(8,128)(2,1)S(1)}, bf16[144,1792]{1,0:T(8,128)(2,1)S(1)}, u32[]{:S(2)}, u32[]{:S(2)}) collective-permute-start(bf16[144,1792]{1,0:T(8,128)(2,1)S(1)} %collective-permute-done.2.refs_0_), channel_id=1, source_target_pairs={{0,16},{1,113},{16,32},{17,1},{32,48},{33,17},{48,64},{49,33},{64,... | collective-permute-start | bytes 1548296 | tf_op jit(solution)/shard_map/ppermute | solution.py:30
  27.3 0.0 collective-permute-done.5
  27.3 2.2 %collective-permute-start.6 = (bf16[144,1792]{1,0:T(8,128)(2,1)S(1)}, bf16[144,1792]{1,0:T(8,128)(2,1)S(1)}, u32[]{:S(2)}, u32[]{:S(2)}) collective-permute-start(bf16[144,1792]{1,0:T(8,128)(2,1)S(1)} %collective-permute-done.5), channel_id=1, source_target_pairs={{0,16},{1,113},{16,32},{17,1},{32,48},{33,17},{48,64},{49,33},{64,... | collective-permute-start | bytes 1548296 | tf_op jit(solution)/shard_map/ppermute | solution.py:30
  29.6 5.1 %collective-permute-start.8 = (bf16[288,1792]{1,0:T(8,128)(2,1)S(1)}, bf16[288,1792]{1,0:T(8,128)(2,1)S(1)}, u32[]{:S(2)}, u32[]{:S(2)}) collective-permute-start(bf16[288,1792]{1,0:T(8,128)(2,1)S(1)} %constant_dynamic-update-slice_fusion.refs_1_), channel_id=1, source_target_pairs={{0,2},{1,15},{2,4},{3,1},{4,6},{5,3},{6,8},{7,5},{8,10},{9,7},{10,... | collective-permute-start | bytes 3096584 | tf_op jit(solution)/shard_map/ppermute | solution.py:30
  34.7 0.0 collective-permute-done.3.refs_1_
  34.7 3.9 %collective-permute-start.7 = (bf16[144,1792]{1,0:T(8,128)(2,1)S(1)}, bf16[144,1792]{1,0:T(8,128)(2,1)S(1)}, u32[]{:S(2)}, u32[]{:S(2)}) collective-permute-start(bf16[144,1792]{1,0:T(8,128)(2,1)S(1)} %collective-permute-done.3.refs_1_), channel_id=1, source_target_pairs={{0,16},{1,113},{16,32},{17,1},{32,48},{33,17},{48,64},{49,33},{64,... | collective-permute-start | bytes 1548296 | tf_op jit(solution)/shard_map/ppermute | solution.py:30
  38.6 0.0 collective-permute-done.1
  38.7 0.1 copy.12.refs_2_.beside_ref
  38.8 3.1 %collective-permute-start.4 = (bf16[1,68,3584]{2,1,0:T(8,128)(2,1)S(1)}, bf16[1,68,3584]{2,1,0:T(8,128)(2,1)S(1)}, u32[]{:S(2)}, u32[]{:S(2)}) collective-permute-start(bf16[1,68,3584]{2,1,0:T(8,128)(2,1)S(1)} %slice.8), channel_id=1, source_target_pairs={{0,128},{1,385},{128,256},{129,1},{256,384},{257,129},{384,0},{385... | collective-permute-start | bytes 1462280 | tf_op jit(solution)/shard_map/ppermute | solution.py:30
  42.0 0.0 collective-permute-done.6
  42.0 4.1 %collective-permute-start.10 = (bf16[288,1792]{1,0:T(8,128)(2,1)S(1)}, bf16[288,1792]{1,0:T(8,128)(2,1)S(1)}, u32[]{:S(2)}, u32[]{:S(2)}) collective-permute-start(bf16[288,1792]{1,0:T(8,128)(2,1)S(1)} %constant_dynamic-update-slice_fusion.2.refs_2_), channel_id=1, source_target_pairs={{0,2},{1,15},{2,4},{3,1},{4,6},{5,3},{6,8},{7,5},{8,10},{9,7},{10,... | collective-permute-start | bytes 3096584 | tf_op jit(solution)/shard_map/ppermute | solution.py:30
  46.2 2.8 %collective-permute-start.13 = (bf16[144,1792]{1,0:T(8,128)(2,1)S(1)}, bf16[144,1792]{1,0:T(8,128)(2,1)S(1)}, u32[]{:S(2)}, u32[]{:S(2)}) collective-permute-start(bf16[144,1792]{1,0:T(8,128)(2,1)S(1)} %collective-permute-done.6), channel_id=1, source_target_pairs={{0,16},{1,113},{16,32},{17,1},{32,48},{33,17},{48,64},{49,33},{64,... | collective-permute-start | bytes 1548296 | tf_op jit(solution)/shard_map/ppermute | solution.py:30
  49.0 0.0 collective-permute-done.7.refs_1_.refs_0_
  49.0 1.9 %collective-permute-start.9 = (bf16[144,1792]{1,0:T(8,128)(2,1)S(1)}, bf16[144,1792]{1,0:T(8,128)(2,1)S(1)}, u32[]{:S(2)}, u32[]{:S(2)}) collective-permute-start(bf16[144,1792]{1,0:T(8,128)(2,1)S(1)} %collective-permute-done.7.refs_1_.refs_0_), channel_id=1, source_target_pairs={{0,16},{1,113},{16,32},{17,1},{32,48},{33,17},{48,64},{49,33},{64,... | collective-permute-start | bytes 1548296 | tf_op jit(solution)/shard_map/ppermute | solution.py:30
  50.9 0.0 collective-permute-done.8.refs_3_
  50.9 0.0 collective-permute-done.4.refs_2_.distant_ref
  51.0 0.0 copy-start.3
  51.0 0.2 pad_maximum_fusion
  51.1 2.1 %collective-permute-start.11 = (bf16[3,68,3584]{2,1,0:T(8,128)(2,1)S(1)}, bf16[3,68,3584]{2,1,0:T(8,128)(2,1)S(1)}, u32[]{:S(2)}, u32[]{:S(2)}) collective-permute-start(bf16[3,68,3584]{2,1,0:T(8,128)(2,1)S(1)} %pad_maximum_fusion), channel_id=1, source_target_pairs={{0,1},{1,0},{2,3},{3,2},{4,5},{5,4},{6,7},{7,6},{8,9},{9,8},{10,11... | collective-permute-start | bytes 4386824 | tf_op jit(solution)/shard_map/ppermute | solution.py:30
  53.2 0.1 dynamic-slice_bitcast_fusion.refs_0_
  53.3 4.1 %collective-permute-start.14 = (bf16[144,1792]{1,0:T(8,128)(2,1)S(1)}, bf16[144,1792]{1,0:T(8,128)(2,1)S(1)}, u32[]{:S(2)}, u32[]{:S(2)}) collective-permute-start(bf16[144,1792]{1,0:T(8,128)(2,1)S(1)} %collective-permute-done.7.refs_1_.refs_0_), channel_id=1, source_target_pairs={{0,2},{1,15},{2,4},{3,1},{4,6},{5,3},{6,8},{7,5},{8,10},{9,7},{10,... | collective-permute-start | bytes 1548296 | tf_op jit(solution)/shard_map/ppermute | solution.py:30
  57.4 0.0 collective-permute-done.13.refs_1_
  57.4 3.0 %collective-permute-start.15 = (bf16[144,1792]{1,0:T(8,128)(2,1)S(1)}, bf16[144,1792]{1,0:T(8,128)(2,1)S(1)}, u32[]{:S(2)}, u32[]{:S(2)}) collective-permute-start(bf16[144,1792]{1,0:T(8,128)(2,1)S(1)} %collective-permute-done.13.refs_1_), channel_id=1, source_target_pairs={{0,2},{1,15},{2,4},{3,1},{4,6},{5,3},{6,8},{7,5},{8,10},{9,7},{10,... | collective-permute-start | bytes 1548296 | tf_op jit(solution)/shard_map/ppermute | solution.py:30
  60.4 1.4 %collective-permute-done.9.refs_1_.refs_0_ = bf16[144,1792]{1,0:T(8,128)(2,1)S(1)} collective-permute-done((bf16[144,1792]{1,0:T(8,128)(2,1)S(1)}, bf16[144,1792]{1,0:T(8,128)(2,1)S(1)}, u32[]{:S(2)}, u32[]{:S(2)}) %collective-permute-start.9) | collective-permute-done | bytes 516128 | tf_op jit(solution)/shard_map/ppermute | solution.py:30
  61.8 3.0 %collective-permute-start.12 = (bf16[144,1792]{1,0:T(8,128)(2,1)S(1)}, bf16[144,1792]{1,0:T(8,128)(2,1)S(1)}, u32[]{:S(2)}, u32[]{:S(2)}) collective-permute-start(bf16[144,1792]{1,0:T(8,128)(2,1)S(1)} %collective-permute-done.9.refs_1_.refs_0_), channel_id=1, source_target_pairs={{0,2},{1,15},{2,4},{3,1},{4,6},{5,3},{6,8},{7,5},{8,10},{9,7},{10,... | collective-permute-start | bytes 1548296 | tf_op jit(solution)/shard_map/ppermute | solution.py:30
  64.8 0.0 collective-permute-done.10.refs_2_.refs_4_
  64.8 0.6 mark.9
  65.4 0.0 collective-permute-done.11.swapped_ref
  65.4 0.8 line_up.1.a_ref
  66.2 4.7 %project.3.refs_4_ = bf16[8,68,1152]{2,1,0:T(8,128)(2,1)S(1)} custom-call(s32[5]{0:T(128)S(1)} %stack.23.place_ref, bf16[640,3584]{1,0:T(8,128)(2,1)S(1)} %line_up.1.a_ref, bf16[144,3584]{1,0:T(8,128)(2,1)S(1)} %dynamic-slice_bitcast_fusion.refs_0_, bf16[288,1792]{1,0:T(8,128)(2,1)S(1)} %constant_dynamic-update-slice_fusion.refs_1_, ...), custom_call_target="tpu_custom_call" | custom-call | bytes 1024 | tf_op jit(solution)/shard_map/project/pallas_call | solution.py:180
  71.0 0.0 collective-permute-done.14.refs_2_
  71.0 0.0 collective-permute-done.15.refs_3_
  71.0 3.4 %project.4.refs_2_ = bf16[8,68,1152]{2,1,0:T(8,128)(2,1)S(1)} custom-call(s32[5]{0:T(128)S(1)} %stack.23.place_ref, bf16[640,3584]{1,0:T(8,128)(2,1)S(1)} %line_up.1.a_ref, bf16[144,1792]{1,0:T(8,128)(2,1)S(1)} %collective-permute-done.7.refs_1_.refs_0_, bf16[144,1792]{1,0:T(8,128)(2,1)S(1)} %collective-permute-done.13.refs_1_, ...), custom_call_target="tpu_custom_call", output_to_operand_aliasing={{}: (6, {})} | custom-call | bytes 1024 | tf_op jit(solution)/shard_map/project/pallas_call | solution.py:180
  74.4 0.1 collective-permute-done.12.refs_1_
  74.5 2.2 %project.5 = bf16[8,68,1152]{2,1,0:T(8,128)(2,1)S(1)} custom-call(s32[5]{0:T(128)S(1)} %stack.23.place_ref, bf16[640,3584]{1,0:T(8,128)(2,1)S(1)} %line_up.1.a_ref, bf16[144,1792]{1,0:T(8,128)(2,1)S(1)} %collective-permute-done.9.refs_1_.refs_0_, bf16[144,1792]{1,0:T(8,128)(2,1)S(1)} %collective-permute-done.12.refs_1_, ...), custom_call_target="tpu_custom_call", output_to_operand_aliasing={{}: (4, {})} | custom-call | bytes 1024 | tf_op jit(solution)/shard_map/project/pallas_call | solution.py:180
  76.7 24.4 %all_to_all.5.ref = bf16[8,68,1152]{2,1,0:T(8,128)(2,1)S(1)} all-to-all(bf16[8,68,1152]{2,1,0:T(8,128)(2,1)S(1)} %project.5), channel_id=1, replica_groups=mesh['x'=4,'z'=8,'y'=8,'core'=2] {'x','core'}, dimensions={0} | all-to-all | bytes 2506752 | tf_op jit(solution)/shard_map/all_to_all | solution.py:283
  101.0 3.2 %settle.1 = bf16[68,9216]{1,0:T(8,128)(2,1)} custom-call(s32[5]{0:T(128)S(1)} %stack.23.place_ref, bf16[8,68,1152]{2,1,0:T(8,128)(2,1)S(1)} %all_to_all.5.ref), custom_call_target="tpu_custom_call" | custom-call | bytes 1024 | tf_op jit(solution)/shard_map/settle/pallas_call | solution.py:212
  (20 shorter events, 0.2 us)
Async XLA Ops:
  0.0 12.9 %copy-start.4 = (f32[3584]{0:T(1024)S(1)}, f32[3584]{0:T(1024)}, u32[]{:S(2)}) copy-start(f32[3584]{0:T(1024)} %param.6) | copy-start | bytes 43012
  0.0 13.0 %copy-start.1 = (s32[64]{0:T(128)S(1)}, s32[64]{0:T(128)}, u32[]{:S(2)}) copy-start(s32[64]{0:T(128)} %param.8) | copy-start | bytes 772
  0.0 13.0 %copy-start.2 = (s32[64]{0:T(128)S(1)}, s32[64]{0:T(128)}, u32[]{:S(2)}) copy-start(s32[64]{0:T(128)} %param.9) | copy-start | bytes 772
  0.0 13.0 %copy-start = (bf16[68,3584]{1,0:T(8,128)(2,1)S(1)}, bf16[68,3584]{1,0:T(8,128)(2,1)}, u32[]{:S(2)}) copy-start(bf16[68,3584]{1,0:T(8,128)(2,1)} %rows_ref.1) | copy-start | bytes 1462276
  1.4 22.2 %collective-permute-start.2 = (bf16[144,1792]{1,0:T(8,128)(2,1)S(1)}, bf16[144,1792]{1,0:T(8,128)(2,1)S(1)}, u32[]{:S(2)}, u32[]{:S(2)}) collective-permute-start(bf16[144,1792]{1,0:T(8,128)(2,1)S(1)} %get-tuple-element.24), channel_id=1, source_target_pairs={{0,16},{1,113},{16,32},{17,1},{32,48},{33,17},{48,64},{49,33},{64,... | collective-permute-start | bytes 1548296 | tf_op jit(solution)/shard_map/ppermute | solution.py:30
  13.8 4.5 %collective-permute-start = (bf16[68,3584]{1,0:T(8,128)(2,1)S(1)}, bf16[68,3584]{1,0:T(8,128)(2,1)S(1)}, u32[]{:S(2)}, u32[]{:S(2)}) collective-permute-start(bf16[68,3584]{1,0:T(8,128)(2,1)S(1)} %normalize.1.one_ref), channel_id=1, source_target_pairs={{0,1},{1,0},{2,3},{3,2},{4,5},{5,4},{6,7},{7,6},{8,9},{9,8},{10,11... | collective-permute-start | bytes 1462280 | tf_op jit(solution)/shard_map/ppermute | solution.py:30
  15.8 11.5 %collective-permute-start.5 = (bf16[144,1792]{1,0:T(8,128)(2,1)S(1)}, bf16[144,1792]{1,0:T(8,128)(2,1)S(1)}, u32[]{:S(2)}, u32[]{:S(2)}) collective-permute-start(bf16[144,1792]{1,0:T(8,128)(2,1)S(1)} %get-tuple-element.23), channel_id=1, source_target_pairs={{0,16},{1,113},{16,32},{17,1},{32,48},{33,17},{48,64},{49,33},{64,... | collective-permute-start | bytes 1548296 | tf_op jit(solution)/shard_map/ppermute | solution.py:30
  19.2 19.4 %collective-permute-start.1 = (bf16[2,68,3584]{2,0,1:T(2,128)(2,1)S(1)}, bf16[2,68,3584]{2,0,1:T(2,128)(2,1)S(1)}, u32[]{:S(2)}, u32[]{:S(2)}) collective-permute-start(bf16[2,68,3584]{2,0,1:T(2,128)(2,1)S(1)} %copy.8), channel_id=1, source_target_pairs={{0,128},{1,385},{128,256},{129,1},{256,384},{257,129},{384,0},{385... | collective-permute-start | bytes 2924552 | tf_op jit(solution)/shard_map/ppermute | solution.py:30
  23.6 11.1 %collective-permute-start.3 = (bf16[144,1792]{1,0:T(8,128)(2,1)S(1)}, bf16[144,1792]{1,0:T(8,128)(2,1)S(1)}, u32[]{:S(2)}, u32[]{:S(2)}) collective-permute-start(bf16[144,1792]{1,0:T(8,128)(2,1)S(1)} %collective-permute-done.2.refs_0_), channel_id=1, source_target_pairs={{0,16},{1,113},{16,32},{17,1},{32,48},{33,17},{48,64},{49,33},{64,... | collective-permute-start | bytes 1548296 | tf_op jit(solution)/shard_map/ppermute | solution.py:30
  27.3 14.7 %collective-permute-start.6 = (bf16[144,1792]{1,0:T(8,128)(2,1)S(1)}, bf16[144,1792]{1,0:T(8,128)(2,1)S(1)}, u32[]{:S(2)}, u32[]{:S(2)}) collective-permute-start(bf16[144,1792]{1,0:T(8,128)(2,1)S(1)} %collective-permute-done.5), channel_id=1, source_target_pairs={{0,16},{1,113},{16,32},{17,1},{32,48},{33,17},{48,64},{49,33},{64,... | collective-permute-start | bytes 1548296 | tf_op jit(solution)/shard_map/ppermute | solution.py:30
  29.6 21.4 %collective-permute-start.8 = (bf16[288,1792]{1,0:T(8,128)(2,1)S(1)}, bf16[288,1792]{1,0:T(8,128)(2,1)S(1)}, u32[]{:S(2)}, u32[]{:S(2)}) collective-permute-start(bf16[288,1792]{1,0:T(8,128)(2,1)S(1)} %constant_dynamic-update-slice_fusion.refs_1_), channel_id=1, source_target_pairs={{0,2},{1,15},{2,4},{3,1},{4,6},{5,3},{6,8},{7,5},{8,10},{9,7},{10,... | collective-permute-start | bytes 3096584 | tf_op jit(solution)/shard_map/ppermute | solution.py:30
  34.7 14.3 %collective-permute-start.7 = (bf16[144,1792]{1,0:T(8,128)(2,1)S(1)}, bf16[144,1792]{1,0:T(8,128)(2,1)S(1)}, u32[]{:S(2)}, u32[]{:S(2)}) collective-permute-start(bf16[144,1792]{1,0:T(8,128)(2,1)S(1)} %collective-permute-done.3.refs_1_), channel_id=1, source_target_pairs={{0,16},{1,113},{16,32},{17,1},{32,48},{33,17},{48,64},{49,33},{64,... | collective-permute-start | bytes 1548296 | tf_op jit(solution)/shard_map/ppermute | solution.py:30
  38.8 12.1 %collective-permute-start.4 = (bf16[1,68,3584]{2,1,0:T(8,128)(2,1)S(1)}, bf16[1,68,3584]{2,1,0:T(8,128)(2,1)S(1)}, u32[]{:S(2)}, u32[]{:S(2)}) collective-permute-start(bf16[1,68,3584]{2,1,0:T(8,128)(2,1)S(1)} %slice.8), channel_id=1, source_target_pairs={{0,128},{1,385},{128,256},{129,1},{256,384},{257,129},{384,0},{385... | collective-permute-start | bytes 1462280 | tf_op jit(solution)/shard_map/ppermute | solution.py:30
  42.0 22.8 %collective-permute-start.10 = (bf16[288,1792]{1,0:T(8,128)(2,1)S(1)}, bf16[288,1792]{1,0:T(8,128)(2,1)S(1)}, u32[]{:S(2)}, u32[]{:S(2)}) collective-permute-start(bf16[288,1792]{1,0:T(8,128)(2,1)S(1)} %constant_dynamic-update-slice_fusion.2.refs_2_), channel_id=1, source_target_pairs={{0,2},{1,15},{2,4},{3,1},{4,6},{5,3},{6,8},{7,5},{8,10},{9,7},{10,... | collective-permute-start | bytes 3096584 | tf_op jit(solution)/shard_map/ppermute | solution.py:30
  46.2 11.2 %collective-permute-start.13 = (bf16[144,1792]{1,0:T(8,128)(2,1)S(1)}, bf16[144,1792]{1,0:T(8,128)(2,1)S(1)}, u32[]{:S(2)}, u32[]{:S(2)}) collective-permute-start(bf16[144,1792]{1,0:T(8,128)(2,1)S(1)} %collective-permute-done.6), channel_id=1, source_target_pairs={{0,16},{1,113},{16,32},{17,1},{32,48},{33,17},{48,64},{49,33},{64,... | collective-permute-start | bytes 1548296 | tf_op jit(solution)/shard_map/ppermute | solution.py:30
  49.0 12.8 %collective-permute-start.9 = (bf16[144,1792]{1,0:T(8,128)(2,1)S(1)}, bf16[144,1792]{1,0:T(8,128)(2,1)S(1)}, u32[]{:S(2)}, u32[]{:S(2)}) collective-permute-start(bf16[144,1792]{1,0:T(8,128)(2,1)S(1)} %collective-permute-done.7.refs_1_.refs_0_), channel_id=1, source_target_pairs={{0,16},{1,113},{16,32},{17,1},{32,48},{33,17},{48,64},{49,33},{64,... | collective-permute-start | bytes 1548296 | tf_op jit(solution)/shard_map/ppermute | solution.py:30
  51.0 2.2 %copy-start.3 = (bf16[3584,288]{0,1:T(8,128)(2,1)S(1)}, bf16[3584,288]{0,1:T(8,128)(2,1)}, u32[]{:S(2)}) copy-start(bf16[3584,288]{0,1:T(8,128)(2,1)} %param.7) | copy-start | bytes 6193156
  51.1 14.3 %collective-permute-start.11 = (bf16[3,68,3584]{2,1,0:T(8,128)(2,1)S(1)}, bf16[3,68,3584]{2,1,0:T(8,128)(2,1)S(1)}, u32[]{:S(2)}, u32[]{:S(2)}) collective-permute-start(bf16[3,68,3584]{2,1,0:T(8,128)(2,1)S(1)} %pad_maximum_fusion), channel_id=1, source_target_pairs={{0,1},{1,0},{2,3},{3,2},{4,5},{5,4},{6,7},{7,6},{8,9},{9,8},{10,11... | collective-permute-start | bytes 4386824 | tf_op jit(solution)/shard_map/ppermute | solution.py:30
  53.3 17.7 %collective-permute-start.14 = (bf16[144,1792]{1,0:T(8,128)(2,1)S(1)}, bf16[144,1792]{1,0:T(8,128)(2,1)S(1)}, u32[]{:S(2)}, u32[]{:S(2)}) collective-permute-start(bf16[144,1792]{1,0:T(8,128)(2,1)S(1)} %collective-permute-done.7.refs_1_.refs_0_), channel_id=1, source_target_pairs={{0,2},{1,15},{2,4},{3,1},{4,6},{5,3},{6,8},{7,5},{8,10},{9,7},{10,... | collective-permute-start | bytes 1548296 | tf_op jit(solution)/shard_map/ppermute | solution.py:30
  57.4 13.6 %collective-permute-start.15 = (bf16[144,1792]{1,0:T(8,128)(2,1)S(1)}, bf16[144,1792]{1,0:T(8,128)(2,1)S(1)}, u32[]{:S(2)}, u32[]{:S(2)}) collective-permute-start(bf16[144,1792]{1,0:T(8,128)(2,1)S(1)} %collective-permute-done.13.refs_1_), channel_id=1, source_target_pairs={{0,2},{1,15},{2,4},{3,1},{4,6},{5,3},{6,8},{7,5},{8,10},{9,7},{10,... | collective-permute-start | bytes 1548296 | tf_op jit(solution)/shard_map/ppermute | solution.py:30
  61.8 12.7 %collective-permute-start.12 = (bf16[144,1792]{1,0:T(8,128)(2,1)S(1)}, bf16[144,1792]{1,0:T(8,128)(2,1)S(1)}, u32[]{:S(2)}, u32[]{:S(2)}) collective-permute-start(bf16[144,1792]{1,0:T(8,128)(2,1)S(1)} %collective-permute-done.9.refs_1_.refs_0_), channel_id=1, source_target_pairs={{0,2},{1,15},{2,4},{3,1},{4,6},{5,3},{6,8},{7,5},{8,10},{9,7},{10,... | collective-permute-start | bytes 1548296 | tf_op jit(solution)/shard_map/ppermute | solution.py:30
